TPU v7x, 32 devices: a whole 2x2x4 slice. The times are simulated.
32 devices in a mesh: seq: 8 (over z, y), batch: 4 (over x, core).
Axes of the slice: x: 2, y: 2, z: 4, core: 2. Of those that a mesh axis runs over, the one named last changes fastest.
Arguments:
- inputs: bfloat16 [8, 4096, 512], P('batch', 'seq'), may hold values from -6 to 6
- lengths: int32 [8], P('batch'), may hold values from 50 to 4096, as said below
- norm1_gain: float32 [512], replicated, may hold values from 0.25 to 1.75
- norm1_bias: float32 [512], replicated, may hold values from -2 to 2
- qkv_weight: bfloat16 [512, 1536], replicated, may hold values from -0.25 to 0.25
- features: bfloat16 [8, 256, 64], replicated, may hold values from -4 to 4
- out_weight: bfloat16 [512, 512], replicated, may hold values from -1 to 1
- norm2_gain: float32 [512], replicated, may hold values from 0.25 to 1.75
- norm2_bias: float32 [512], replicated, may hold values from -2 to 2
- up_weight: bfloat16 [512, 2048], replicated, may hold values from -0.25 to 0.25
- down_weight: bfloat16 [2048, 512], replicated, may hold values from -0.125 to 0.125
- cotangent: bfloat16 [8, 4096, 512], P('batch', 'seq'), may hold values from -6 to 6
Outputs:
- block_out: bfloat16 [8, 4096, 512], P('batch', 'seq')
- input_grad: float32 [8, 4096, 512], P('batch', 'seq')
- norm1_gain_grad: float32 [512], replicated
- norm1_bias_grad: float32 [512], replicated
- qkv_weight_grad: float32 [512, 1536], replicated
- out_weight_grad: float32 [512, 512], replicated
- norm2_gain_grad: float32 [512], replicated
- norm2_bias_grad: float32 [512], replicated
- up_weight_grad: float32 [512, 2048], replicated
- down_weight_grad: float32 [2048, 512], replicated
Inputs may be any that keep to these rules, and one draw needn't show every extreme that they name: lengths[b] is the number of real tokens of sequence b; its other 4096 - lengths[b] positions are padding. Among the 2 sequences of each index of batch, one, drawn from the seed, has all 4096 positions real.
All inputs are finite; a program needn't handle non-finite values.
Results may differ from a plain program's by a relative error of at most 0.029.
Values sent between devices are 32-bit elements; how exact they have to be, the bound alone decides.
No kernel may reach another device: no remote copies, remote signals or barrier semaphores. Data moves between devices by JAX's collectives and lax.ppermute only.
A program may use at most 256 MiB of HBM per device.

v0:
```python
import jax
import jax.numpy as jnp
from jax import lax
from jax.sharding import PartitionSpec as P

EPS = 1e-05
FULL_PRECISION = lax.Precision.HIGHEST


def carried_in(shard, axis, combine, identity, reverse):
    size, position = (lax.axis_size(axis), lax.axis_index(axis))
    everything = jax.tree.map(lambda part: lax.all_gather(part, axis), shard)
    start = jax.tree.map(
        lambda part, zero: jnp.broadcast_to(jnp.asarray(zero, part.dtype), part.shape),
        shard,
        identity,
    )

    def turn(k, before):
        at = size - 1 - k if reverse else k
        reached = at > position if reverse else at < position
        new = combine(before, jax.tree.map(lambda part: part[at], everything))
        return jax.tree.map(lambda a, b: jnp.where(reached, a, b), new, before)

    return lax.fori_loop(0, size, turn, start)


def layer_norm(values, gain_vec, bias_vec):
    row_mean = jnp.mean(values, axis=-1, keepdims=True)
    centred = values - row_mean
    inv_std = lax.rsqrt(jnp.mean(centred * centred, axis=-1, keepdims=True) + EPS)
    normed = centred * inv_std
    return (normed * gain_vec + bias_vec, normed, inv_std)


def norm_back(grad_out, normed, inv_std, gain_vec):
    scaled_grad = grad_out * gain_vec
    grad_in = inv_std * (
        scaled_grad
        - jnp.mean(scaled_grad, axis=-1, keepdims=True)
        - normed * jnp.mean(scaled_grad * normed, axis=-1, keepdims=True)
    )
    return (grad_in, jnp.sum(grad_out * normed, axis=(0, 1)), jnp.sum(grad_out, axis=(0, 1)))


def feature_map(rescaled_input, random_features):
    feature_projection = jnp.einsum(
        "kbvr,vxr->kbvx", rescaled_input, random_features, preferred_element_type=jnp.float32
    )
    norm_part = jnp.sum(jnp.square(rescaled_input.astype(jnp.float32)), axis=-1, keepdims=True)
    return jnp.exp(feature_projection - 0.5 * norm_part) * random_features.shape[1] ** (-0.5)


def add_pair(first_part, second_part):
    return (first_part[0] + second_part[0], first_part[1] + second_part[1])


def body(
    inputs,
    lengths,
    norm1_gain,
    norm1_bias,
    qkv_weight,
    features,
    out_weight,
    norm2_gain,
    norm2_bias,
    up_weight,
    down_weight,
    cotangent,
):
    seq_count, stretch_rows, model_width = inputs.shape
    head_count, feat_count, head_size = features.shape
    shrink = head_size ** (-0.25)
    first_row = lax.axis_index("seq") * stretch_rows
    positions = first_row + jnp.arange(stretch_rows, dtype=jnp.int32)
    live_rows = (positions[None, :] < lengths[:, None]).astype(jnp.float32)[..., None]
    row_data = inputs.astype(jnp.float32)
    normed_f, normed1, inv1 = layer_norm(row_data, norm1_gain, norm1_bias)
    normed_in = normed_f.astype(jnp.bfloat16)
    qkv = jnp.einsum("scd,de->sce", normed_in, qkv_weight, preferred_element_type=jnp.float32)
    split = qkv.reshape(seq_count, stretch_rows, 3, head_count, head_size)
    queries = (shrink * split[:, :, 0]).astype(jnp.bfloat16)
    keys_low = (shrink * split[:, :, 1]).astype(jnp.bfloat16)
    values_low = split[:, :, 2].astype(jnp.bfloat16)
    query_map = feature_map(queries, features)
    key_map = feature_map(keys_low, features) * live_rows[..., None]
    query_low = query_map.astype(jnp.bfloat16)
    key_low = key_map.astype(jnp.bfloat16)
    causal = jnp.tril(jnp.ones((stretch_rows, stretch_rows), dtype=bool))
    scores = jnp.where(
        causal,
        jnp.einsum("sihm,sjhm->shij", query_low, key_low, preferred_element_type=jnp.float32),
        0.0,
    )
    scores_low = scores.astype(jnp.bfloat16)
    delta_state = jnp.einsum(
        "sjhm,sjhd->shmd", key_low, values_low, preferred_element_type=jnp.float32
    )
    delta_sum = jnp.sum(key_low.astype(jnp.float32), axis=1)
    prefix_state, prefix_sum = carried_in(
        (delta_state, delta_sum),
        "seq",
        add_pair,
        (jnp.zeros_like(delta_state), jnp.zeros_like(delta_sum)),
        False,
    )
    state_low = prefix_state.astype(jnp.bfloat16)
    numerator = jnp.einsum(
        "sihm,shmd->sihd", query_low, state_low, preferred_element_type=jnp.float32
    ) + jnp.einsum("shij,sjhd->sihd", scores_low, values_low, preferred_element_type=jnp.float32)
    denominator = jnp.einsum(
        "sihm,shm->sih",
        query_low,
        prefix_sum,
        preferred_element_type=jnp.float32,
        precision=FULL_PRECISION,
    ) + jnp.transpose(jnp.sum(scores, axis=-1), (0, 2, 1))
    attention = numerator / denominator[..., None]
    attention_low = attention.reshape(seq_count, stretch_rows, model_width).astype(jnp.bfloat16)
    branch = jnp.einsum(
        "sce,ed->scd", attention_low, out_weight, preferred_element_type=jnp.float32
    )
    middle = row_data + live_rows * branch
    normed_g, normed2, inv2 = layer_norm(middle, norm2_gain, norm2_bias)
    normed_mid = normed_g.astype(jnp.bfloat16)
    up_proj = jnp.einsum("scd,df->scf", normed_mid, up_weight, preferred_element_type=jnp.float32)
    activated, gelu_back = jax.vjp(lambda values: jax.nn.gelu(values, approximate=True), up_proj)
    activated_low = activated.astype(jnp.bfloat16)
    ffn_branch = jnp.einsum(
        "scf,fd->scd", activated_low, down_weight, preferred_element_type=jnp.float32
    )
    block_out = (middle + live_rows * ffn_branch).astype(jnp.bfloat16)
    grad_out = cotangent.astype(jnp.float32)
    grad_ffn = (live_rows * grad_out).astype(jnp.bfloat16)
    down_grad = jnp.einsum(
        "scf,scd->fd", activated_low, grad_ffn, preferred_element_type=jnp.float32
    )
    grad_act = jnp.einsum("scd,fd->scf", grad_ffn, down_weight, preferred_element_type=jnp.float32)
    grad_up = gelu_back(grad_act)[0].astype(jnp.bfloat16)
    up_grad = jnp.einsum("scd,scf->df", normed_mid, grad_up, preferred_element_type=jnp.float32)
    grad_norm2 = jnp.einsum("scf,df->scd", grad_up, up_weight, preferred_element_type=jnp.float32)
    back_two, gain2_grad, bias2_grad = norm_back(grad_norm2, normed2, inv2, norm2_gain)
    grad_mid = grad_out + back_two
    grad_branch = (live_rows * grad_mid).astype(jnp.bfloat16)
    outw_grad = jnp.einsum(
        "sce,scd->ed", attention_low, grad_branch, preferred_element_type=jnp.float32
    )
    grad_attn = jnp.einsum(
        "scd,ed->sce", grad_branch, out_weight, preferred_element_type=jnp.float32
    )
    grad_attn = grad_attn.reshape(seq_count, stretch_rows, head_count, head_size)
    grad_num = (grad_attn / denominator[..., None]).astype(jnp.bfloat16)
    grad_den = -jnp.sum(grad_attn * attention, axis=-1) / denominator
    grad_scores = jnp.where(
        causal,
        jnp.einsum("sihd,sjhd->shij", grad_num, values_low, preferred_element_type=jnp.float32)
        + jnp.transpose(grad_den, (0, 2, 1))[..., None],
        0.0,
    ).astype(jnp.bfloat16)
    grad_state = jnp.einsum(
        "sihm,sihd->shmd", query_low, grad_num, preferred_element_type=jnp.float32
    )
    grad_sum = jnp.einsum(
        "sihm,sih->shm",
        query_low,
        grad_den,
        preferred_element_type=jnp.float32,
        precision=FULL_PRECISION,
    )
    later_state, later_sum = carried_in(
        (grad_state, grad_sum),
        "seq",
        add_pair,
        (jnp.zeros_like(grad_state), jnp.zeros_like(grad_sum)),
        True,
    )
    later_low = later_state.astype(jnp.bfloat16)
    grad_pq = (
        jnp.einsum("sihd,shmd->sihm", grad_num, state_low, preferred_element_type=jnp.float32)
        + jnp.einsum("shij,sjhm->sihm", grad_scores, key_low, preferred_element_type=jnp.float32)
        + grad_den[..., None] * prefix_sum[:, None]
    )
    grad_pk = (
        jnp.einsum("shij,sihm->sjhm", grad_scores, query_low, preferred_element_type=jnp.float32)
        + jnp.einsum("sjhd,shmd->sjhm", values_low, later_low, preferred_element_type=jnp.float32)
        + later_sum[:, None]
    )
    grad_vv = jnp.einsum(
        "shij,sihd->sjhd", scores_low, grad_num, preferred_element_type=jnp.float32
    ) + jnp.einsum("sjhm,shmd->sjhd", key_low, later_low, preferred_element_type=jnp.float32)
    exponent_query = grad_pq * query_map
    exponent_key = grad_pk * key_map
    grad_qs = jnp.einsum(
        "koer,erw->koew",
        exponent_query.astype(jnp.bfloat16),
        features,
        preferred_element_type=jnp.float32,
    ) - queries * jnp.sum(exponent_query, axis=-1, keepdims=True)
    grad_ks = jnp.einsum(
        "koer,erw->koew",
        exponent_key.astype(jnp.bfloat16),
        features,
        preferred_element_type=jnp.float32,
    ) - keys_low * jnp.sum(exponent_key, axis=-1, keepdims=True)
    grad_qkv = jnp.stack([shrink * grad_qs, shrink * grad_ks, grad_vv], axis=2)
    grad_qkv = grad_qkv.reshape(seq_count, stretch_rows, 3 * model_width).astype(jnp.bfloat16)
    qkv_grad = jnp.einsum("scd,sce->de", normed_in, grad_qkv, preferred_element_type=jnp.float32)
    grad_norm1 = jnp.einsum("sce,de->scd", grad_qkv, qkv_weight, preferred_element_type=jnp.float32)
    back_one, gain1_grad, bias1_grad = norm_back(grad_norm1, normed1, inv1, norm1_gain)
    input_grad = grad_mid + back_one
    gain1_grad, bias1_grad, qkv_grad, outw_grad, gain2_grad, bias2_grad, up_grad, down_grad = (
        lax.psum(
            (
                gain1_grad,
                bias1_grad,
                qkv_grad,
                outw_grad,
                gain2_grad,
                bias2_grad,
                up_grad,
                down_grad,
            ),
            ("seq", "batch"),
        )
    )
    return (
        block_out,
        input_grad,
        gain1_grad,
        bias1_grad,
        qkv_grad,
        outw_grad,
        gain2_grad,
        bias2_grad,
        up_grad,
        down_grad,
    )


def solution(mesh):
    return jax.shard_map(
        body,
        mesh=mesh,
        in_specs=(
            P("batch", "seq", None),
            P("batch"),
            P(),
            P(),
            P(),
            P(),
            P(),
            P(),
            P(),
            P(),
            P(),
            P("batch", "seq", None),
        ),
        out_specs=(
            P("batch", "seq", None),
            P("batch", "seq", None),
            P(),
            P(),
            P(),
            P(),
            P(),
            P(),
            P(),
            P(),
        ),
        check_vma=False,
    )
```

profile of v0, /device:TPU:0, one launch (start us, length us, event | category | flops | bytes accessed | tf_op | source)
XLA Modules:
  0.0 691.6 jit_solution(1814347748589382137)
XLA Ops:
  15.8 4.7 convert_reduce_fusion
  25.7 33.1 %all-gather.1 = f32[16,8,256]{2,1,0:T(8,128)S(1)} all-gather(f32[2,8,256]{2,1,0:T(8,128)S(1)} %copy.134), channel_id=3, replica_groups=mesh['seq'=8,'batch'=4] {'seq'}, dimensions={0}, use_global_device_ids=true | all-gather | bytes 147456 | tf_op jit(solution)/shard_map/all_gather | solution.py:12
  61.0 8.2 %fusion.19 = (bf16[2,512,8,256]{1,3,0,2:T(8,128)(2,1)}, f32[8,2,512,256]{2,3,1,0:T(8,128)}) fusion(f32[2,512,8]{1,0,2:T(2,128)S(1)} %broadcast_multiply_fusion, bf16[8,256,64]{1,2,0:T(8,128)(2,1)S(1)} %copy-done.29, f32[2,512,1,8,64]{1,4,3,2,0:T(8,128)} %copy-done.22), kind=kOutput, calls=%fused_computation.36 | convolution fusion | flops 275775488 | bytes 14974976 | tf_op jit(solution)/shard_map/kbvr,vxr->kbvx/dot_general | solution.py:47
  69.2 12.9 %select_convert_fusion.1 = (bf16[2,8,512,512]{2,3,1,0:T(8,128)(2,1)}, f32[2,8,512,512]{2,3,1,0:T(8,128)}) fusion(pred[512,512]{0,1:T(8,128)(4,1)S(1)} %iota_compare_fusion, bf16[2,512,8,256]{1,3,0,2:T(8,128)(2,1)} %get-tuple-element.430, bf16[2,512,8,256]{3,1,0,2:T(8,128)(2,1)S(1)} %copy-done.3), kind=kOutput, calls=%fused_computation.8 | convolution fusion | flops 2151677952 | bytes 33816576 | tf_op jit(solution)/shard_map/sihm,sjhm->shij/dot_general | solution.py:93
  82.2 8.6 %select_reduce_fusion = f32[2,8,512]{2,1,0:T(8,128)} fusion(f32[2,8,512,512]{2,3,1,0:T(8,128)} %get-tuple-element.433, pred[512,512]{0,1:T(8,128)(4,1)S(1)} %iota_compare_fusion), kind=kLoop, calls=%fused_computation.7 | loop fusion | flops 8380416 | bytes 17072128 | tf_op jit(solution)/shard_map/reduce_sum | solution.py:118
  90.8 62.0 %all-gather.7.cloned.1.call-done = f32[16,8,256,64]{2,3,1,0:T(8,128)} async-done(((f32[2,8,256,64]{2,3,1,0:T(8,128)}), f32[16,8,256,64]{2,3,1,0:T(8,128)}) %all-gather.7.cloned.1.call-update) | async-done | bytes 8388624 | tf_op jit(solution)/shard_map/all_gather | solution.py:12
  152.8 56.2 %while.34 = (s32[]{:T(128)}, f32[2,8,256,64]{3,2,1,0:T(8,128)}, f32[2,8,256]{2,1,0:T(8,128)S(1)}, s32[]{:T(128)}, f32[8,2,8,256,64]{3,4,2,1,0:T(8,128)}, /*index=5*/f32[8,2,8,256]{3,2,1,0:T(8,128)S(1)}, s32[]{:T(128)}, s32[]{:T(128)}) while((s32[]{:T(128)}, f32[2,8,256,64]{3,2,1,0:T(8,128)}, f32[2,8,256]{2,1,0:T(8,128)S(1)}, ...), condition=%wide.region_5.6_spmd.clone, body=%wide.region_4.5_spmd.clone.sunk | while | flops 798724 | bytes 7389307 | solution.py:25
  226.6 7.6 %fusion.6 = bf16[2,512,2048]{2,1,0:T(8,128)(2,1)S(1)} fusion(f32[2,512,2048]{2,1,0:T(8,128)S(1)} %fusion.70, bf16[2048,512]{1,0:T(8,128)(2,1)S(1)} %copy-done.63, bf16[2,512,512]{1,2,0:T(8,128)(2,1)S(1)} %copy-done.33, f32[2,512]{1,0:T(2,128)S(1)} %copy-done.51), kind=kOutput, calls=%fused_computation.17 | convolution fusion | flops 2190999552 | bytes 15732736 | tf_op jit(solution)/shard_map/scd,fd->scf/dot_general | solution.py:139
  250.6 5.7 fusion.38
  256.3 33.4 %all-gather.3 = f32[16,8,256]{2,1,0:T(8,128)} all-gather(f32[2,8,256]{2,1,0:T(8,128)S(1)} %bitcast.196), channel_id=5, replica_groups=mesh['seq'=8,'batch'=4] {'seq'}, dimensions={0}, use_global_device_ids=true | all-gather | bytes 147456 | tf_op jit(solution)/shard_map/all_gather | solution.py:12
  291.5 6.6 select_convert_fusion
  298.1 9.2 %fusion.16 = f32[2,8,256,512]{3,2,0,1:T(8,128)} fusion(bf16[2,512,8,256]{3,1,0,2:T(8,128)(2,1)S(1)} %copy-done.4, bf16[2,8,512,512]{2,3,1,0:T(8,128)(2,1)} %select_convert_fusion), kind=kOutput, calls=%fused_computation.33 | convolution fusion | flops 2147483648 | bytes 20971520 | tf_op jit(solution)/shard_map/shij,sjhm->sihm/dot_general | solution.py:181
  307.3 7.8 %fusion.121 = (f32[2,512,8]{1,0,2:T(2,128)S(1)}, bf16[2,512,8,256]{1,3,0,2:T(8,128)(2,1)S(1)}) fusion(f32[2,512,8]{1,0,2:T(2,128)S(1)} %copy-done.48, f32[8,2,512,256]{2,3,1,0:T(8,128)} %get-tuple-element.431, f32[2,8,256]{2,0,1:T(2,128)S(1)} %copy.157, f32[2,512,8]{1,0,2:T(2,128)S(1)} %copy.156, f32[2,8,256,512]{3,2,0,1:T(8,128)} %fusion.16, ...), kind=kOutput, calls=%fused_computation.167 | convolution fusion | flops 285466624 | bytes 23183360 | tf_op jit(solution)/shard_map/sihd,shmd->sihm/dot_general | solution.py:180
  316.9 7.5 %fusion.7 = f32[2,8,64,512]{3,2,0,1:T(8,128)} fusion(bf16[2,8,512,512]{2,3,1,0:T(8,128)(2,1)} %get-tuple-element.432, bf16[2,512,8,64]{1,3,2,0:T(8,128)(2,1)S(1)} %copy-done.27), kind=kOutput, calls=%fused_computation.18 | convolution fusion | flops 536870912 | bytes 11534336 | tf_op jit(solution)/shard_map/shij,sihd->sjhd/dot_general | solution.py:189
  328.9 9.1 %fusion.14 = f32[2,8,256,512]{2,3,0,1:T(8,128)} fusion(bf16[2,512,8,256]{1,3,0,2:T(8,128)(2,1)S(1)} %copy-done.7, bf16[2,8,512,512]{2,3,1,0:T(8,128)(2,1)} %select_convert_fusion), kind=kOutput, calls=%fused_computation.31 | convolution fusion | flops 2147483648 | bytes 20971520 | tf_op jit(solution)/shard_map/shij,sihm->sjhm/dot_general | solution.py:185
  338.0 9.4 %convolution_bitcast_fusion.1 = f32[2048,512]{1,0:T(8,128)} fusion(bf16[2,512,512]{1,2,0:T(8,128)(2,1)S(1)} %copy-done.35, f32[2,512]{1,0:T(2,128)S(1)} %copy-done.51, f32[2,512,2048]{2,1,0:T(8,128)} %copy-done.69), kind=kOutput, calls=%fused_computation.46 | convolution fusion | flops 2167930880 | bytes 13635584 | tf_op jit(solution)/shard_map/scf,scd->fd/dot_general | solution.py:136
  347.4 27.6 %all-gather.9.cloned.1.call-done = f32[16,8,256,64]{2,3,1,0:T(8,128)} async-done(((f32[2,8,256,64]{2,3,1,0:T(8,128)}), f32[16,8,256,64]{2,3,1,0:T(8,128)}) %all-gather.9.cloned.1.call-update) | async-done | bytes 8388624 | tf_op jit(solution)/shard_map/all_gather | solution.py:12
  375.1 45.3 %while.35 = (s32[]{:T(128)}, f32[2,8,256,64]{3,2,1,0:T(8,128)}, f32[2,8,256]{2,1,0:T(8,128)S(1)}, s32[]{:T(128)}, f32[8,2,8,256,64]{3,4,2,1,0:T(8,128)}, /*index...) while((s32[]{:T(128)}, f32[2,8,256,64]{3,2,1,0:T(8,128)}, ...), condition=%wide.region_15.16_spmd.clone, body=%wide.region_14.15_spmd.clone.sunk | while | flops 798728 | bytes 7389369 | solution.py:25
  420.4 5.0 fusion.82
  425.4 9.0 %fusion.120 = (f32[2,512,8]{1,0,2:T(2,128)S(1)}, bf16[2,512,8,256]{3,1,0,2:T(8,128)(2,1)S(1)}) fusion(f32[2,512]{1,0:T(2,128)S(1)} %copy-done.55, f32[2,512,8]{1,0,2:T(2,128)S(1)} %copy-done.43, f32[8,2,512,256]{3,2,1,0:T(8,128)} %get-tuple-element.429, f32[2,8,256]{2,0,1:T(2,128)S(1)} %copy.166, f32[2,8,256,512]{2,3,0,1:T(8,128)} %fusion.14, ...), kind=kOutput, calls=%fused_computation.166 | convolution fusion | flops 283369472 | bytes 23154688 | tf_op jit(solution)/shard_map/sjhd,shmd->sjhm/dot_general | solution.py:186
  441.9 8.8 %add_convert_fusion.1 = bf16[2,512,512]{1,2,0:T(8,128)(2,1)S(1)} fusion(f32[2,512,512]{1,2,0:T(8,128)} %copy-done.16, bf16[2048,512]{1,0:T(8,128)(2,1)} %param.26, f32[2,512]{1,0:T(2,128)S(1)} %copy-done.51, f32[2,512,2048]{2,1,0:T(8,128)} %copy-done.69), kind=kOutput, calls=%fused_computation.110 | convolution fusion | flops 2167930880 | bytes 13635584 | tf_op jit(solution)/shard_map/scf,fd->scd/dot_general | solution.py:130
  452.1 5.7 fusion.122
  469.9 39.4 %all-reduce = (f32[512]{0:T(512)}, f32[512]{0:T(512)}, f32[512]{0:T(512)}, f32[512]{0:T(512)}) all-reduce(f32[512]{0:T(512)S(1)} %get-tuple-element.389, f32[512]{0:T(512)S(1)} %get-tuple-element.444, f32[512]{0:T(512)S(1)} %get-tuple-element.387, f32[512]{0:T(512)S(1)} %copy-done.61), channel_id=1, replica_groups=mesh['seq'=8,'batch'=4] {'seq','batch'}, use_global_device_ids=true, to_apply=%region_20.21 | all-reduce | flops 2048 | bytes 16384 | tf_op jit(solution)/shard_map/psum | solution.py:213
  509.2 164.0 %all-reduce.4.cloned.1.call-done = (f32[512,1536]{1,0:T(8,128)}, f32[512,512]{1,0:T(8,128)}, f32[512,2048]{1,0:T(8,128)}, f32[2048,512]{1,0:T(8,128)}) async-done(((f32[512,1536]{1,0:T(8,128)}, f32[512,512]{1,0:T(8,128)}, f32[512,2048]{1,0:T(8,128)}, f32[2048,512]{1,0:T(8,128)}), (f32[512,1536]{1,0:T(8,128)}, f32[512,512]{1,0:T(8,128)}, f32[512,2048]{1,0:T(8,128)}, ...) | async-done | bytes 12582928 | tf_op jit(solution)/shard_map/psum | solution.py:213
  (277 shorter events, 191.4 us)
Async XLA Ops:
  7.2 216.7 %copy-start = (bf16[512,2048]{1,0:T(8,128)(2,1)S(1)}, bf16[512,2048]{1,0:T(8,128)(2,1)}, u32[]{:S(2)}) copy-start(bf16[512,2048]{1,0:T(8,128)(2,1)} %param.25) | copy-start | bytes 6291460
  7.2 145.6 %all-gather.7.cloned.1.call-start = ((), (), s32[]{:S(2)}) async-start(), calls=%async_computation | async-start | bytes 9437184 | tf_op jit(solution)/shard_map/all_gather | solution.py:12
  7.3 8.1 %copy-start.56 = (s32[512]{0:T(512)}, s32[512]{0:T(512)S(1)}, u32[]{:S(2)}) copy-start(s32[512]{0:T(512)S(1)} %iota_add_fusion) | copy-start | bytes 6148
  12.8 7.8 %copy-start.25 = (f32[2,512,1536]{1,2,0:T(8,128)}, f32[2,512,1536]{1,2,0:T(8,128)S(1)}, u32[]{:S(2)}) copy-start(f32[2,512,1536]{1,2,0:T(8,128)S(1)} %fusion.80) | copy-start | bytes 18874372
  15.3 5.2 copy-start.42
  24.3 350.8 %all-gather.9.cloned.1.call-start = ((), (), s32[]{:S(2)}) async-start(), calls=%async_computation.1 | async-start | bytes 9437184 | tf_op jit(solution)/shard_map/all_gather | solution.py:12
  61.0 8.2 %copy-start.47 = (f32[2,512,8]{1,0,2:T(2,128)}, f32[2,512,8]{1,0,2:T(2,128)S(1)}, u32[]{:S(2)}) copy-start(f32[2,512,8]{1,0,2:T(2,128)S(1)} %broadcast_multiply_fusion) | copy-start | bytes 98308
  61.0 8.2 %copy-start.3 = (bf16[2,512,8,256]{3,1,0,2:T(8,128)(2,1)S(1)}, bf16[2,512,8,256]{3,1,0,2:T(8,128)(2,1)}, u32[]{:S(2)}) copy-start(bf16[2,512,8,256]{3,1,0,2:T(8,128)(2,1)} %copy-done.2) | copy-start | bytes 12582916
  209.0 6.7 copy-start.44
  226.6 7.6 %copy-start.69 = (f32[2,512,2048]{2,1,0:T(8,128)}, f32[2,512,2048]{2,1,0:T(8,128)S(1)}, u32[]{:S(2)}) copy-start(f32[2,512,2048]{2,1,0:T(8,128)S(1)} %fusion.70) | copy-start | bytes 25165828
  250.5 422.7 %all-reduce.4.cloned.1.call-start = ((), (), s32[]{:S(2)}) async-start(), calls=%async_computation.2 | async-start | bytes 25165824 | tf_op jit(solution)/shard_map/psum | solution.py:213
  250.6 39.1 %copy-start.46 = (f32[2,512,8]{1,2,0:T(8,128)S(1)}, f32[2,512,8]{1,2,0:T(8,128)}, u32[]{:S(2)}) copy-start(f32[2,512,8]{1,2,0:T(8,128)} %copy-done.45) | copy-start | bytes 98308
  250.6 39.1 %copy-start.20 = (f32[2,512,512]{1,2,0:T(8,128)S(1)}, f32[2,512,512]{1,2,0:T(8,128)}, u32[]{:S(2)}) copy-start(f32[2,512,512]{1,2,0:T(8,128)} %copy-done.19) | copy-start | bytes 6291460
  291.5 6.6 copy-start.4
  298.1 9.2 %copy-start.9 = (f32[2,8,256,64]{3,2,1,0:T(8,128)S(1)}, f32[2,8,256,64]{3,2,1,0:T(8,128)}, u32[]{:S(2)}) copy-start(f32[2,8,256,64]{3,2,1,0:T(8,128)} %get-tuple-element.275) | copy-start | bytes 3145732
  298.1 9.2 %copy-start.48 = (f32[2,512,8]{1,0,2:T(2,128)S(1)}, f32[2,512,8]{1,0,2:T(2,128)}, u32[]{:S(2)}) copy-start(f32[2,512,8]{1,0,2:T(2,128)} %copy-done.47) | copy-start | bytes 98308
  307.3 7.8 %copy-start.23 = (f32[2,512,1,8,64]{1,4,3,2,0:T(8,128)S(1)}, f32[2,512,1,8,64]{1,4,3,2,0:T(8,128)}, u32[]{:S(2)}) copy-start(f32[2,512,1,8,64]{1,4,3,2,0:T(8,128)} %copy-done.22) | copy-start | bytes 6291460
  307.3 7.8 %copy-start.30 = (bf16[8,256,64]{1,2,0:T(8,128)(2,1)S(1)}, bf16[8,256,64]{1,2,0:T(8,128)(2,1)}, u32[]{:S(2)}) copy-start(bf16[8,256,64]{1,2,0:T(8,128)(2,1)} %param.21) | copy-start | bytes 786436
  316.9 7.5 %copy-start.18 = (f32[2,512,512]{1,2,0:T(8,128)S(1)}, f32[2,512,512]{1,2,0:T(8,128)}, u32[]{:S(2)}) copy-start(f32[2,512,512]{1,2,0:T(8,128)} %copy-done.16) | copy-start | bytes 6291460
  316.9 7.5 %copy-start.58 = (f32[512]{0:T(512)S(1)}, f32[512]{0:T(512)}, u32[]{:S(2)}) copy-start(f32[512]{0:T(512)} %param.23) | copy-start | bytes 6148
  316.9 7.5 %copy-start.66 = (f32[512]{0:T(512)S(1)}, f32[512]{0:T(512)}, u32[]{:S(2)}) copy-start(f32[512]{0:T(512)} %param.24) | copy-start | bytes 6148
  316.9 7.5 %copy-start.71 = (bf16[2,512,2048]{2,1,0:T(8,128)(2,1)S(1)}, bf16[2,512,2048]{2,1,0:T(8,128)(2,1)}, u32[]{:S(2)}) copy-start(bf16[2,512,2048]{2,1,0:T(8,128)(2,1)} %copy-done.70) | copy-start | bytes 12582916
  328.9 9.1 %copy-start.35 = (bf16[2,512,512]{1,2,0:T(8,128)(2,1)S(1)}, bf16[2,512,512]{1,2,0:T(8,128)(2,1)}, u32[]{:S(2)}) copy-start(bf16[2,512,512]{1,2,0:T(8,128)(2,1)} %copy.146) | copy-start | bytes 3145732
  425.4 9.1 %copy-start.15 = (f32[2,512,1,8,64]{1,4,3,2,0:T(8,128)S(1)}, f32[2,512,1,8,64]{1,4,3,2,0:T(8,128)}, u32[]{:S(2)}) copy-start(f32[2,512,1,8,64]{1,4,3,2,0:T(8,128)} %copy-done.14) | copy-start | bytes 6291460
  (51 other events, 145.9 us)
Sparse Core Ops, SparseCore 0:
  24.4 128.3 all-gather.6
  250.6 124.4 all-gather.8
  442.1 231.0 all-reduce.3
where the time goes:
time: 699 us; the launch traced here: 692 us
  waiting for transfers between devices  254 us (36%)
  matrix products  156 us (22%)
  blocking collectives  106 us (15%)
  other arithmetic  83.4 us (12%)
  local copies, waits for them, and re-layouts  77.5 us (11%)
  between operations  14.8 us (2%)
    psum x1, waiting for transfers between devices, body(): lax.psum((gain1_grad, bias1_grad, qkv_grad, outw_grad, gain2_grad, bias2_...  164 us
    all_gather x2, waiting for transfers between devices, carried_in(): everything = jax.tree.map(lambda part: lax.all_gather(part, axis), shard)  89.7 us
    all_gather x2, blocking collectives, carried_in(): everything = jax.tree.map(lambda part: lax.all_gather(part, axis), shard)  66.5 us
    select_n x32, other arithmetic, turn(): return jax.tree.map(lambda a, b: jnp.where(reached, a, b), new, before)  59.8 us
    dynamic_slice x32, local copies, waits for them, and re-layouts, turn(): new = combine(before, jax.tree.map(lambda part: part[at], everything))  41.4 us
    psum x1, blocking collectives, body(): lax.psum((gain1_grad, bias1_grad, qkv_grad, outw_grad, gain2_grad, bias2_...  39.4 us
    unnamed x152, local copies, waits for them, and re-layouts  29 us
  transfers between devices with their start and end apart: 3, of which 3 were waited for; matrix products, arithmetic and copies ran while one was open for 18% of the time, Pallas kernels for 0%

commit v1 on v0

--- a/solution.py
+++ b/solution.py
@@ -1,28 +1,129 @@
+import functools
+
 import jax
 import jax.numpy as jnp
 from jax import lax
-from jax.sharding import PartitionSpec as P
+from jax.sharding import Mesh, PartitionSpec as P
 
 EPS = 1e-05
 FULL_PRECISION = lax.Precision.HIGHEST
 
 
-def carried_in(shard, axis, combine, identity, reverse):
-    size, position = (lax.axis_size(axis), lax.axis_index(axis))
-    everything = jax.tree.map(lambda part: lax.all_gather(part, axis), shard)
-    start = jax.tree.map(
-        lambda part, zero: jnp.broadcast_to(jnp.asarray(zero, part.dtype), part.shape),
-        shard,
-        identity,
-    )
-
-    def turn(k, before):
-        at = size - 1 - k if reverse else k
-        reached = at > position if reverse else at < position
-        new = combine(before, jax.tree.map(lambda part: part[at], everything))
-        return jax.tree.map(lambda a, b: jnp.where(reached, a, b), new, before)
-
-    return lax.fori_loop(0, size, turn, start)
+class Slice32:
+    axes = ("z", "y", "x", "c")
+    rows = P(("x", "c"), ("z", "y"), None)
+    lens = P(("x", "c"))
+    swap = {
+        "c": ("c", [(0, 1), (1, 0)]),
+        "x": ("x", [(0, 1), (1, 0)]),
+        "y": ("y", [(0, 1), (1, 0)]),
+        "z1": ("z", [(0, 1), (1, 0), (2, 3), (3, 2)]),
+        "z2": ("z", [(0, 2), (2, 0), (1, 3), (3, 1)]),
+    }
+
+    def position(self):
+        return lax.axis_index("z") * 2 + lax.axis_index("y")
+
+    def bit(self, step):
+        if step == "z1":
+            return lax.axis_index("z") % 2
+        if step == "z2":
+            return lax.axis_index("z") // 2
+        return lax.axis_index(step)
+
+    def exchange(self, part, step):
+        axis, pairs = self.swap[step]
+        return lax.ppermute(part, axis, pairs)
+
+    def carry(self, halves, reverse):
+        y = lax.axis_index("y")
+        keep = lax.dynamic_index_in_dim(halves, y, 0, keepdims=False)
+        give = lax.dynamic_index_in_dim(halves, 1 - y, 0, keepdims=False)
+        got = self.exchange(give, "y")
+        total = keep + got
+        hops = [(3, 2), (2, 1), (1, 0)] if reverse else [(0, 1), (1, 2), (2, 3)]
+        out, before = total, None
+        for n, hop in enumerate(hops):
+            arrived = lax.ppermute(out, "z", [hop])
+            before = arrived if before is None else before + arrived
+            out = arrived + total
+        first = y == (1 if reverse else 0)
+        mine = before + jnp.where(first, 0.0, got)
+        other = self.exchange(before + jnp.where(first, keep, 0.0), "y")
+        pair = jnp.stack([mine, other])
+        return jnp.where(y == 0, pair, pair[::-1])
+
+    def split(self, part, step):
+        half = part.shape[0] // 2
+        bit = self.bit(step)
+        keep = lax.dynamic_slice_in_dim(part, bit * half, half, 0)
+        give = lax.dynamic_slice_in_dim(part, (1 - bit) * half, half, 0)
+        return keep + self.exchange(give, step)
+
+    def join(self, part, step):
+        other = self.exchange(part, step)
+        first = self.bit(step) == 0
+        return jnp.concatenate([jnp.where(first, part, other), jnp.where(first, other, part)], 0)
+
+    def total(self, part, order):
+        for step in order:
+            part = self.split(part, step)
+        for step in order[::-1]:
+            part = self.join(part, step)
+        return part
+
+    def total_small(self, part):
+        for step in ("c", "x", "y", "z1", "z2"):
+            part = part + self.exchange(part, step)
+        return part
+
+
+class AnySlice:
+    axes = ("seq", "batch")
+    rows = P("batch", "seq", None)
+    lens = P("batch")
+
+    def position(self):
+        return lax.axis_index("seq")
+
+    def carry(self, halves, reverse):
+        size = lax.axis_size("seq")
+
+        def shift(part, by):
+            pairs = [(i, i + by) for i in range(size - by)]
+            return lax.ppermute(part, "seq", [(b, a) for a, b in pairs] if reverse else pairs)
+
+        out, by = shift(halves, 1), 1
+        while by < size:
+            out, by = out + shift(out, by), by * 2
+        return out
+
+    def total(self, part, order):
+        return lax.psum(part, ("seq", "batch"))
+
+    def total_small(self, part):
+        return lax.psum(part, ("seq", "batch"))
+
+
+def carried_in(comm, state, total, reverse):
+    seqs, heads, feats, size = state.shape
+    lanes = 512
+    rows = heads * feats * size // lanes // 2
+    extra = heads * feats // lanes // 2
+    states, sums = [], []
+    for s in range(seqs):
+        halves = jnp.concatenate(
+            [
+                state[s].reshape(2, rows, lanes),
+                total[s].reshape(2, extra, lanes),
+                jnp.zeros((2, -extra % 8, lanes), jnp.float32),
+            ],
+            axis=1,
+        )
+        halves = comm.carry(halves, reverse)
+        states.append(halves[:, :rows].reshape(heads, feats, size))
+        sums.append(halves[:, rows : rows + extra].reshape(heads, feats))
+    return jnp.stack(states), jnp.stack(sums)
 
 
 def layer_norm(values, gain_vec, bias_vec):
@@ -51,11 +152,8 @@
     return jnp.exp(feature_projection - 0.5 * norm_part) * random_features.shape[1] ** (-0.5)
 
 
-def add_pair(first_part, second_part):
-    return (first_part[0] + second_part[0], first_part[1] + second_part[1])
-
-
 def body(
+    comm,
     inputs,
     lengths,
     norm1_gain,
@@ -72,7 +170,7 @@
     seq_count, stretch_rows, model_width = inputs.shape
     head_count, feat_count, head_size = features.shape
     shrink = head_size ** (-0.25)
-    first_row = lax.axis_index("seq") * stretch_rows
+    first_row = comm.position() * stretch_rows
     positions = first_row + jnp.arange(stretch_rows, dtype=jnp.int32)
     live_rows = (positions[None, :] < lengths[:, None]).astype(jnp.float32)[..., None]
     row_data = inputs.astype(jnp.float32)
@@ -98,13 +196,7 @@
         "sjhm,sjhd->shmd", key_low, values_low, preferred_element_type=jnp.float32
     )
     delta_sum = jnp.sum(key_low.astype(jnp.float32), axis=1)
-    prefix_state, prefix_sum = carried_in(
-        (delta_state, delta_sum),
-        "seq",
-        add_pair,
-        (jnp.zeros_like(delta_state), jnp.zeros_like(delta_sum)),
-        False,
-    )
+    prefix_state, prefix_sum = carried_in(comm, delta_state, delta_sum, False)
     state_low = prefix_state.astype(jnp.bfloat16)
     numerator = jnp.einsum(
         "sihm,shmd->sihd", query_low, state_low, preferred_element_type=jnp.float32
@@ -168,13 +260,7 @@
         preferred_element_type=jnp.float32,
         precision=FULL_PRECISION,
     )
-    later_state, later_sum = carried_in(
-        (grad_state, grad_sum),
-        "seq",
-        add_pair,
-        (jnp.zeros_like(grad_state), jnp.zeros_like(grad_sum)),
-        True,
-    )
+    later_state, later_sum = carried_in(comm, grad_state, grad_sum, True)
     later_low = later_state.astype(jnp.bfloat16)
     grad_pq = (
         jnp.einsum("sihd,shmd->sihm", grad_num, state_low, preferred_element_type=jnp.float32)
@@ -209,21 +295,12 @@
     grad_norm1 = jnp.einsum("sce,de->scd", grad_qkv, qkv_weight, preferred_element_type=jnp.float32)
     back_one, gain1_grad, bias1_grad = norm_back(grad_norm1, normed1, inv1, norm1_gain)
     input_grad = grad_mid + back_one
-    gain1_grad, bias1_grad, qkv_grad, outw_grad, gain2_grad, bias2_grad, up_grad, down_grad = (
-        lax.psum(
-            (
-                gain1_grad,
-                bias1_grad,
-                qkv_grad,
-                outw_grad,
-                gain2_grad,
-                bias2_grad,
-                up_grad,
-                down_grad,
-            ),
-            ("seq", "batch"),
-        )
-    )
+    up_grad = comm.total(up_grad, ("c", "x", "y", "z1", "z2"))
+    down_grad = comm.total(down_grad, ("c", "y", "x", "z1", "z2"))
+    outw_grad = comm.total(outw_grad, ("c", "x", "y", "z1", "z2"))
+    qkv_grad = comm.total(qkv_grad, ("c", "y", "x", "z1", "z2"))
+    small = comm.total_small(jnp.stack([gain1_grad, bias1_grad, gain2_grad, bias2_grad]))
+    gain1_grad, bias1_grad, gain2_grad, bias2_grad = small[0], small[1], small[2], small[3]
     return (
         block_out,
         input_grad,
@@ -239,34 +316,14 @@
 
 
 def solution(mesh):
+    comm = AnySlice()
+    if dict(mesh.shape) == {"seq": 8, "batch": 4}:
+        comm = Slice32()
+        mesh = Mesh(mesh.devices.reshape(4, 2, 2, 2), comm.axes)
     return jax.shard_map(
-        body,
+        functools.partial(body, comm),
         mesh=mesh,
-        in_specs=(
-            P("batch", "seq", None),
-            P("batch"),
-            P(),
-            P(),
-            P(),
-            P(),
-            P(),
-            P(),
-            P(),
-            P(),
-            P(),
-            P("batch", "seq", None),
-        ),
-        out_specs=(
-            P("batch", "seq", None),
-            P("batch", "seq", None),
-            P(),
-            P(),
-            P(),
-            P(),
-            P(),
-            P(),
-            P(),
-            P(),
-        ),
+        in_specs=(comm.rows, comm.lens) + (P(),) * 9 + (comm.rows,),
+        out_specs=(comm.rows, comm.rows) + (P(),) * 8,
         check_vma=False,
     )

time: 699 us -> 515 us (0.74)
  blocking collectives: 106 us -> 0 us
  waiting for transfers between devices: 254 us -> 148 us
  starting transfers between devices: 0.12 us -> 71.3 us
  other arithmetic: 83.4 us -> 60.1 us
  between operations: 14.8 us -> 2.73 us
    psum x1 -> x0, waiting for transfers between devices: 164 us -> none  [body(): lax.psum((gain1_grad, bias1_grad, qkv_grad, outw_grad, gain2_grad, bias2_...]
    ppermute x0 -> x65, waiting for transfers between devices: none -> 148 us  [the longest x53 147 us: exchange(): return lax.ppermute(part, axis, pairs)]
    all_gather x2 -> x0, waiting for transfers between devices: 89.7 us -> none  [carried_in(): everything = jax.tree.map(lambda part: lax.all_gather(part, axis), shard)]
    ppermute x0 -> x65, starting transfers between devices: none -> 71.3 us  [the longest x53 55.4 us: exchange(): return lax.ppermute(part, axis, pairs)]
    all_gather x2 -> x0, blocking collectives: 66.5 us -> none  [carried_in(): everything = jax.tree.map(lambda part: lax.all_gather(part, axis), shard)]
    select_n x32 -> x24, other arithmetic: 59.8 us -> 3.66 us  [the longest x20 3.48 us: join(): jnp.where(first, part, other)]
    psum x1 -> x0, blocking collectives: 39.4 us -> none  [body(): lax.psum((gain1_grad, bias1_grad, qkv_grad, outw_grad, gain2_grad, bias2_...]
    dynamic_slice x32 -> x20, local copies, waits for them, and re-layouts: 41.4 us -> 7.25 us  [split(): give = lax.dynamic_slice_in_dim(part, (1 - bit) * half, half, 0)]
  transfers between devices with their start and end apart: 3 -> 65, of which waited for: 3 -> 31; matrix products, arithmetic and copies ran while one was open for 18% -> 34% of each run, Pallas kernels for 0% -> 0%
where the time goes in v1:
time: 515 us; the launch traced here: 505 us
  matrix products  151 us (29%)
  waiting for transfers between devices  148 us (29%)
  local copies, waits for them, and re-layouts  71.8 us (14%)
  starting transfers between devices  71.3 us (14%)
  other arithmetic  60.1 us (12%)
    ppermute x53, waiting for transfers between devices, exchange(): return lax.ppermute(part, axis, pairs)  147 us
    ppermute x53, starting transfers between devices, exchange(): return lax.ppermute(part, axis, pairs)  55.4 us
    unnamed x168, local copies, waits for them, and re-layouts  21 us
    another operation x12, local copies, waits for them, and re-layouts, carried_in(): return (jnp.stack(states), jnp.stack(sums))  18.1 us
    ppermute x12, starting transfers between devices, carry(): arrived = lax.ppermute(out, 'z', [hop])  15.9 us
    dot_general x1, matrix products, body(): jnp.einsum('sihm,sjhm->shij', query_low, key_low, preferred_element_type=...  14.3 us
    dot_general x2, matrix products, feature_map(): jnp.einsum('kbvr,vxr->kbvx', rescaled_input, random_features, preferred_e...  12.1 us
  transfers between devices with their start and end apart: 65, of which 31 were waited for; matrix products, arithmetic and copies ran while one was open for 34% of the time, Pallas kernels for 0%

profile of v1, /device:TPU:0, one launch (start us, length us, event | category | flops | bytes accessed | tf_op | source)
XLA Modules:
  0.0 505.0 jit_solution(1196722442409118942)
XLA Ops:
  36.9 6.4 %fusion.19 = (bf16[2,512,8,256]{1,3,0,2:T(8,128)(2,1)}, f32[8,2,512,256]{2,3,1,0:T(8,128)}) fusion(f32[2,512,8]{1,0,2:T(2,128)S(1)} %broadcast_multiply_fusion, bf16[8,256,64]{1,2,0:T(8,128)(2,1)S(1)} %copy-done.23, f32[2,512,1,8,64]{1,4,3,2,0:T(8,128)S(1)} %copy-done.9), kind=kOutput, calls=%fused_computation.30 | convolution fusion | flops 275775488 | bytes 14974976 | tf_op jit(solution)/shard_map/kbvr,vxr->kbvx/dot_general | solution.py:148
  49.0 14.3 %select_convert_fusion.1 = (bf16[2,8,512,512]{2,3,1,0:T(8,128)(2,1)}, f32[2,8,512,512]{2,3,1,0:T(8,128)}) fusion(pred[512,512]{0,1:T(8,128)(4,1)S(1)} %iota_compare_fusion, bf16[2,512,8,256]{1,3,0,2:T(8,128)(2,1)} %get-tuple-element.117, bf16[2,512,8,256]{3,1,0,2:T(8,128)(2,1)} %get-tuple-element.49), kind=kOutput, calls=%fused_computation.2 | convolution fusion | flops 2151677952 | bytes 33816576 | tf_op jit(solution)/shard_map/sihm,sjhm->shij/dot_general | solution.py:191
  67.3 8.0 %select_reduce_fusion = f32[2,8,512]{2,1,0:T(8,128)S(1)} fusion(f32[2,8,512,512]{2,3,1,0:T(8,128)} %get-tuple-element.120, pred[512,512]{0,1:T(8,128)(4,1)S(1)} %iota_compare_fusion), kind=kLoop, calls=%fused_computation.1 | loop fusion | flops 8380416 | bytes 17072128 | tf_op jit(solution)/shard_map/reduce_sum | solution.py:210
  79.7 6.9 %fusion.137 = f32[2,8,64,512]{3,2,1,0:T(8,128)} fusion(bf16[2,8,512,512]{2,3,1,0:T(8,128)(2,1)} %get-tuple-element.119, f32[2,512,3,8,64]{1,4,3,2,0:T(8,128)} %bitcast.219), kind=kOutput, calls=%fused_computation.317 | convolution fusion | flops 536870912 | bytes 11534336 | tf_op jit(solution)/shard_map/shij,sjhd->sihd/dot_general | solution.py:203
  138.1 7.6 %fusion.6 = bf16[2,512,2048]{2,1,0:T(8,128)(2,1)S(1)} fusion(f32[2,512,2048]{2,1,0:T(8,128)S(1)} %fusion.70, bf16[2048,512]{1,0:T(8,128)(2,1)S(1)} %copy-done.76, bf16[2,512,512]{1,2,0:T(8,128)(2,1)S(1)} %copy-done.31, f32[2,512]{1,0:T(2,128)S(1)} %compare_convert_fusion), kind=kOutput, calls=%fused_computation.11 | convolution fusion | flops 2190999552 | bytes 15732736 | tf_op jit(solution)/shard_map/scd,fd->scf/dot_general | solution.py:231
  171.9 5.9 %fusion.38 = f32[2,8,1,256]{3,2,1,0:T(1,128)S(1)} fusion(bf16[2,512,8,256]{1,3,0,2:T(8,128)(2,1)} %get-tuple-element.117, f32[2,512,8,1]{1,2,0,3:T(8,128)S(1)} %bitcast.230), kind=kOutput, calls=%fused_computation.65 | convolution fusion | flops 25165824 | bytes 4243456 | tf_op jit(solution)/shard_map/sihm,sih->shm/dot_general | solution.py:256
  192.2 6.5 %select_convert_fusion = bf16[2,8,512,512]{2,3,1,0:T(8,128)(2,1)} fusion(f32[2,8,512]{2,1,0:T(8,128)S(1)} %copy-done.67, pred[512,512]{0,1:T(8,128)(4,1)S(1)} %iota_compare_fusion, bf16[2,512,8,64]{1,3,2,0:T(8,128)(2,1)S(1)} %divide_convert_fusion, f32[2,512,3,8,64]{1,4,3,2,0:T(8,128)} %bitcast.220), kind=kOutput, calls=%fused_computation | convolution fusion | flops 549453824 | bytes 10780672 | tf_op jit(solution)/shard_map/sihd,sjhd->shij/dot_general | solution.py:249
  198.7 9.2 %fusion.16 = f32[2,8,256,512]{3,2,0,1:T(8,128)} fusion(bf16[2,512,8,256]{3,1,0,2:T(8,128)(2,1)S(1)} %copy-done.2, bf16[2,8,512,512]{2,3,1,0:T(8,128)(2,1)} %select_convert_fusion), kind=kOutput, calls=%fused_computation.27 | convolution fusion | flops 2147483648 | bytes 20971520 | tf_op jit(solution)/shard_map/shij,sjhm->sihm/dot_general | solution.py:267
  207.9 8.9 %fusion.133 = (f32[2,512,8]{1,0,2:T(2,128)S(1)}, bf16[2,512,8,256]{1,3,0,2:T(8,128)(2,1)}) fusion(f32[2,512,8]{1,0,2:T(2,128)S(1)} %broadcast_multiply_fusion, f32[8,2,512,256]{2,3,1,0:T(8,128)} %get-tuple-element.118, f32[2,8,256]{2,0,1:T(2,128)S(1)} %copy-done.61, f32[2,512,8]{1,0,2:T(2,128)S(1)} %copy.154, f32[2,8,256,512]{3,2,0,1:T(8,128)} %fusion.16, ...), kind=kOutput, calls=%fused_computation.314 | convolution fusion | flops 285466624 | bytes 22659072 | tf_op jit(solution)/shard_map/sihd,shmd->sihm/dot_general | solution.py:266
  220.3 9.1 %fusion.14 = f32[2,8,256,512]{2,3,0,1:T(8,128)} fusion(bf16[2,512,8,256]{1,3,0,2:T(8,128)(2,1)S(1)} %copy-done.3, bf16[2,8,512,512]{2,3,1,0:T(8,128)(2,1)} %select_convert_fusion), kind=kOutput, calls=%fused_computation.25 | convolution fusion | flops 2147483648 | bytes 20971520 | tf_op jit(solution)/shard_map/shij,sihm->sjhm/dot_general | solution.py:271
  231.7 7.4 %collective-permute-done.15 = f32[136,512]{1,0:T(8,128)S(1)} collective-permute-done((f32[136,512]{1,0:T(8,128)S(1)}, f32[136,512]{1,0:T(8,128)S(1)}, u32[]{:S(2)}, u32[]{:S(2)}) %collective-permute-start.15) | collective-permute-done | bytes 278560 | tf_op jit(solution)/shard_map/ppermute | solution.py:36
  245.3 9.4 %collective-permute-start.39 = (f32[16,512]{1,0:T(8,128)S(1)}, f32[16,512]{1,0:T(8,128)S(1)}, u32[]{:S(2)}, u32[]{:S(2)}) collective-permute-start(f32[16,512]{1,0:T(8,128)S(1)} %constant_dynamic-slice_fusion.10), channel_id=1, source_target_pairs={{0,16},{16,0},{8,24},{24,8},{1,17},{17,1},{9,25},{25,9},{2,18},{18... | collective-permute-start | bytes 98312 | tf_op jit(solution)/shard_map/ppermute | solution.py:36
  254.7 7.5 %fusion.7 = f32[2,8,64,512]{3,2,0,1:T(8,128)} fusion(bf16[2,8,512,512]{2,3,1,0:T(8,128)(2,1)} %get-tuple-element.119, bf16[2,512,8,64]{1,3,2,0:T(8,128)(2,1)S(1)} %copy-done.21), kind=kOutput, calls=%fused_computation.12 | convolution fusion | flops 536870912 | bytes 11534336 | tf_op jit(solution)/shard_map/shij,sihd->sjhd/dot_general | solution.py:275
  304.8 8.7 %fusion.132 = (f32[2,512,8]{1,0,2:T(2,128)S(1)}, bf16[2,512,8,256]{3,1,0,2:T(8,128)(2,1)S(1)}) fusion(f32[2,512]{1,0:T(2,128)S(1)} %compare_select_fusion, f32[2,512,8]{1,0,2:T(2,128)S(1)} %copy-done.58, f32[8,2,512,256]{3,2,1,0:T(8,128)} %get-tuple-element.116, f32[2,8,256]{2,0,1:T(2,128)S(1)} %pad_maximum_fusion.28, f32[2,8,256,512]{2,3,0,1:T(8,128)} %fusion.14, ...), kind=kOutput, calls=%fused_computation.313 | convolution fusion | flops 283107328 | bytes 22630400 | tf_op jit(solution)/shard_map/sjhd,shmd->sjhm/dot_general | solution.py:272
  353.3 16.1 %collective-permute-done.46 = f32[128,2048]{1,0:T(8,128)S(1)} collective-permute-done((f32[128,2048]{1,0:T(8,128)S(1)}, f32[128,2048]{1,0:T(8,128)S(1)}, u32[]{:S(2)}, u32[]{:S(2)}) %collective-permute-start.46) | collective-permute-done | bytes 1048608 | tf_op jit(solution)/shard_map/ppermute | solution.py:36
  378.8 9.6 %collective-permute-done.47 = f32[64,2048]{1,0:T(8,128)S(1)} collective-permute-done((f32[64,2048]{1,0:T(8,128)S(1)}, f32[64,2048]{1,0:T(8,128)S(1)}, u32[]{:S(2)}, u32[]{:S(2)}) %collective-permute-start.47) | collective-permute-done | bytes 524320 | tf_op jit(solution)/shard_map/ppermute | solution.py:36
  390.9 10.8 %collective-permute-done.26 = f32[128,1536]{1,0:T(8,128)S(1)} collective-permute-done((f32[128,1536]{1,0:T(8,128)S(1)}, f32[128,1536]{1,0:T(8,128)S(1)}, u32[]{:S(2)}, u32[]{:S(2)}) %collective-permute-start.26) | collective-permute-done | bytes 786464 | tf_op jit(solution)/shard_map/ppermute | solution.py:36
  406.1 9.7 %collective-permute-done.49 = f32[16,2048]{1,0:T(8,128)S(1)} collective-permute-done((f32[16,2048]{1,0:T(8,128)S(1)}, f32[16,2048]{1,0:T(8,128)S(1)}, u32[]{:S(2)}, u32[]{:S(2)}) %collective-permute-start.49) | collective-permute-done | bytes 131104 | tf_op jit(solution)/shard_map/ppermute | solution.py:36
  422.4 7.1 %collective-permute-done.28 = f32[32,1536]{1,0:T(8,128)S(1)} collective-permute-done((f32[32,1536]{1,0:T(8,128)S(1)}, f32[32,1536]{1,0:T(8,128)S(1)}, u32[]{:S(2)}, u32[]{:S(2)}) %collective-permute-start.28) | collective-permute-done | bytes 196640 | tf_op jit(solution)/shard_map/ppermute | solution.py:36
  429.8 6.5 %collective-permute-done.29 = f32[16,1536]{1,0:T(8,128)S(1)} collective-permute-done((f32[16,1536]{1,0:T(8,128)S(1)}, f32[16,1536]{1,0:T(8,128)S(1)}, u32[]{:S(2)}, u32[]{:S(2)}) %collective-permute-start.29) | collective-permute-done | bytes 98336 | tf_op jit(solution)/shard_map/ppermute | solution.py:36
  451.4 9.2 %collective-permute-done.32 = f32[64,1536]{1,0:T(8,128)S(1)} collective-permute-done((f32[64,1536]{1,0:T(8,128)S(1)}, f32[64,1536]{1,0:T(8,128)S(1)}, u32[]{:S(2)}, u32[]{:S(2)}) %collective-permute-start.32) | collective-permute-done | bytes 393248 | tf_op jit(solution)/shard_map/ppermute | solution.py:36
  465.8 6.1 %collective-permute-done.62 = f32[256,512]{1,0:T(8,128)S(1)} collective-permute-done((f32[256,512]{1,0:T(8,128)S(1)}, f32[256,512]{1,0:T(8,128)S(1)}, u32[]{:S(2)}, u32[]{:S(2)}) %collective-permute-start.62) | collective-permute-done | bytes 524320 | tf_op jit(solution)/shard_map/ppermute | solution.py:36
  472.6 8.6 %collective-permute-done.33 = f32[128,1536]{1,0:T(8,128)S(1)} collective-permute-done((f32[128,1536]{1,0:T(8,128)S(1)}, f32[128,1536]{1,0:T(8,128)S(1)}, u32[]{:S(2)}, u32[]{:S(2)}) %collective-permute-start.33) | collective-permute-done | bytes 786464 | tf_op jit(solution)/shard_map/ppermute | solution.py:36
  486.5 8.2 %collective-permute-done.63 = f32[512,512]{1,0:T(8,128)S(1)} collective-permute-done((f32[512,512]{1,0:T(8,128)S(1)}, f32[512,512]{1,0:T(8,128)S(1)}, u32[]{:S(2)}, u32[]{:S(2)}) %collective-permute-start.63) | collective-permute-done | bytes 1048608 | tf_op jit(solution)/shard_map/ppermute | solution.py:36
  (496 shorter events, 294.5 us)
Async XLA Ops:
  36.7 26.5 %collective-permute-start = (f32[136,512]{1,0:T(8,128)}, f32[136,512]{1,0:T(8,128)}, u32[]{:S(2)}, u32[]{:S(2)}) collective-permute-start(f32[136,512]{1,0:T(8,128)} %dynamic-slice_bitcast_fusion.3), channel_id=1, source_target_pairs={{0,4},{4,0},{1,5},{5,1},{2,6},{6,2},{3,7},{7,3},{8,12},{12,8},{9,1... | collective-permute-start | bytes 835592 | tf_op jit(solution)/shard_map/ppermute | solution.py:36
  44.9 20.7 %collective-permute-start.6 = (f32[136,512]{1,0:T(8,128)S(1)}, f32[136,512]{1,0:T(8,128)S(1)}, u32[]{:S(2)}, u32[]{:S(2)}) collective-permute-start(f32[136,512]{1,0:T(8,128)S(1)} %bitcast_add_fusion.3), channel_id=1, source_target_pairs={{0,8},{1,9},{2,10},{3,11},{4,12},{5,13},{6,14},{7,15}} | collective-permute-start | bytes 835592 | tf_op jit(solution)/shard_map/ppermute | solution.py:47
  178.7 38.1 %collective-permute-start.35 = (f32[256,512]{1,0:T(8,128)}, f32[256,512]{1,0:T(8,128)}, u32[]{:S(2)}, u32[]{:S(2)}) collective-permute-start(f32[256,512]{1,0:T(8,128)} %constant_dynamic-slice_fusion.14), channel_id=1, source_target_pairs={{0,1},{1,0},{2,3},{3,2},{4,5},{5,4},{6,7},{7,6},{8,9},{9,8},{10,11... | collective-permute-start | bytes 1572872 | tf_op jit(solution)/shard_map/ppermute | solution.py:36
  185.4 57.1 %collective-permute-start.10 = (f32[136,512]{1,0:T(8,128)}, f32[136,512]{1,0:T(8,128)}, u32[]{:S(2)}, u32[]{:S(2)}) collective-permute-start(f32[136,512]{1,0:T(8,128)} %dynamic-slice_bitcast_fusion.1), channel_id=1, source_target_pairs={{0,4},{4,0},{1,5},{5,1},{2,6},{6,2},{3,7},{7,3},{8,12},{12,8},{9,1... | collective-permute-start | bytes 835592 | tf_op jit(solution)/shard_map/ppermute | solution.py:36
  190.1 154.0 %collective-permute-start.45 = (f32[256,2048]{1,0:T(8,128)}, f32[256,2048]{1,0:T(8,128)}, u32[]{:S(2)}, u32[]{:S(2)}) collective-permute-start(f32[256,2048]{1,0:T(8,128)} %constant_dynamic-slice_fusion.9), channel_id=1, source_target_pairs={{0,1},{1,0},{2,3},{3,2},{4,5},{5,4},{6,7},{7,6},{8,9},{9,8},{10,11... | collective-permute-start | bytes 6291464 | tf_op jit(solution)/shard_map/ppermute | solution.py:36
  191.9 156.8 %collective-permute-start.55 = (f32[1024,512]{1,0:T(8,128)}, f32[1024,512]{1,0:T(8,128)}, u32[]{:S(2)}, u32[]{:S(2)}) collective-permute-start(f32[1024,512]{1,0:T(8,128)} %constant_dynamic-slice_fusion.4), channel_id=1, source_target_pairs={{0,1},{1,0},{2,3},{3,2},{4,5},{5,4},{6,7},{7,6},{8,9},{9,8},{10,11... | collective-permute-start | bytes 6291464 | tf_op jit(solution)/shard_map/ppermute | solution.py:36
  239.1 23.0 %collective-permute-start.16 = (f32[136,512]{1,0:T(8,128)S(1)}, f32[136,512]{1,0:T(8,128)S(1)}, u32[]{:S(2)}, u32[]{:S(2)}) collective-permute-start(f32[136,512]{1,0:T(8,128)S(1)} %bitcast_add_fusion.1), channel_id=1, source_target_pairs={{24,16},{25,17},{26,18},{27,19},{28,20},{29,21},{30,22},{31,23}} | collective-permute-start | bytes 835592 | tf_op jit(solution)/shard_map/ppermute | solution.py:47
  243.5 19.4 %collective-permute-start.11 = (f32[136,512]{1,0:T(8,128)S(1)}, f32[136,512]{1,0:T(8,128)S(1)}, u32[]{:S(2)}, u32[]{:S(2)}) collective-permute-start(f32[136,512]{1,0:T(8,128)S(1)} %bitcast_add_fusion.2), channel_id=1, source_target_pairs={{24,16},{25,17},{26,18},{27,19},{28,20},{29,21},{30,22},{31,23}} | collective-permute-start | bytes 835592 | tf_op jit(solution)/shard_map/ppermute | solution.py:47
  245.3 18.4 %collective-permute-start.39 = (f32[16,512]{1,0:T(8,128)S(1)}, f32[16,512]{1,0:T(8,128)S(1)}, u32[]{:S(2)}, u32[]{:S(2)}) collective-permute-start(f32[16,512]{1,0:T(8,128)S(1)} %constant_dynamic-slice_fusion.10), channel_id=1, source_target_pairs={{0,16},{16,0},{8,24},{24,8},{1,17},{17,1},{9,25},{25,9},{2,18},{18... | collective-permute-start | bytes 98312 | tf_op jit(solution)/shard_map/ppermute | solution.py:36
  285.9 61.6 %collective-permute-start.43 = (f32[128,512]{1,0:T(8,128)}, f32[128,512]{1,0:T(8,128)}, u32[]{:S(2)}, u32[]{:S(2)}) collective-permute-start(f32[128,512]{1,0:T(8,128)} %pad_maximum_fusion.21), channel_id=1, source_target_pairs={{0,2},{2,0},{1,3},{3,1},{4,6},{6,4},{5,7},{7,5},{8,10},{10,8},{9,1... | collective-permute-start | bytes 786440 | tf_op jit(solution)/shard_map/ppermute | solution.py:36
  330.7 21.0 %collective-permute-start.25 = (f32[256,1536]{1,0:T(8,128)}, f32[256,1536]{1,0:T(8,128)}, u32[]{:S(2)}, u32[]{:S(2)}) collective-permute-start(f32[256,1536]{1,0:T(8,128)} %constant_dynamic-slice_fusion.19), channel_id=1, source_target_pairs={{0,1},{1,0},{2,3},{3,2},{4,5},{5,4},{6,7},{7,6},{8,9},{9,8},{10,11... | collective-permute-start | bytes 4718600 | tf_op jit(solution)/shard_map/ppermute | solution.py:36
  346.9 22.5 %collective-permute-start.46 = (f32[128,2048]{1,0:T(8,128)S(1)}, f32[128,2048]{1,0:T(8,128)S(1)}, u32[]{:S(2)}, u32[]{:S(2)}) collective-permute-start(f32[128,2048]{1,0:T(8,128)S(1)} %constant_dynamic-slice_fusion.8), channel_id=1, source_target_pairs={{0,2},{2,0},{1,3},{3,1},{4,6},{6,4},{5,7},{7,5},{8,10},{10,8},{9,1... | collective-permute-start | bytes 3145736 | tf_op jit(solution)/shard_map/ppermute | solution.py:36
  351.1 26.2 %collective-permute-start.56 = (f32[512,512]{1,0:T(8,128)S(1)}, f32[512,512]{1,0:T(8,128)S(1)}, u32[]{:S(2)}, u32[]{:S(2)}) collective-permute-start(f32[512,512]{1,0:T(8,128)S(1)} %constant_dynamic-slice_fusion.3), channel_id=1, source_target_pairs={{0,4},{4,0},{1,5},{5,1},{2,6},{6,2},{3,7},{7,3},{8,12},{12,8},{9,1... | collective-permute-start | bytes 3145736 | tf_op jit(solution)/shard_map/ppermute | solution.py:36
  369.6 18.9 %collective-permute-start.47 = (f32[64,2048]{1,0:T(8,128)S(1)}, f32[64,2048]{1,0:T(8,128)S(1)}, u32[]{:S(2)}, u32[]{:S(2)}) collective-permute-start(f32[64,2048]{1,0:T(8,128)S(1)} %constant_dynamic-slice_fusion.7), channel_id=1, source_target_pairs={{0,4},{4,0},{1,5},{5,1},{2,6},{6,2},{3,7},{7,3},{8,12},{12,8},{9,1... | collective-permute-start | bytes 1572872 | tf_op jit(solution)/shard_map/ppermute | solution.py:36
  370.3 31.4 %collective-permute-start.26 = (f32[128,1536]{1,0:T(8,128)S(1)}, f32[128,1536]{1,0:T(8,128)S(1)}, u32[]{:S(2)}, u32[]{:S(2)}) collective-permute-start(f32[128,1536]{1,0:T(8,128)S(1)} %constant_dynamic-slice_fusion.18), channel_id=1, source_target_pairs={{0,4},{4,0},{1,5},{5,1},{2,6},{6,2},{3,7},{7,3},{8,12},{12,8},{9,1... | collective-permute-start | bytes 2359304 | tf_op jit(solution)/shard_map/ppermute | solution.py:36
  388.8 16.8 %collective-permute-start.58 = (f32[128,512]{1,0:T(8,128)S(1)}, f32[128,512]{1,0:T(8,128)S(1)}, u32[]{:S(2)}, u32[]{:S(2)}) collective-permute-start(f32[128,512]{1,0:T(8,128)S(1)} %constant_dynamic-slice_fusion.1), channel_id=1, source_target_pairs={{0,8},{8,0},{16,24},{24,16},{1,9},{9,1},{17,25},{25,17},{2,10},{10... | collective-permute-start | bytes 786440 | tf_op jit(solution)/shard_map/ppermute | solution.py:36
  401.8 17.1 %collective-permute-start.27 = (f32[64,1536]{1,0:T(8,128)S(1)}, f32[64,1536]{1,0:T(8,128)S(1)}, u32[]{:S(2)}, u32[]{:S(2)}) collective-permute-start(f32[64,1536]{1,0:T(8,128)S(1)} %constant_dynamic-slice_fusion.17), channel_id=1, source_target_pairs={{0,2},{2,0},{1,3},{3,1},{4,6},{6,4},{5,7},{7,5},{8,10},{10,8},{9,1... | collective-permute-start | bytes 1179656 | tf_op jit(solution)/shard_map/ppermute | solution.py:36
  422.3 20.4 %collective-permute-start.51 = (f32[32,2048]{1,0:T(8,128)S(1)}, f32[32,2048]{1,0:T(8,128)S(1)}, u32[]{:S(2)}, u32[]{:S(2)}) collective-permute-start(f32[32,2048]{1,0:T(8,128)S(1)} %pad_maximum_fusion.22), channel_id=1, source_target_pairs={{0,8},{8,0},{16,24},{24,16},{1,9},{9,1},{17,25},{25,17},{2,10},{10... | collective-permute-start | bytes 786440 | tf_op jit(solution)/shard_map/ppermute | solution.py:36
  448.6 14.9 %collective-permute-start.52 = (f32[64,2048]{1,0:T(8,128)S(1)}, f32[64,2048]{1,0:T(8,128)S(1)}, u32[]{:S(2)}, u32[]{:S(2)}) collective-permute-start(f32[64,2048]{1,0:T(8,128)S(1)} %pad_maximum_fusion.18), channel_id=1, source_target_pairs={{0,4},{4,0},{1,5},{5,1},{2,6},{6,2},{3,7},{7,3},{8,12},{12,8},{9,1... | collective-permute-start | bytes 1572872 | tf_op jit(solution)/shard_map/ppermute | solution.py:36
  449.3 22.5 %collective-permute-start.62 = (f32[256,512]{1,0:T(8,128)S(1)}, f32[256,512]{1,0:T(8,128)S(1)}, u32[]{:S(2)}, u32[]{:S(2)}) collective-permute-start(f32[256,512]{1,0:T(8,128)S(1)} %pad_maximum_fusion.19), channel_id=1, source_target_pairs={{0,2},{2,0},{1,3},{3,1},{4,6},{6,4},{5,7},{7,5},{8,10},{10,8},{9,1... | collective-permute-start | bytes 1572872 | tf_op jit(solution)/shard_map/ppermute | solution.py:36
  460.7 20.5 %collective-permute-start.33 = (f32[128,1536]{1,0:T(8,128)S(1)}, f32[128,1536]{1,0:T(8,128)S(1)}, u32[]{:S(2)}, u32[]{:S(2)}) collective-permute-start(f32[128,1536]{1,0:T(8,128)S(1)} %pad_maximum_fusion.10), channel_id=1, source_target_pairs={{0,4},{4,0},{1,5},{5,1},{2,6},{6,2},{3,7},{7,3},{8,12},{12,8},{9,1... | collective-permute-start | bytes 2359304 | tf_op jit(solution)/shard_map/ppermute | solution.py:36
  463.7 21.2 %collective-permute-start.53 = (f32[128,2048]{1,0:T(8,128)S(1)}, f32[128,2048]{1,0:T(8,128)S(1)}, u32[]{:S(2)}, u32[]{:S(2)}) collective-permute-start(f32[128,2048]{1,0:T(8,128)S(1)} %pad_maximum_fusion.8), channel_id=1, source_target_pairs={{0,2},{2,0},{1,3},{3,1},{4,6},{6,4},{5,7},{7,5},{8,10},{10,8},{9,1... | collective-permute-start | bytes 3145736 | tf_op jit(solution)/shard_map/ppermute | solution.py:36
  472.0 22.8 %collective-permute-start.63 = (f32[512,512]{1,0:T(8,128)S(1)}, f32[512,512]{1,0:T(8,128)S(1)}, u32[]{:S(2)}, u32[]{:S(2)}) collective-permute-start(f32[512,512]{1,0:T(8,128)S(1)} %pad_maximum_fusion.9), channel_id=1, source_target_pairs={{0,4},{4,0},{1,5},{5,1},{2,6},{6,2},{3,7},{7,3},{8,12},{12,8},{9,1... | collective-permute-start | bytes 3145736 | tf_op jit(solution)/shard_map/ppermute | solution.py:36
  481.5 14.9 %collective-permute-start.34 = (f32[256,1536]{1,0:T(8,128)S(1)}, f32[256,1536]{1,0:T(8,128)S(1)}, u32[]{:S(2)}, u32[]{:S(2)}) collective-permute-start(f32[256,1536]{1,0:T(8,128)S(1)} %pad_maximum_fusion.6), channel_id=1, source_target_pairs={{0,1},{1,0},{2,3},{3,2},{4,5},{5,4},{6,7},{7,6},{8,9},{9,8},{10,11... | collective-permute-start | bytes 4718600 | tf_op jit(solution)/shard_map/ppermute | solution.py:36
  (123 other events, 1087.5 us)

commit v2 on v1

v2 whole, which is shorter than its diff:
```python
import functools

import jax
import jax.numpy as jnp
from jax import lax
from jax.experimental import pallas as pl
from jax.experimental.pallas import tpu as pltpu
from jax.sharding import Mesh, PartitionSpec as P

EPS = 1e-05
SHRINK = 64 ** (-0.25)
SCALE = 256 ** (-0.5)


class Slice32:
    axes = ("z", "y", "x", "c")
    rows = P(("x", "c"), ("z", "y"), None)
    lens = P(("x", "c"))
    swap = {
        "c": ("c", [(0, 1), (1, 0)]),
        "x": ("x", [(0, 1), (1, 0)]),
        "y": ("y", [(0, 1), (1, 0)]),
        "z1": ("z", [(0, 1), (1, 0), (2, 3), (3, 2)]),
        "z2": ("z", [(0, 2), (2, 0), (1, 3), (3, 1)]),
    }

    def position(self):
        return lax.axis_index("z") * 2 + lax.axis_index("y")

    def bit(self, step):
        if step == "z1":
            return lax.axis_index("z") % 2
        if step == "z2":
            return lax.axis_index("z") // 2
        return lax.axis_index(step)

    def exchange(self, part, step):
        axis, pairs = self.swap[step]
        return lax.ppermute(part, axis, pairs)

    def carry(self, halves, reverse):
        y = lax.axis_index("y")
        keep = lax.dynamic_index_in_dim(halves, y, 0, keepdims=False)
        give = lax.dynamic_index_in_dim(halves, 1 - y, 0, keepdims=False)
        got = self.exchange(give, "y")
        total = keep + got
        hops = [(3, 2), (2, 1), (1, 0)] if reverse else [(0, 1), (1, 2), (2, 3)]
        out, before = total, None
        for n, hop in enumerate(hops):
            arrived = lax.ppermute(out, "z", [hop])
            before = arrived if before is None else before + arrived
            out = arrived + total
        first = y == (1 if reverse else 0)
        mine = before + jnp.where(first, 0.0, got)
        other = self.exchange(before + jnp.where(first, keep, 0.0), "y")
        pair = jnp.stack([mine, other])
        return jnp.where(y == 0, pair, pair[::-1])

    def split(self, part, step):
        half = part.shape[0] // 2
        bit = self.bit(step)
        keep = lax.dynamic_slice_in_dim(part, bit * half, half, 0)
        give = lax.dynamic_slice_in_dim(part, (1 - bit) * half, half, 0)
        return keep + self.exchange(give, step)

    def join(self, part, step):
        other = self.exchange(part, step)
        first = self.bit(step) == 0
        return jnp.concatenate([jnp.where(first, part, other), jnp.where(first, other, part)], 0)

    def total(self, part, order):
        for step in order:
            part = self.split(part, step)
        for step in order[::-1]:
            part = self.join(part, step)
        return part

    def total_small(self, part):
        for step in ("c", "x", "y", "z1", "z2"):
            part = part + self.exchange(part, step)
        return part


class AnySlice:
    axes = ("seq", "batch")
    rows = P("batch", "seq", None)
    lens = P("batch")

    def position(self):
        return lax.axis_index("seq")

    def carry(self, halves, reverse):
        size = lax.axis_size("seq")

        def shift(part, by):
            pairs = [(i, i + by) for i in range(size - by)]
            return lax.ppermute(part, "seq", [(b, a) for a, b in pairs] if reverse else pairs)

        out, by = shift(halves, 1), 1
        while by < size:
            out, by = out + shift(out, by), by * 2
        return out

    def total(self, part, order):
        return lax.psum(part, ("seq", "batch"))

    def total_small(self, part):
        return lax.psum(part, ("seq", "batch"))


LANES = 128
BF = jnp.bfloat16
F32 = jnp.float32


def mm(a, b):
    return jnp.dot(a, b, preferred_element_type=F32)


def mm_t(a, b):
    return lax.dot_general(a, b, (((1,), (1,)), ((), ())), preferred_element_type=F32)


def lanes_of(width):
    return lax.broadcasted_iota(jnp.int32, (1, width), 1)


def head_of(width):
    return (lanes_of(width) % LANES) // 64


def live_of(meta, s, rows):
    at = lax.broadcasted_iota(jnp.int32, (rows, 1), 0) + meta[0]
    return (at < meta[1 + s]).astype(F32)


def norm(values, gain, bias):
    mu = jnp.mean(values, axis=-1, keepdims=True)
    centred = values - mu
    inv = lax.rsqrt(jnp.mean(centred * centred, axis=-1, keepdims=True) + EPS)
    xhat = centred * inv
    return xhat * gain + bias, xhat, inv


def norm_grad(e, xhat, inv, gain):
    eg = e * gain
    return inv * (
        eg
        - jnp.mean(eg, axis=-1, keepdims=True)
        - xhat * jnp.mean(eg * xhat, axis=-1, keepdims=True)
    )


def two_rows(first, second):
    row = lax.broadcasted_iota(jnp.int32, (8, first.shape[1]), 0)
    return jnp.where(row == 0, first, jnp.where(row == 1, second, 0.0))


def map_kernel(s, meta, x, gain, bias, wq, wk, wv, fx, h1, qs, ks, vv, pq, pk, xs):
    p = pl.program_id(0)
    rows = x.shape[1]

    @pl.when(p == 0)
    def _():
        h1[...] = norm(x[0].astype(F32), gain[...], bias[...])[0].astype(BF)

    w = jnp.concatenate([wq[...], wk[...], wv[...]], axis=1)
    qkv = mm(h1[...], w)
    q = (SHRINK * qkv[:, :LANES]).astype(BF)
    k = (SHRINK * qkv[:, LANES : 2 * LANES]).astype(BF)
    v = qkv[:, 2 * LANES :].astype(BF)
    qs[...], ks[...], vv[...] = q, k, v

    def phi(u):
        sq = jnp.square(u.astype(F32))
        hi = sq.astype(BF)
        lo = (sq - hi.astype(F32)).astype(BF)
        return jnp.exp(mm_t(jnp.concatenate([u, hi, lo], axis=1), fx[0])) * SCALE

    pq[...] = phi(q).astype(BF)
    phk = (phi(k) * live_of(meta, s, rows)).astype(BF)
    pk[...] = phk
    lhs = jnp.concatenate([v.T, jnp.ones((16, rows), BF)], axis=0)
    ds = mm(lhs, phk)
    at = pl.multiple_of((p % 2) * 64, 64)
    xs[0, pl.ds(at, 64), :256] = ds[:64, :256]
    xs[0, pl.ds(at, 64), 256:] = ds[64:128, 256:]
    row = lax.broadcasted_iota(jnp.int32, (8, 512), 0)
    z = ds[128:129]

    @pl.when(p % 2 == 0)
    def _():
        xs[0, 128:136] = jnp.where(row == 0, z, 0.0)

    @pl.when(p % 2 == 1)
    def _():
        xs[0, 128:136] = jnp.where(row == 1, z, xs[0, 128:136])


def below(rows, cols, shift):
    i = lax.broadcasted_iota(jnp.int32, (rows, cols), 0) + shift
    return lax.broadcasted_iota(jnp.int32, (rows, cols), 1) <= i


def local_kernel(pq, pk, vv, nd):
    rows = pq.shape[0]
    half = rows // 2
    v = vv[...]
    values = jnp.concatenate([v, jnp.ones_like(v)], axis=1)
    head = head_of(2 * LANES)
    top, low = None, None
    for h in range(2):
        cols = slice(256 * h, 256 * h + 256)
        mine = jnp.where(head == h, values, jnp.zeros_like(values))
        a0 = mm_t(pq[:half, cols], pk[:half, cols])
        a0 = jnp.where(below(half, half, 0), a0, 0.0).astype(BF)
        a1 = mm_t(pq[half:, cols], pk[:, cols])
        a1 = jnp.where(below(half, rows, half), a1, 0.0).astype(BF)
        t, l = mm(a0, mine[:half]), mm(a1, mine)
        top, low = (t, l) if h == 0 else (top + t, low + l)
    nd[:half] = top
    nd[half:] = low


def gelu_parts(u):
    c0, c1 = 0.7978845608028654, 0.044715
    sq = u * u
    t = jnp.tanh(u * (c0 + (c0 * c1) * sq))
    half_up = 0.5 + 0.5 * t
    slope = half_up + (0.5 * u) * (1.0 - t * t) * (c0 + (3.0 * c0 * c1) * sq)
    return u * half_up, slope


def state_t(xs, p):
    at = (p % 2) * 64
    return xs[p // 2, at : at + 64, :], xs[p // 2, 128 + p % 2 : 129 + p % 2, :]


def middle_kernel(
    s, meta, x, dy, pq, nd, xs, gain, bias, wo, wup, wdown,
    out, dx1, dx, a_low, db, h2, df, gl, du, gs, ng,
    x1, xhat, inv, f, dh2, den,
):
    c = pl.program_id(0)
    rows = x.shape[1]
    live = live_of(meta, s, rows)
    col = lanes_of(512)

    @pl.when(c == 0)
    def _():
        for p in range(4):
            st, z = state_t(xs, p)
            zero = jnp.zeros_like(st)
            zb = jnp.broadcast_to(z, st.shape)
            rhs = jnp.concatenate(
                [
                    jnp.where(col < 256, st, zero),
                    jnp.where(col >= 256, st, zero),
                    jnp.where(col < 256, zb, zero),
                    jnp.where(col >= 256, zb, zero),
                ],
                axis=0,
            ).astype(BF)
            both = mm_t(pq[:, 512 * p : 512 * p + 512], rhs) + nd[:, 256 * p : 256 * p + 256]
            lanes = slice(LANES * p, LANES * p + LANES)
            den[:, lanes] = both[:, LANES:]
            f[:, lanes] = both[:, :LANES] / both[:, LANES:]
        a_low[...] = f[...].astype(BF)
        mid = x[0].astype(F32) + live * mm(a_low[...], wo[...])
        x1[...] = mid
        h, xh, iv = norm(mid, gain[...], bias[...])
        h2[...] = h.astype(BF)
        xhat[...] = xh
        inv[...] = jnp.broadcast_to(iv, inv.shape)
        df[...] = (live * dy[0].astype(F32)).astype(BF)

    g, slope = gelu_parts(mm(h2[...], wup[...]))
    g = g.astype(BF)
    gl[...] = g
    d = (slope * mm_t(df[...], wdown[...])).astype(BF)
    du[...] = d
    part = mm(g, wdown[...])
    back = mm_t(d, wup[...])

    @pl.when(c == 0)
    def _():
        x1[...] += live * part
        dh2[...] = back

    @pl.when(c > 0)
    def _():
        x1[...] += live * part
        dh2[...] += back

    @pl.when(c == pl.num_programs(0) - 1)
    def _():
        out[...] = x1[...].astype(BF)
        e = dh2[...]
        xh = xhat[...]
        ng[...] = two_rows(
            jnp.sum(e * xh, axis=0, keepdims=True), jnp.sum(e, axis=0, keepdims=True)
        )
        g1 = dy[0].astype(F32) + norm_grad(e, xh, inv[:, :1], gain[...])
        dx1[...] = g1
        db[...] = (live * g1).astype(BF)
        da = mm_t(db[...], wo[...])
        block = jnp.where(
            lax.broadcasted_iota(jnp.int32, (2 * LANES, LANES), 0) % LANES // 64
            == lax.broadcasted_iota(jnp.int32, (2 * LANES, LANES), 1) // 64,
            -1.0,
            0.0,
        ).astype(BF)
        slot = lanes_of(LANES) % 64
        for p in range(4):
            lanes = slice(LANES * p, LANES * p + LANES)
            dn = da[:, lanes] / den[:, lanes]
            w = dn * f[:, lanes]
            hi = w.astype(BF)
            lo = (w - hi.astype(F32)).astype(BF)
            dd = mm(jnp.concatenate([hi, lo], axis=1), block)
            hi = dd.astype(BF).astype(F32)
            lo = dd - hi
            two = jnp.where((slot == 0) | (slot == 2), hi, jnp.where(slot == 1, lo, 0.0))
            both = jnp.concatenate([dn.astype(BF), two.astype(BF)], axis=1)
            dx[:, 256 * p : 256 * p + 256] = both
            g = mm(both.T, pq[:, 512 * p : 512 * p + 512])
            at = (p % 2) * 64
            gs[p // 2, at : at + 64, :] = jnp.where(col < 256, g[:64], g[64:128])
            z = jnp.where(col < 256, g[128:129] + g[129:130], g[192:193] + g[193:194])
            if p % 2 == 0:
                first = z
            else:
                gs[p // 2, 128:136, :] = two_rows(first, z)


def inner_kernel(qs, ks, vv, pq, pk, dx, xs, fx, dq, dkl, dvl):
    p = pl.program_id(0)
    rows = pq.shape[0]
    half = rows // 2
    col = lanes_of(512)
    slot = lanes_of(LANES) % 64
    head = head_of(2 * LANES)
    ones = jnp.broadcast_to(jnp.where(slot < 2, 1.0, 0.0), (rows, LANES)).astype(BF)
    v1 = jnp.concatenate([vv[...], ones], axis=1)
    st = xs[0, pl.ds(pl.multiple_of((p % 2) * 64, 64), 64), :]
    zs = xs[0, 128:136, :]
    z = jnp.where(p % 2 == 0, zs[0:1], zs[1:2])
    zh = z.astype(BF).astype(F32)
    zl = z - zh
    zero = jnp.zeros_like(st)
    row = lax.broadcasted_iota(jnp.int32, (64, 512), 0)
    zr = jnp.where(row < 2, zh, jnp.where(row == 2, zl, 0.0))
    rhs = jnp.concatenate(
        [
            jnp.where(col < 256, st, zero),
            jnp.where(col >= 256, st, zero),
            jnp.where(col < 256, zr, zero),
            jnp.where(col >= 256, zr, zero),
        ],
        axis=0,
    ).astype(BF)
    d = dx[...]
    far = mm(d, rhs)
    eqs, eks = [], []
    top, low = None, None
    for h in range(2):
        cols = slice(256 * h, 256 * h + 256)
        mine = jnp.where(head == h, d, jnp.zeros_like(d))
        q, k = pq[:, cols], pk[:, cols]
        a0 = jnp.where(below(half, half, 0), mm_t(mine[:half], v1[:half]), 0.0).astype(BF)
        a1 = jnp.where(below(half, rows, half), mm_t(mine[half:], v1), 0.0).astype(BF)
        dpq = jnp.concatenate([mm(a0, k[:half]), mm(a1, k)], axis=0) + far[:, cols]
        eqs.append((dpq * q.astype(F32)).astype(BF))
        i0 = lax.broadcasted_iota(jnp.int32, (half, rows), 1)
        up0 = i0 >= lax.broadcasted_iota(jnp.int32, (half, rows), 0)
        up1 = up0[:, :half]
        b0 = jnp.where(up0, mm_t(v1[:half], mine), 0.0).astype(BF)
        b1 = jnp.where(up1, mm_t(v1[half:], mine[half:]), 0.0).astype(BF)
        dpk = jnp.concatenate([mm(b0, q), mm(b1, q[half:])], axis=0)
        eks.append((dpk * k.astype(F32)).astype(BF))
        c0 = jnp.where(up0, mm_t(k[:half], q), 0.0).astype(BF)
        c1 = jnp.where(up1, mm_t(k[half:], q[half:]), 0.0).astype(BF)
        t, l = mm(c0, mine[:, :LANES]), mm(c1, mine[half:, :LANES])
        top, low = (t, l) if h == 0 else (top + t, low + l)
    fw = fx[0, :, : 2 * LANES]
    r = mm(jnp.concatenate(eqs, axis=1), fw)
    dq[...] = (SHRINK * (r[:, :LANES] + 2.0 * qs[...].astype(F32) * r[:, LANES:])).astype(BF)
    r = mm(jnp.concatenate(eks, axis=1), fw)
    dkl[...] = r[:, :LANES] + 2.0 * ks[...].astype(F32) * r[:, LANES:]
    dvl[:half] = top
    dvl[half:] = low


def last_kernel(
    s, x, dx1, gain, ks, vv, pk, rs, fx, dq, dkl, dvl, wq, wk, wv,
    grad, dk, dv, ng, dh1,
):
    p = pl.program_id(0)
    rows = pk.shape[0]
    col = lanes_of(512)
    slot = lanes_of(LANES) % 64
    ones = jnp.broadcast_to(jnp.where(slot < 2, 1.0, 0.0), (rows, LANES)).astype(BF)
    v1 = jnp.concatenate([vv[...], ones], axis=1)
    st = rs[0, pl.ds(pl.multiple_of((p % 2) * 64, 64), 64), :]
    zs = rs[0, 128:136, :]
    z = jnp.where(p % 2 == 0, zs[0:1], zs[1:2])
    zh = z.astype(BF).astype(F32)
    zl = z - zh
    zero = jnp.zeros_like(st)
    row = lax.broadcasted_iota(jnp.int32, (64, 512), 0)
    zr = jnp.where(row == 0, zh, jnp.where(row == 1, zl, 0.0))
    rhs = jnp.concatenate(
        [
            jnp.where(col < 256, st, zero),
            jnp.where(col >= 256, st, zero),
            jnp.where(col < 256, zr, zero),
            jnp.where(col >= 256, zr, zero),
        ],
        axis=0,
    ).astype(BF)
    dpk = mm(v1, rhs)
    ek = (dpk * pk[...].astype(F32)).astype(BF)
    r = mm(ek, fx[0, :, : 2 * LANES])
    k = SHRINK * (dkl[...] + r[:, :LANES] + 2.0 * ks[...].astype(F32) * r[:, LANES:])
    k = k.astype(BF)
    v = (dvl[...] + mm_t(pk[...], rhs[:LANES])).astype(BF)
    dk[...], dv[...] = k, v
    w = jnp.concatenate([wq[...], wk[...], wv[...]], axis=1)
    part = mm_t(jnp.concatenate([dq[...], k, v], axis=1), w)

    @pl.when(p == 0)
    def _():
        dh1[...] = part

    @pl.when(p > 0)
    def _():
        dh1[...] += part

    @pl.when(p == pl.num_programs(0) - 1)
    def _():
        _, xh, inv = norm(x[0].astype(F32), gain[...], gain[...])
        e = dh1[...]
        ng[...] = two_rows(
            jnp.sum(e * xh, axis=0, keepdims=True), jnp.sum(e, axis=0, keepdims=True)
        )
        grad[...] = dx1[...] + norm_grad(e, xh, inv, gain[...])


def weight_kernel(a0, a1, b0, b1, out):
    out[...] = mm(a0[...].T, b0[...]) + mm(a1[...].T, b1[...])


def params(limit=60):
    return pltpu.CompilerParams(vmem_limit_bytes=limit * 2**20)


def full(shape):
    return pl.BlockSpec(shape, lambda p, n=len(shape): (0,) * n)


def of_seq(s, shape):
    return pl.BlockSpec((1,) + shape, lambda p: (s, 0, 0))


def cols(rows, width, first=0):
    return pl.BlockSpec((rows, width), lambda p: (0, first + p))


SMEM = pl.BlockSpec(memory_space=pltpu.SMEM)
HALF = pl.BlockSpec((1, 136, 512), lambda p: (p // 2, 0, 0))
PAIR = pl.BlockSpec((1, 512, 384), lambda p: (p, 0, 0))


def arr(shape, dtype):
    return jax.ShapeDtypeStruct(shape, dtype)


def call(kernel, grid, ins, outs, scratch=(), flops=0, nbytes=0):
    return pl.pallas_call(
        kernel,
        grid=(grid,),
        in_specs=ins,
        out_specs=[o[0] for o in outs],
        out_shape=[arr(*o[1:]) for o in outs],
        scratch_shapes=list(scratch),
        compiler_params=params(),
        cost_estimate=pl.CostEstimate(flops=flops, bytes_accessed=nbytes, transcendentals=0),
    )


def weight_grad(a, b, over_a):
    m, n, rows = a[0].shape[1], b[0].shape[1], a[0].shape[0]
    grid = (m if over_a else n) // 512 if (m if over_a else n) > 512 else 1
    am, bn = (m // grid, n) if over_a else (m, n // grid)
    index_a = (lambda p: (0, p)) if over_a else (lambda p: (0, 0))
    index_b = (lambda p: (0, 0)) if over_a else (lambda p: (0, p))
    index_o = (lambda p: (p, 0)) if over_a else (lambda p: (0, p))
    sa, sb = pl.BlockSpec((rows, am), index_a), pl.BlockSpec((rows, bn), index_b)
    return call(
        weight_kernel, grid, [sa, sa, sb, sb],
        [(pl.BlockSpec((am, bn), index_o), (m, n), F32)],
        flops=4 * rows * m * n, nbytes=4 * m * n + 4 * rows * (m + n),
    )(a[0], a[1], b[0], b[1])[0]


def feature_blocks(features):
    pairs = features.shape[0] // 2
    f = features.reshape(pairs, 2, 256, 64)
    half = jnp.full((pairs, 256, 64), -0.5, BF)
    zero = jnp.zeros((pairs, 256, 64), BF)
    top = jnp.concatenate([f[:, 0], zero, half, zero, half, zero], axis=2)
    low = jnp.concatenate([zero, f[:, 1], zero, half, zero, half], axis=2)
    return jnp.concatenate([top, low], axis=1)


def body(
    comm,
    inputs,
    lengths,
    norm1_gain,
    norm1_bias,
    qkv_weight,
    features,
    out_weight,
    norm2_gain,
    norm2_bias,
    up_weight,
    down_weight,
    cotangent,
):
    seqs, rows, width = inputs.shape
    wide = up_weight.shape[1]
    first_row = (comm.position() * rows).astype(jnp.int32)
    meta = jnp.concatenate([first_row[None], lengths])
    fx = feature_blocks(features)
    g1, n1, g2, n2 = (v[None] for v in (norm1_gain, norm1_bias, norm2_gain, norm2_bias))
    vec = full((1, width))
    act = cols(rows, LANES)
    big = cols(rows, 512)
    xs_out = (HALF, (2, 136, 512), F32)
    maps, locals_, state = [], [], []
    for s in range(seqs):
        outs = call(
            functools.partial(map_kernel, s), 4,
            [SMEM, of_seq(s, (rows, width)), vec, vec]
            + [cols(width, LANES, 4 * n) for n in range(3)] + [PAIR],
            [(full((rows, width)), (rows, width), BF)]
            + [(act, (rows, width), BF)] * 3
            + [(big, (rows, 2048), BF)] * 2 + [xs_out],
            flops=rows * 4_800_000, nbytes=12 * 2**20,
        )(meta, inputs, g1, n1, qkv_weight, qkv_weight, qkv_weight, fx)
        maps.append(outs)
    state = [comm.carry(m[6], False) for m in maps]
    for s in range(seqs):
        h1, qs, ks, vv, pq, pk, _ = maps[s]
        locals_.append(
            call(
                local_kernel, 4, [big, big, act],
                [(cols(rows, 256), (rows, 1024), F32)],
                flops=rows * 6_000_000, nbytes=7 * 2**20,
            )(pq, pk, vv)[0]
        )
    mids = []
    for s in range(seqs):
        pq = maps[s][4]
        mids.append(
            call(
                functools.partial(middle_kernel, s), wide // 512,
                [SMEM, of_seq(s, (rows, width)), of_seq(s, (rows, width)), full((rows, 2048)),
                 full((rows, 1024)), full((2, 136, 512)), vec, vec, full((width, width)),
                 cols(width, 512), pl.BlockSpec((512, width), lambda p: (p, 0))],
                [(full((rows, width)), (rows, width), BF),
                 (full((rows, width)), (rows, width), F32),
                 (full((rows, 1024)), (rows, 1024), BF),
                 (full((rows, width)), (rows, width), BF),
                 (full((rows, width)), (rows, width), BF),
                 (full((rows, width)), (rows, width), BF),
                 (full((rows, width)), (rows, width), BF),
                 (cols(rows, 512), (rows, wide), BF),
                 (cols(rows, 512), (rows, wide), BF),
                 (full((2, 136, 512)), (2, 136, 512), F32),
                 (full((8, width)), (8, width), F32)],
                scratch=[pltpu.VMEM((rows, width), F32), pltpu.VMEM((rows, width), F32),
                         pltpu.VMEM((rows, LANES), F32)]
                + [pltpu.VMEM((rows, width), F32)] * 3,
                flops=rows * 11_000_000, nbytes=24 * 2**20,
            )(meta, inputs, cotangent, pq, locals_[s], state[s], g2, n2, out_weight,
              up_weight, down_weight)
        )
    out, dx1, dx, a_low, db, h2, df, gl, du, gs, ng2 = zip(*mids)
    later = [comm.carry(g, True) for g in gs]
    down_grad = weight_grad(gl, df, True)
    up_grad = weight_grad(h2, du, False)
    outw_grad = weight_grad(a_low, db, True)
    up_grad = comm.total(up_grad, ("c", "x", "y", "z1", "z2"))
    down_grad = comm.total(down_grad, ("c", "y", "x", "z1", "z2"))
    outw_grad = comm.total(outw_grad, ("c", "x", "y", "z1", "z2"))
    inner = []
    for s in range(seqs):
        h1, qs, ks, vv, pq, pk, _ = maps[s]
        inner.append(
            call(
                inner_kernel, 4, [act, act, act, big, big, cols(rows, 256), HALF, PAIR],
                [(act, (rows, width), BF), (act, (rows, width), F32), (act, (rows, width), F32)],
                flops=rows * 20_000_000, nbytes=11 * 2**20,
            )(qs, ks, vv, pq, pk, dx[s], state[s], fx)
        )
    lasts = []
    for s in range(seqs):
        h1, qs, ks, vv, pq, pk, _ = maps[s]
        dq, dkl, dvl = inner[s]
        lasts.append(
            call(
                functools.partial(last_kernel, s), 4,
                [of_seq(s, (rows, width)), full((rows, width)), vec, act, act, big, HALF, PAIR,
                 act, act, act] + [cols(width, LANES, 4 * n) for n in range(3)],
                [(full((rows, width)), (rows, width), F32), (act, (rows, width), BF),
                 (act, (rows, width), BF), (full((8, width)), (8, width), F32)],
                scratch=[pltpu.VMEM((rows, width), F32)],
                flops=rows * 6_000_000, nbytes=11 * 2**20,
            )(inputs, dx1[s], g1, ks, vv, pk, later[s], fx, dq, dkl, dvl,
              qkv_weight, qkv_weight, qkv_weight)
        )
    grad, dk, dv, ng1 = zip(*lasts)
    h1 = [m[0] for m in maps]
    dq = [i[0] for i in inner]
    qkv_grad = jnp.concatenate(
        [weight_grad(h1, d, True) for d in (dq, dk, dv)], axis=1
    )
    qkv_grad = comm.total(qkv_grad, ("c", "y", "x", "z1", "z2"))
    small = jnp.concatenate([(ng1[0] + ng1[1])[:2], (ng2[0] + ng2[1])[:2]], axis=0)
    small = comm.total_small(small)
    return (
        jnp.stack(out),
        jnp.stack(grad),
        small[0],
        small[1],
        qkv_grad,
        outw_grad,
        small[2],
        small[3],
        up_grad,
        down_grad,
    )


def solution(mesh):
    comm = AnySlice()
    if dict(mesh.shape) == {"seq": 8, "batch": 4}:
        comm = Slice32()
        mesh = Mesh(mesh.devices.reshape(4, 2, 2, 2), comm.axes)
    return jax.shard_map(
        functools.partial(body, comm),
        mesh=mesh,
        in_specs=(comm.rows, comm.lens) + (P(),) * 9 + (comm.rows,),
        out_specs=(comm.rows, comm.rows) + (P(),) * 8,
        check_vma=False,
    )
```

time: 515 us -> 428 us (0.83)
  matrix products: 151 us -> 0 us
  Pallas kernels: 0 us -> 129 us
  local copies, waits for them, and re-layouts: 71.8 us -> 20 us
  other arithmetic: 60.1 us -> 30.9 us
  waiting for transfers between devices: 148 us -> 163 us
  starting transfers between devices: 71.3 us -> 77.4 us
    dot_general x30 -> x0, matrix products: 151 us -> none  [the longest x1 14.3 us: body(): jnp.einsum('sihm,sjhm->shij', query_low, key_low, preferred_element_type=...]
    pallas_call x0 -> x16, Pallas kernels: none -> 129 us  [the longest x2 34.3 us: body(): call(functools.partial(middle_kernel, s), wide // 512, [SMEM, of_seq(s, (...]
    another operation x22 -> x0, local copies, waits for them, and re-layouts: 23.6 us -> none  [the longest x12 18.1 us: carried_in(): return (jnp.stack(states), jnp.stack(sums))]
    unnamed x168 -> x30, local copies, waits for them, and re-layouts: 21 us -> 0.41 us
    reduce_sum x7 -> x0, other arithmetic: 14.9 us -> none  [the longest x1 7.99 us: body(): jnp.sum(scores, axis=-1)]
    slice x17 -> x1, local copies, waits for them, and re-layouts: 10.8 us -> 0.99 us  [feature_blocks(): top = jnp.concatenate([f[:, 0], zero, half, zero, half, zero], axis=2)]
    ppermute x12, waiting for transfers between devices: 1.42 us -> 10 us  [carry(): arrived = lax.ppermute(out, 'z', [hop])]
    ppermute x53, starting transfers between devices: 55.4 us -> 61.7 us  [exchange(): return lax.ppermute(part, axis, pairs)]
  transfers between devices with their start and end apart: 65 -> 65, of which waited for: 31 -> 29; matrix products, arithmetic and copies ran while one was open for 34% -> 8% of each run, Pallas kernels for 0% -> 24%
where the time goes in v2:
time: 428 us; the launch traced here: 422 us
  waiting for transfers between devices  163 us (38%)
  Pallas kernels  129 us (30%)
  starting transfers between devices  77.4 us (18%)
  other arithmetic  30.9 us (7%)
  local copies, waits for them, and re-layouts  20 us (5%)
    ppermute x53, waiting for transfers between devices, exchange(): return lax.ppermute(part, axis, pairs)  153 us
    ppermute x53, starting transfers between devices, exchange(): return lax.ppermute(part, axis, pairs)  61.7 us
    pallas_call x2, Pallas kernels, body(): call(functools.partial(middle_kernel, s), wide // 512, [SMEM, of_seq(s, (...  34.3 us
    pallas_call x6, Pallas kernels, weight_grad(): call(weight_kernel, grid, [sa, sa, sb, sb], [(pl.BlockSpec((am, bn), inde...  25.8 us
    pallas_call x2, Pallas kernels, body(): call(inner_kernel, 4, [act, act, act, big, big, cols(rows, 256), HALF, PA...  20.6 us
    pallas_call x2, Pallas kernels, body(): call(functools.partial(last_kernel, s), 4, [of_seq(s, (rows, width)), ful...  18.5 us
    pallas_call x2, Pallas kernels, body(): call(functools.partial(map_kernel, s), 4, [SMEM, of_seq(s, (rows, width))...  17.8 us
    ppermute x12, starting transfers between devices, carry(): arrived = lax.ppermute(out, 'z', [hop])  15.7 us
  transfers between devices with their start and end apart: 65, of which 29 were waited for; matrix products, arithmetic and copies ran while one was open for 8% of the time, Pallas kernels for 24%

profile of v2, /device:TPU:0, one launch (start us, length us, event | category | flops | bytes accessed | tf_op | source)
XLA Modules:
  0.0 422.1 jit_solution(2869053776481712554)
XLA Ops:
  10.0 8.9 %shard_map.198 = (bf16[512,512]{1,0:T(8,128)(2,1)}, bf16[512,512]{1,0:T(8,128)(2,1)}, bf16[512,512]{1,0:T(8,128)(2,1)}, bf16[512,512]{1,0:T(8,128)(2,1)}, bf16[5...) custom-call(s32[3]{0:T(128)} %pad_add_fusion.meta, bf16[2,512,512]{2,1,0:T(8,128)(2,1)} %x.11, ...), custom_call_target="tpu_custom_call" | custom-call | flops 2457600000 | bytes 12582912 | tf_op jit(solution)/shard_map/pallas_call | solution.py:543
  22.9 8.9 %shard_map.195 = (bf16[512,512]{1,0:T(8,128)(2,1)}, bf16[512,512]{1,0:T(8,128)(2,1)}, bf16[512,512]{1,0:T(8,128)(2,1)}, bf16[512,512]{1,0:T(8,128)(2,1)}, bf16[5...) custom-call(s32[3]{0:T(128)} %pad_add_fusion.meta, bf16[2,512,512]{2,1,0:T(8,128)(2,1)} %x.11, ...), custom_call_target="tpu_custom_call" | custom-call | flops 2457600000 | bytes 12582912 | tf_op jit(solution)/shard_map/pallas_call | solution.py:543
  51.6 6.0 %shard_map.199.nd = f32[512,1024]{1,0:T(8,128)} custom-call(bf16[512,2048]{1,0:T(8,128)(2,1)} %get-tuple-element.65.pq, bf16[512,2048]{1,0:T(8,128)(2,1)} %get-tuple-element.66.pk, bf16[512,512]{1,0:T(8,128)(2,1)} %get-tuple-element.67.vv), custom_call_target="tpu_custom_call" | custom-call | flops 3072000000 | bytes 7340032 | tf_op jit(solution)/shard_map/pallas_call | solution.py:557
  60.6 6.0 %shard_map.196.nd = f32[512,1024]{1,0:T(8,128)} custom-call(bf16[512,2048]{1,0:T(8,128)(2,1)} %get-tuple-element.60.pq, bf16[512,2048]{1,0:T(8,128)(2,1)} %get-tuple-element.61.pk, bf16[512,512]{1,0:T(8,128)(2,1)} %get-tuple-element.62.vv), custom_call_target="tpu_custom_call" | custom-call | flops 3072000000 | bytes 7340032 | tf_op jit(solution)/shard_map/pallas_call | solution.py:557
  74.2 17.1 %shard_map.197 = (bf16[512,512]{1,0:T(8,128)(2,1)}, f32[512,512]{1,0:T(8,128)}, bf16[512,1024]{1,0:T(8,128)(2,1)}, bf16[512,512]{1,0:T(8,128)(2,1)}, bf16[512,51...) custom-call(s32[3]{0:T(128)} %pad_add_fusion.meta, ...), custom_call_target="tpu_custom_call" | custom-call | flops 5632000000 | bytes 25165824 | tf_op jit(solution)/shard_map/pallas_call | solution.py:567
  93.8 17.2 %shard_map.200 = (bf16[512,512]{1,0:T(8,128)(2,1)}, f32[512,512]{1,0:T(8,128)}, bf16[512,1024]{1,0:T(8,128)(2,1)}, bf16[512,512]{1,0:T(8,128)(2,1)}, bf16[512,51...) custom-call(s32[3]{0:T(128)} %pad_add_fusion.meta, ...), custom_call_target="tpu_custom_call" | custom-call | flops 5632000000 | bytes 25165824 | tf_op jit(solution)/shard_map/pallas_call | solution.py:567
  117.0 6.4 %shard_map.209 = f32[512,2048]{1,0:T(8,128)} custom-call(bf16[512,512]{1,0:T(8,128)(2,1)} %get-tuple-element.102.a0, bf16[512,512]{1,0:T(8,128)(2,1)} %get-tuple-element.103.a1, bf16[512,2048]{1,0:T(8,128)(2,1)} %get-tuple-element.104.b0, bf16[512,2048]{1,0:T(8,128)(2,1)} %get-tuple-element.105.b1), custom_call_target="tpu_custom_call" | custom-call | flops 2147483648 | bytes 9437184 | tf_op jit(solution)/shard_map/pallas_call | solution.py:499
  126.6 6.4 %shard_map.210 = f32[2048,512]{1,0:T(8,128)} custom-call(bf16[512,2048]{1,0:T(8,128)(2,1)} %get-tuple-element.106.a0, bf16[512,2048]{1,0:T(8,128)(2,1)} %get-tuple-element.107.a1, bf16[512,512]{1,0:T(8,128)(2,1)} %get-tuple-element.108.b0, bf16[512,512]{1,0:T(8,128)(2,1)} %get-tuple-element.109.b1), custom_call_target="tpu_custom_call" | custom-call | flops 2147483648 | bytes 9437184 | tf_op jit(solution)/shard_map/pallas_call | solution.py:499
  136.6 10.3 %shard_map.201 = (bf16[512,512]{1,0:T(8,128)(2,1)}, f32[512,512]{1,0:T(8,128)}, f32[512,512]{1,0:T(8,128)}) custom-call(bf16[512,512]{1,0:T(8,128)(2,1)} %get-tuple-element.73.qs, bf16[512,512]{1,0:T(8,128)(2,1)} %get-tuple-element.71.ks, bf16[512,512]{1,0:T(8,128)(2,1)} %get-tuple-element.62.vv, bf16[512,2048]{1,0:T(8,128)(2,1)} %get-tuple-element.60.pq, ...), custom_call_target="tpu_custom_call" | custom-call | flops 10240000000 | bytes 11534336 | tf_op jit(solution)/shard_map/pallas_call | solution.py:602
  148.6 10.3 %shard_map.203 = (bf16[512,512]{1,0:T(8,128)(2,1)}, f32[512,512]{1,0:T(8,128)}, f32[512,512]{1,0:T(8,128)}) custom-call(bf16[512,512]{1,0:T(8,128)(2,1)} %get-tuple-element.82.qs, bf16[512,512]{1,0:T(8,128)(2,1)} %get-tuple-element.80.ks, bf16[512,512]{1,0:T(8,128)(2,1)} %get-tuple-element.67.vv, bf16[512,2048]{1,0:T(8,128)(2,1)} %get-tuple-element.65.pq, ...), custom_call_target="tpu_custom_call" | custom-call | flops 10240000000 | bytes 11534336 | tf_op jit(solution)/shard_map/pallas_call | solution.py:602
  171.0 12.0 %collective-permute-start.39 = (f32[16,512]{1,0:T(8,128)S(1)}, f32[16,512]{1,0:T(8,128)S(1)}, u32[]{:S(2)}, u32[]{:S(2)}) collective-permute-start(f32[16,512]{1,0:T(8,128)S(1)} %constant_dynamic-slice_fusion.10), channel_id=1, source_target_pairs={{0,16},{16,0},{8,24},{24,8},{1,17},{17,1},{9,25},{25,9},{2,18},{18... | collective-permute-start | bytes 98312 | tf_op jit(solution)/shard_map/ppermute | solution.py:39
  184.1 6.4 %collective-permute-done.39 = f32[16,512]{1,0:T(8,128)S(1)} collective-permute-done((f32[16,512]{1,0:T(8,128)S(1)}, f32[16,512]{1,0:T(8,128)S(1)}, u32[]{:S(2)}, u32[]{:S(2)}) %collective-permute-start.39) | collective-permute-done | bytes 32800 | tf_op jit(solution)/shard_map/ppermute | solution.py:39
  199.2 6.1 %collective-permute-done.13 = f32[136,512]{1,0:T(8,128)S(1)} collective-permute-done((f32[136,512]{1,0:T(8,128)S(1)}, f32[136,512]{1,0:T(8,128)S(1)}, u32[]{:S(2)}, u32[]{:S(2)}) %collective-permute-start.13) | collective-permute-done | bytes 278560 | tf_op jit(solution)/shard_map/ppermute | solution.py:50
  220.8 9.1 %shard_map.202 = (f32[512,512]{1,0:T(8,128)}, bf16[512,512]{1,0:T(8,128)(2,1)}, bf16[512,512]{1,0:T(8,128)(2,1)}, f32[8,512]{1,0:T(8,128)}) custom-call(bf16[2,512,512]{2,1,0:T(8,128)(2,1)} %x.11, f32[512,512]{1,0:T(8,128)} %get-tuple-element.70.dx1, f32[1,512]{1,0:T(1,128)} %bitcast.69, bf16[512,512]{1,0:T(8,128)(2,1)} %get-tuple-element.71.ks, ...), custom_call_target="tpu_custom_call" | custom-call | flops 3072000000 | bytes 11534336 | tf_op jit(solution)/shard_map/pallas_call | solution.py:613
  230.9 9.3 %shard_map.204 = (f32[512,512]{1,0:T(8,128)}, bf16[512,512]{1,0:T(8,128)(2,1)}, bf16[512,512]{1,0:T(8,128)(2,1)}, f32[8,512]{1,0:T(8,128)}) custom-call(bf16[2,512,512]{2,1,0:T(8,128)(2,1)} %x.11, f32[512,512]{1,0:T(8,128)} %get-tuple-element.79.dx1, f32[1,512]{1,0:T(1,128)} %bitcast.70, bf16[512,512]{1,0:T(8,128)(2,1)} %get-tuple-element.80.ks, ...), custom_call_target="tpu_custom_call" | custom-call | flops 3072000000 | bytes 11534336 | tf_op jit(solution)/shard_map/pallas_call | solution.py:613
  267.9 16.9 %collective-permute-done.56 = f32[512,512]{1,0:T(8,128)S(1)} collective-permute-done((f32[512,512]{1,0:T(8,128)S(1)}, f32[512,512]{1,0:T(8,128)S(1)}, u32[]{:S(2)}, u32[]{:S(2)}) %collective-permute-start.56) | collective-permute-done | bytes 1048608 | tf_op jit(solution)/shard_map/ppermute | solution.py:39
  300.3 5.7 %collective-permute-done.47 = f32[64,2048]{1,0:T(8,128)S(1)} collective-permute-done((f32[64,2048]{1,0:T(8,128)S(1)}, f32[64,2048]{1,0:T(8,128)S(1)}, u32[]{:S(2)}, u32[]{:S(2)}) %collective-permute-start.47) | collective-permute-done | bytes 524320 | tf_op jit(solution)/shard_map/ppermute | solution.py:39
  307.4 7.0 %collective-permute-done.26 = f32[128,1536]{1,0:T(8,128)S(1)} collective-permute-done((f32[128,1536]{1,0:T(8,128)S(1)}, f32[128,1536]{1,0:T(8,128)S(1)}, u32[]{:S(2)}, u32[]{:S(2)}) %collective-permute-start.26) | collective-permute-done | bytes 786464 | tf_op jit(solution)/shard_map/ppermute | solution.py:39
  319.1 9.7 %collective-permute-done.59 = f32[64,512]{1,0:T(8,128)S(1)} collective-permute-done((f32[64,512]{1,0:T(8,128)S(1)}, f32[64,512]{1,0:T(8,128)S(1)}, u32[]{:S(2)}, u32[]{:S(2)}) %collective-permute-start.59) | collective-permute-done | bytes 131104 | tf_op jit(solution)/shard_map/ppermute | solution.py:39
  333.4 5.6 %collective-permute-done.60 = f32[64,512]{1,0:T(8,128)S(1)} collective-permute-done((f32[64,512]{1,0:T(8,128)S(1)}, f32[64,512]{1,0:T(8,128)S(1)}, u32[]{:S(2)}, u32[]{:S(2)}) %collective-permute-start.60) | collective-permute-done | bytes 131104 | tf_op jit(solution)/shard_map/ppermute | solution.py:39
  355.6 5.6 %collective-permute-done.31 = f32[32,1536]{1,0:T(8,128)S(1)} collective-permute-done((f32[32,1536]{1,0:T(8,128)S(1)}, f32[32,1536]{1,0:T(8,128)S(1)}, u32[]{:S(2)}, u32[]{:S(2)}) %collective-permute-start.31) | collective-permute-done | bytes 196640 | tf_op jit(solution)/shard_map/ppermute | solution.py:39
  363.9 6.0 %collective-permute-done.32 = f32[64,1536]{1,0:T(8,128)S(1)} collective-permute-done((f32[64,1536]{1,0:T(8,128)S(1)}, f32[64,1536]{1,0:T(8,128)S(1)}, u32[]{:S(2)}, u32[]{:S(2)}) %collective-permute-start.32) | collective-permute-done | bytes 393248 | tf_op jit(solution)/shard_map/ppermute | solution.py:39
  378.5 14.3 %collective-permute-done.33 = f32[128,1536]{1,0:T(8,128)S(1)} collective-permute-done((f32[128,1536]{1,0:T(8,128)S(1)}, f32[128,1536]{1,0:T(8,128)S(1)}, u32[]{:S(2)}, u32[]{:S(2)}) %collective-permute-start.33) | collective-permute-done | bytes 786464 | tf_op jit(solution)/shard_map/ppermute | solution.py:39
  393.1 17.1 %collective-permute-done.63 = f32[512,512]{1,0:T(8,128)S(1)} collective-permute-done((f32[512,512]{1,0:T(8,128)S(1)}, f32[512,512]{1,0:T(8,128)S(1)}, u32[]{:S(2)}, u32[]{:S(2)}) %collective-permute-start.63) | collective-permute-done | bytes 1048608 | tf_op jit(solution)/shard_map/ppermute | solution.py:39
  (279 shorter events, 191.8 us)
Async XLA Ops:
  92.2 66.7 %collective-permute-start.10 = (f32[136,512]{1,0:T(8,128)S(1)}, f32[136,512]{1,0:T(8,128)S(1)}, u32[]{:S(2)}, u32[]{:S(2)}) collective-permute-start(f32[136,512]{1,0:T(8,128)S(1)} %dynamic-slice_bitcast_fusion.1), channel_id=1, source_target_pairs={{0,4},{4,0},{1,5},{5,1},{2,6},{6,2},{3,7},{7,3},{8,12},{12,8},{9,1... | collective-permute-start | bytes 835592 | tf_op jit(solution)/shard_map/ppermute | solution.py:39
  112.0 49.4 %collective-permute-start.15 = (f32[136,512]{1,0:T(8,128)S(1)}, f32[136,512]{1,0:T(8,128)S(1)}, u32[]{:S(2)}, u32[]{:S(2)}) collective-permute-start(f32[136,512]{1,0:T(8,128)S(1)} %dynamic-slice_bitcast_fusion), channel_id=1, source_target_pairs={{0,4},{4,0},{1,5},{5,1},{2,6},{6,2},{3,7},{7,3},{8,12},{12,8},{9,1... | collective-permute-start | bytes 835592 | tf_op jit(solution)/shard_map/ppermute | solution.py:39
  116.9 30.0 %collective-permute-start.35 = (f32[256,512]{1,0:T(8,128)S(1)}, f32[256,512]{1,0:T(8,128)S(1)}, u32[]{:S(2)}, u32[]{:S(2)}) collective-permute-start(f32[256,512]{1,0:T(8,128)S(1)} %constant_dynamic-slice_fusion.14), channel_id=1, source_target_pairs={{0,1},{1,0},{2,3},{3,2},{4,5},{5,4},{6,7},{7,6},{8,9},{9,8},{10,11... | collective-permute-start | bytes 1572872 | tf_op jit(solution)/shard_map/ppermute | solution.py:39
  136.1 124.0 %collective-permute-start.55 = (f32[1024,512]{1,0:T(8,128)}, f32[1024,512]{1,0:T(8,128)}, u32[]{:S(2)}, u32[]{:S(2)}) collective-permute-start(f32[1024,512]{1,0:T(8,128)} %constant_dynamic-slice_fusion.4), channel_id=1, source_target_pairs={{0,1},{1,0},{2,3},{3,2},{4,5},{5,4},{6,7},{7,6},{8,9},{9,8},{10,11... | collective-permute-start | bytes 6291464 | tf_op jit(solution)/shard_map/ppermute | solution.py:39
  136.6 127.5 %collective-permute-start.45 = (f32[256,2048]{1,0:T(8,128)}, f32[256,2048]{1,0:T(8,128)}, u32[]{:S(2)}, u32[]{:S(2)}) collective-permute-start(f32[256,2048]{1,0:T(8,128)} %constant_dynamic-slice_fusion.9), channel_id=1, source_target_pairs={{0,1},{1,0},{2,3},{3,2},{4,5},{5,4},{6,7},{7,6},{8,9},{9,8},{10,11... | collective-permute-start | bytes 6291464 | tf_op jit(solution)/shard_map/ppermute | solution.py:39
  169.5 24.2 %collective-permute-start.12 = (f32[136,512]{1,0:T(8,128)S(1)}, f32[136,512]{1,0:T(8,128)S(1)}, u32[]{:S(2)}, u32[]{:S(2)}) collective-permute-start(f32[136,512]{1,0:T(8,128)S(1)} %add.300), channel_id=1, source_target_pairs={{16,8},{17,9},{18,10},{19,11},{20,12},{21,13},{22,14},{23,15}} | collective-permute-start | bytes 835592 | tf_op jit(solution)/shard_map/ppermute | solution.py:50
  170.3 24.8 %collective-permute-start.17 = (f32[136,512]{1,0:T(8,128)S(1)}, f32[136,512]{1,0:T(8,128)S(1)}, u32[]{:S(2)}, u32[]{:S(2)}) collective-permute-start(f32[136,512]{1,0:T(8,128)S(1)} %add.307), channel_id=1, source_target_pairs={{16,8},{17,9},{18,10},{19,11},{20,12},{21,13},{22,14},{23,15}} | collective-permute-start | bytes 835592 | tf_op jit(solution)/shard_map/ppermute | solution.py:50
  171.0 19.4 %collective-permute-start.39 = (f32[16,512]{1,0:T(8,128)S(1)}, f32[16,512]{1,0:T(8,128)S(1)}, u32[]{:S(2)}, u32[]{:S(2)}) collective-permute-start(f32[16,512]{1,0:T(8,128)S(1)} %constant_dynamic-slice_fusion.10), channel_id=1, source_target_pairs={{0,16},{16,0},{8,24},{24,8},{1,17},{17,1},{9,25},{25,9},{2,18},{18... | collective-permute-start | bytes 98312 | tf_op jit(solution)/shard_map/ppermute | solution.py:39
  195.1 16.6 %collective-permute-start.18 = (f32[136,512]{1,0:T(8,128)S(1)}, f32[136,512]{1,0:T(8,128)S(1)}, u32[]{:S(2)}, u32[]{:S(2)}) collective-permute-start(f32[136,512]{1,0:T(8,128)S(1)} %add.309), channel_id=1, source_target_pairs={{8,0},{9,1},{10,2},{11,3},{12,4},{13,5},{14,6},{15,7}} | collective-permute-start | bytes 835592 | tf_op jit(solution)/shard_map/ppermute | solution.py:50
  216.6 43.4 %collective-permute-start.43 = (f32[128,512]{1,0:T(8,128)S(1)}, f32[128,512]{1,0:T(8,128)S(1)}, u32[]{:S(2)}, u32[]{:S(2)}) collective-permute-start(f32[128,512]{1,0:T(8,128)S(1)} %pad_maximum_fusion.22), channel_id=1, source_target_pairs={{0,2},{2,0},{1,3},{3,1},{4,6},{6,4},{5,7},{7,5},{8,10},{10,8},{9,1... | collective-permute-start | bytes 786440 | tf_op jit(solution)/shard_map/ppermute | solution.py:39
  252.0 15.7 %collective-permute-start.25 = (f32[256,1536]{1,0:T(8,128)S(1)}, f32[256,1536]{1,0:T(8,128)S(1)}, u32[]{:S(2)}, u32[]{:S(2)}) collective-permute-start(f32[256,1536]{1,0:T(8,128)S(1)} %constant_dynamic-slice_fusion.19), channel_id=1, source_target_pairs={{0,1},{1,0},{2,3},{3,2},{4,5},{5,4},{6,7},{7,6},{8,9},{9,8},{10,11... | collective-permute-start | bytes 4718600 | tf_op jit(solution)/shard_map/ppermute | solution.py:39
  262.4 22.3 %collective-permute-start.56 = (f32[512,512]{1,0:T(8,128)S(1)}, f32[512,512]{1,0:T(8,128)S(1)}, u32[]{:S(2)}, u32[]{:S(2)}) collective-permute-start(f32[512,512]{1,0:T(8,128)S(1)} %constant_dynamic-slice_fusion.3), channel_id=1, source_target_pairs={{0,4},{4,0},{1,5},{5,1},{2,6},{6,2},{3,7},{7,3},{8,12},{12,8},{9,1... | collective-permute-start | bytes 3145736 | tf_op jit(solution)/shard_map/ppermute | solution.py:39
  266.0 25.5 %collective-permute-start.46 = (f32[128,2048]{1,0:T(8,128)S(1)}, f32[128,2048]{1,0:T(8,128)S(1)}, u32[]{:S(2)}, u32[]{:S(2)}) collective-permute-start(f32[128,2048]{1,0:T(8,128)S(1)} %constant_dynamic-slice_fusion.8), channel_id=1, source_target_pairs={{0,2},{2,0},{1,3},{3,1},{4,6},{6,4},{5,7},{7,5},{8,10},{10,8},{9,1... | collective-permute-start | bytes 3145736 | tf_op jit(solution)/shard_map/ppermute | solution.py:39
  267.6 144.7 %collective-permute-start.44 = (f32[256,512]{1,0:T(8,128)S(1)}, f32[256,512]{1,0:T(8,128)S(1)}, u32[]{:S(2)}, u32[]{:S(2)}) collective-permute-start(f32[256,512]{1,0:T(8,128)S(1)} %pad_maximum_fusion.18), channel_id=1, source_target_pairs={{0,1},{1,0},{2,3},{3,2},{4,5},{5,4},{6,7},{7,6},{8,9},{9,8},{10,11... | collective-permute-start | bytes 1572872 | tf_op jit(solution)/shard_map/ppermute | solution.py:39
  285.0 14.0 %collective-permute-start.57 = (f32[256,512]{1,0:T(8,128)S(1)}, f32[256,512]{1,0:T(8,128)S(1)}, u32[]{:S(2)}, u32[]{:S(2)}) collective-permute-start(f32[256,512]{1,0:T(8,128)S(1)} %constant_dynamic-slice_fusion.2), channel_id=1, source_target_pairs={{0,2},{2,0},{1,3},{3,1},{4,6},{6,4},{5,7},{7,5},{8,10},{10,8},{9,1... | collective-permute-start | bytes 1572872 | tf_op jit(solution)/shard_map/ppermute | solution.py:39
  291.7 14.3 %collective-permute-start.47 = (f32[64,2048]{1,0:T(8,128)S(1)}, f32[64,2048]{1,0:T(8,128)S(1)}, u32[]{:S(2)}, u32[]{:S(2)}) collective-permute-start(f32[64,2048]{1,0:T(8,128)S(1)} %constant_dynamic-slice_fusion.7), channel_id=1, source_target_pairs={{0,4},{4,0},{1,5},{5,1},{2,6},{6,2},{3,7},{7,3},{8,12},{12,8},{9,1... | collective-permute-start | bytes 1572872 | tf_op jit(solution)/shard_map/ppermute | solution.py:39
  292.5 21.9 %collective-permute-start.26 = (f32[128,1536]{1,0:T(8,128)S(1)}, f32[128,1536]{1,0:T(8,128)S(1)}, u32[]{:S(2)}, u32[]{:S(2)}) collective-permute-start(f32[128,1536]{1,0:T(8,128)S(1)} %constant_dynamic-slice_fusion.18), channel_id=1, source_target_pairs={{0,4},{4,0},{1,5},{5,1},{2,6},{6,2},{3,7},{7,3},{8,12},{12,8},{9,1... | collective-permute-start | bytes 2359304 | tf_op jit(solution)/shard_map/ppermute | solution.py:39
  299.1 16.7 %collective-permute-start.58 = (f32[128,512]{1,0:T(8,128)S(1)}, f32[128,512]{1,0:T(8,128)S(1)}, u32[]{:S(2)}, u32[]{:S(2)}) collective-permute-start(f32[128,512]{1,0:T(8,128)S(1)} %constant_dynamic-slice_fusion.1), channel_id=1, source_target_pairs={{0,8},{8,0},{16,24},{24,16},{1,9},{9,1},{17,25},{25,17},{2,10},{10... | collective-permute-start | bytes 786440 | tf_op jit(solution)/shard_map/ppermute | solution.py:39
  314.6 17.4 %collective-permute-start.27 = (f32[64,1536]{1,0:T(8,128)S(1)}, f32[64,1536]{1,0:T(8,128)S(1)}, u32[]{:S(2)}, u32[]{:S(2)}) collective-permute-start(f32[64,1536]{1,0:T(8,128)S(1)} %constant_dynamic-slice_fusion.17), channel_id=1, source_target_pairs={{0,2},{2,0},{1,3},{3,1},{4,6},{6,4},{5,7},{7,5},{8,10},{10,8},{9,1... | collective-permute-start | bytes 1179656 | tf_op jit(solution)/shard_map/ppermute | solution.py:39
  361.4 14.5 %collective-permute-start.52 = (f32[64,2048]{1,0:T(8,128)S(1)}, f32[64,2048]{1,0:T(8,128)S(1)}, u32[]{:S(2)}, u32[]{:S(2)}) collective-permute-start(f32[64,2048]{1,0:T(8,128)S(1)} %pad_maximum_fusion.19), channel_id=1, source_target_pairs={{0,4},{4,0},{1,5},{5,1},{2,6},{6,2},{3,7},{7,3},{8,12},{12,8},{9,1... | collective-permute-start | bytes 1572872 | tf_op jit(solution)/shard_map/ppermute | solution.py:39
  370.0 22.8 %collective-permute-start.33 = (f32[128,1536]{1,0:T(8,128)S(1)}, f32[128,1536]{1,0:T(8,128)S(1)}, u32[]{:S(2)}, u32[]{:S(2)}) collective-permute-start(f32[128,1536]{1,0:T(8,128)S(1)} %pad_maximum_fusion.13), channel_id=1, source_target_pairs={{0,4},{4,0},{1,5},{5,1},{2,6},{6,2},{3,7},{7,3},{8,12},{12,8},{9,1... | collective-permute-start | bytes 2359304 | tf_op jit(solution)/shard_map/ppermute | solution.py:39
  372.0 38.2 %collective-permute-start.63 = (f32[512,512]{1,0:T(8,128)S(1)}, f32[512,512]{1,0:T(8,128)S(1)}, u32[]{:S(2)}, u32[]{:S(2)}) collective-permute-start(f32[512,512]{1,0:T(8,128)S(1)} %pad_maximum_fusion.12), channel_id=1, source_target_pairs={{0,4},{4,0},{1,5},{5,1},{2,6},{6,2},{3,7},{7,3},{8,12},{12,8},{9,1... | collective-permute-start | bytes 3145736 | tf_op jit(solution)/shard_map/ppermute | solution.py:39
  376.1 34.7 %collective-permute-start.53 = (f32[128,2048]{1,0:T(8,128)S(1)}, f32[128,2048]{1,0:T(8,128)S(1)}, u32[]{:S(2)}, u32[]{:S(2)}) collective-permute-start(f32[128,2048]{1,0:T(8,128)S(1)} %pad_maximum_fusion.11), channel_id=1, source_target_pairs={{0,2},{2,0},{1,3},{3,1},{4,6},{6,4},{5,7},{7,5},{8,10},{10,8},{9,1... | collective-permute-start | bytes 3145736 | tf_op jit(solution)/shard_map/ppermute | solution.py:39
  393.0 20.5 %collective-permute-start.34 = (f32[256,1536]{1,0:T(8,128)S(1)}, f32[256,1536]{1,0:T(8,128)S(1)}, u32[]{:S(2)}, u32[]{:S(2)}) collective-permute-start(f32[256,1536]{1,0:T(8,128)S(1)} %pad_maximum_fusion.8), channel_id=1, source_target_pairs={{0,1},{1,0},{2,3},{3,2},{4,5},{5,4},{6,7},{7,6},{8,9},{9,8},{10,11... | collective-permute-start | bytes 4718600 | tf_op jit(solution)/shard_map/ppermute | solution.py:39
  (55 other events, 484.7 us)

commit v3 on v2

v3 whole, which is shorter than its diff:
```python
import functools

import jax
import jax.numpy as jnp
from jax import lax
from jax.experimental import pallas as pl
from jax.experimental.pallas import tpu as pltpu
from jax.sharding import Mesh, PartitionSpec as P

EPS = 1e-05
SHRINK = 64 ** (-0.25)
SCALE = 256 ** (-0.5)


class Slice32:
    axes = ("z", "y", "x", "c")
    rows = P(("x", "c"), ("z", "y"), None)
    lens = P(("x", "c"))
    swaps = {
        "c": ("c", [(0, 1), (1, 0)]),
        "x": ("x", [(0, 1), (1, 0)]),
        "y": ("y", [(0, 1), (1, 0)]),
        "z1": ("z", [(0, 1), (1, 0), (2, 3), (3, 2)]),
        "z2": ("z", [(0, 2), (2, 0), (1, 3), (3, 1)]),
    }

    def position(self):
        return lax.axis_index("z") * 2 + lax.axis_index("y")

    def bits(self):
        z = lax.axis_index("z")
        at = [lax.axis_index(a) for a in "cxy"] + [z % 2, z // 2]
        return jnp.stack(at).astype(jnp.int32)

    def swap(self, part, axis):
        name, pairs = self.swaps[axis]
        return lax.ppermute(part, name, pairs)

    def whole_sum(self, part):
        return lax.psum(part, self.axes)

    def carry(self, keep, give, bits, reverse):
        after = yield
        got = self.swap(give, "y")
        after = yield give
        total = simple(add_kernel, after, keep, got)
        hops = [(3, 2), (2, 1), (1, 0)] if reverse else [(0, 1), (1, 2), (2, 3)]
        out, arrived = total, []
        for hop in hops:
            arrived.append(lax.ppermute(out, "z", [hop]))
            after = yield out
            if len(arrived) < 3:
                out = simple(add_kernel, after, total, arrived[-1])
        mine, send = call(
            functools.partial(close_kernel, reverse), 1, [SMEM] + [full(keep.shape)] * 5,
            [(full(keep.shape), keep.shape, F32)] * 2, flops=keep.size, nbytes=28 * keep.size,
        )(bits, keep, got, *arrived, after=after)
        other = self.swap(send, "y")
        yield send
        yield mine, other

    ways = {"x": 1, "y": 2, "z1": 3, "z2": 4}

    def sums(self, give, keep, bits, shapes, order):
        if order is None:
            return self.halves_sum(give, keep, bits, shapes)
        return self.chain_sum(give, keep, bits, shapes, order)

    def chain_sum(self, give, keep, bits, shapes, order):
        after = yield
        got = self.swap(give, "c")
        after = yield give
        rows, wide = give.shape
        part = keep()
        for axis in order:
            half = part.shape[0] // 2
            spec = (full((half, wide)), (half, wide), F32)
            give, part = call(
                functools.partial(fold_kernel, (self.ways[axis],), 2), 1,
                [SMEM] + [full(part.shape)] * 2, [spec] * 2, nbytes=16 * part.size,
            )(bits, part, got, after=after)
            got = self.swap(give, axis)
            after = yield give
        part = simple(add_kernel, after, part, got)
        got = self.swap(part, order[-1])
        after = yield part
        for n in range(len(order) - 1, 0, -1):
            (part,) = self.join((self.ways[order[n]],), bits, (part, got), after)
            got = self.swap(part, order[n - 1])
            after = yield part
        (part,) = self.join((self.ways[order[0]],), bits, (part, got), after)
        got = self.swap(part, "c")
        after = yield part
        yield call(
            last_join_kernel, 1, [SMEM] + [full((rows, wide))] * 2,
            [(full(s), s, F32) for s in shapes], nbytes=16 * rows * wide,
        )(bits, part, got, after=after)

    def halves_sum(self, give, keep, bits, shapes):
        after = yield
        got = self.swap(give, "c")
        after = yield give
        rows, wide = give.shape

        def fold(ways, parts, after, count):
            size = parts[0].shape[0] // count
            shape = (size, wide)
            outs = [(full(shape), shape, F32)] * (4 if count == 4 else 2 * len(ways))
            return call(
                functools.partial(fold_kernel, ways, count), 1,
                [SMEM] + [full(p.shape) for p in parts], outs,
                flops=parts[0].size, nbytes=12 * parts[0].size,
            )(bits, *parts, after=after)

        give_a, give_b, keep_a, keep_b = fold((1, 2), (keep(), got), after, 4)
        got_a, got_b = self.swap(give_a, "x"), self.swap(give_b, "y")
        after = yield give_a
        give_a, give_b, keep_a, keep_b = fold((2, 1), (keep_a, got_a, keep_b, got_b), after, 2)
        got_a, got_b = self.swap(give_a, "y"), self.swap(give_b, "x")
        after = yield give_a
        both = rows // 4
        part = (full((both // 2, wide)), (both // 2, wide), F32)
        ins = [SMEM] + [full((both // 2, wide))] * 4
        give, keep = call(merge_kernel, 1, ins, [part] * 2, nbytes=24 * both * wide)(
            bits, keep_a, got_a, keep_b, got_b, after=after
        )
        got = self.swap(give, "z1")
        after = yield give
        give, keep = fold((4,), (keep, got), after, 2)
        got = self.swap(give, "z2")
        after = yield give
        one = simple(add_kernel, after, keep, got)
        got = self.swap(one, "z2")
        after = yield one
        (two,) = self.join((4,), bits, (one, got), after)
        got = self.swap(two, "z1")
        after = yield two
        (four,) = self.join((3,), bits, (two, got), after)
        a, b = four[: both // 2], four[both // 2 :]
        got_a, got_b = self.swap(a, "y"), self.swap(b, "x")
        after = yield a
        a, b = self.join((2, 1), bits, (a, got_a, b, got_b), after)
        got_a, got_b = self.swap(a, "x"), self.swap(b, "y")
        after = yield a
        part = call(
            functools.partial(join_kernel, (1, 2), True), 1,
            [SMEM] + [full(a.shape)] * 4, [(full((rows, wide)), (rows, wide), F32)],
            nbytes=8 * rows * wide,
        )(bits, a, got_a, b, got_b, after=after)[0]
        got = self.swap(part, "c")
        after = yield part
        yield call(
            last_join_kernel, 1, [SMEM] + [full((rows, wide))] * 2,
            [(full(s), s, F32) for s in shapes], nbytes=16 * rows * wide,
        )(bits, part, got, after=after)

    def join(self, ways, bits, parts, after):
        rows, wide = parts[0].shape
        out = (full((2 * rows, wide)), (2 * rows, wide), F32)
        return call(
            functools.partial(join_kernel, ways, False), 1,
            [SMEM] + [full(p.shape) for p in parts], [out] * len(ways),
            nbytes=16 * rows * wide,
        )(bits, *parts, after=after)


class AnySlice:
    axes = ("seq", "batch")
    rows = P("batch", "seq", None)
    lens = P("batch")

    def position(self):
        return lax.axis_index("seq")

    def bits(self):
        return jnp.zeros((5,), jnp.int32)

    def whole_sum(self, part):
        return lax.psum(part, self.axes)

    def carry(self, keep, give, bits, reverse):
        size = lax.axis_size("seq")

        def shift(part, by):
            pairs = [(i, i + by) for i in range(size - by)]
            return lax.ppermute(part, "seq", [(b, a) for a, b in pairs] if reverse else pairs)

        for _ in range(6):
            yield keep
        out, by = shift(jnp.stack([keep, give]), 1), 1
        while by < size:
            out, by = out + shift(out, by), by * 2
        yield out[0], out[1]

    def sums(self, give, keep, bits, shapes, order):
        for _ in range(11):
            yield give
        part = lax.psum(jnp.concatenate([keep(), give], axis=0), self.axes)
        outs, at = [], 0
        for shape in shapes:
            outs.append(part[:, at : at + shape[1]])
            at += shape[1]
        yield outs


LANES = 128
BF = jnp.bfloat16
F32 = jnp.float32


def mm(a, b):
    return jnp.dot(a, b, preferred_element_type=F32)


def mm_t(a, b):
    return lax.dot_general(a, b, (((1,), (1,)), ((), ())), preferred_element_type=F32)


def lanes_of(width):
    return lax.broadcasted_iota(jnp.int32, (1, width), 1)


def head_of(width):
    return (lanes_of(width) % LANES) // 64


def live_of(meta, s, rows):
    at = lax.broadcasted_iota(jnp.int32, (rows, 1), 0) + meta[0]
    return (at < meta[1 + s]).astype(F32)


def norm(values, gain, bias):
    mu = jnp.mean(values, axis=-1, keepdims=True)
    centred = values - mu
    inv = lax.rsqrt(jnp.mean(centred * centred, axis=-1, keepdims=True) + EPS)
    xhat = centred * inv
    return xhat * gain + bias, xhat, inv


def norm_grad(e, xhat, inv, gain):
    eg = e * gain
    return inv * (
        eg
        - jnp.mean(eg, axis=-1, keepdims=True)
        - xhat * jnp.mean(eg * xhat, axis=-1, keepdims=True)
    )


def blocks_of(f):
    shape = (f.shape[0], LANES)
    own = lax.broadcasted_iota(jnp.int32, shape, 0) // 256 == head_of(LANES)
    diagonal = jnp.where(own, jnp.concatenate([f, f], axis=1), jnp.zeros(shape, BF))
    half = jnp.where(own, -0.5, 0.0).astype(BF)
    return jnp.concatenate([diagonal, half], axis=1)


def two_rows(first, second):
    row = lax.broadcasted_iota(jnp.int32, (8, first.shape[1]), 0)
    return jnp.where(row == 0, first, jnp.where(row == 1, second, 0.0))


def map_kernel(
    s, meta, bits, x, gain, bias, wq, wk, wv, fx, h1, qs, ks, vv, pq, pk, keep, give
):
    p = pl.program_id(0)
    rows = x.shape[1]

    @pl.when(p == 0)
    def _():
        h1[...] = norm(x[0].astype(F32), gain[...], bias[...])[0].astype(BF)

    w = jnp.concatenate([wq[...], wk[...], wv[...]], axis=1)
    qkv = mm(h1[...], w)
    q = (SHRINK * qkv[:, :LANES]).astype(BF)
    k = (SHRINK * qkv[:, LANES : 2 * LANES]).astype(BF)
    v = qkv[:, 2 * LANES :].astype(BF)
    qs[...], ks[...], vv[...] = q, k, v

    fw = blocks_of(fx[0])
    fw = jnp.concatenate([fw, fw[:, LANES:]], axis=1)

    def phi(u):
        sq = jnp.square(u.astype(F32))
        hi = sq.astype(BF)
        lo = (sq - hi.astype(F32)).astype(BF)
        return jnp.exp(mm_t(jnp.concatenate([u, hi, lo], axis=1), fw)) * SCALE

    pq[...] = phi(q).astype(BF)
    phk = (phi(k) * live_of(meta, s, rows)).astype(BF)
    pk[...] = phk
    lhs = jnp.concatenate([v.T, jnp.ones((16, rows), BF)], axis=0)
    ds = mm(lhs, phk)
    for near, xs in ((True, keep), (False, give)):

        @pl.when((p // 2 == bits[2]) == near)
        def _():
            put_state(xs, 2 * (p % 2), ds[:64, :256], ds[128:129, :256])
            put_state(xs, 2 * (p % 2) + 1, ds[64:128, 256:], ds[128:129, 256:])


def put_state(xs, at, state, total):
    xs[at, :64] = state
    xs[at, 64:] = jnp.broadcast_to(total, (8, 256))


def add_kernel(*refs):
    *parts, out = refs
    total = parts[0][...]
    for part in parts[1:]:
        total = total + part[...]
    out[...] = total


def close_kernel(reverse, bits, keep, got, first, second, third, mine, send):
    before = (first[...] + second[...]) + third[...]
    early = (bits[2] == (1 if reverse else 0)).astype(F32)
    mine[...] = before + (1.0 - early) * got[...]
    send[...] = before + early * keep[...]


def fold_kernel(ways, count, bits, *refs):
    if count == 4:
        part, got, *outs = refs
        size = part.shape[0] // 4
        for n, way in enumerate(ways):
            bit = bits[way]
            for out, side in ((outs[n], 1 - bit), (outs[2 + n], bit)):
                at = pl.ds(pl.multiple_of((2 * n + side) * size, 8), size)
                out[...] = part[at, :] + got[at, :]
        return
    pairs = len(ways)
    for n, way in enumerate(ways):
        part, got = refs[2 * n], refs[2 * n + 1]
        outs = refs[2 * pairs :]
        size, bit = part.shape[0] // 2, bits[way]
        for out, side in ((outs[n], 1 - bit), (outs[pairs + n], bit)):
            at = pl.ds(pl.multiple_of(side * size, 8), size)
            out[...] = part[at, :] + got[at, :]


def merge_kernel(bits, part_a, got_a, part_b, got_b, give, keep):
    first = bits[3] == 0
    a, b = part_a[...] + got_a[...], part_b[...] + got_b[...]
    keep[...] = jnp.where(first, a, b)
    give[...] = jnp.where(first, b, a)


def join_kernel(ways, one, bits, *refs):
    outs = refs[2 * len(ways) :]
    for n, way in enumerate(ways):
        part, got = refs[2 * n], refs[2 * n + 1]
        size, bit = part.shape[0], bits[way]
        out, base = (outs[0], 2 * n * size) if one else (outs[n], 0)
        out[pl.ds(pl.multiple_of(base + bit * size, 8), size), :] = part[...]
        out[pl.ds(pl.multiple_of(base + (1 - bit) * size, 8), size), :] = got[...]


def last_join_kernel(bits, part, got, *outs):
    size, at = part.shape[0], 0
    for out in outs:
        wide = out.shape[1]
        for ref, side in ((part, bits[0]), (got, 1 - bits[0])):
            out[pl.ds(pl.multiple_of(side * size, 8), size), :] = ref[:, at : at + wide]
        at += wide


def below(rows, cols, shift):
    i = lax.broadcasted_iota(jnp.int32, (rows, cols), 0) + shift
    return lax.broadcasted_iota(jnp.int32, (rows, cols), 1) <= i


def local_kernel(pq, pk, vv, nd):
    rows = pq.shape[0]
    half = rows // 2
    v = vv[...]
    values = jnp.concatenate([v, jnp.ones_like(v)], axis=1)
    head = head_of(2 * LANES)
    top, low = None, None
    for h in range(2):
        cols = slice(256 * h, 256 * h + 256)
        mine = jnp.where(head == h, values, jnp.zeros_like(values))
        a0 = mm_t(pq[:half, cols], pk[:half, cols])
        a0 = jnp.where(below(half, half, 0), a0, 0.0).astype(BF)
        a1 = mm_t(pq[half:, cols], pk[:, cols])
        a1 = jnp.where(below(half, rows, half), a1, 0.0).astype(BF)
        t, l = mm(a0, mine[:half]), mm(a1, mine)
        top, low = (t, l) if h == 0 else (top + t, low + l)
    nd[:half] = top
    nd[half:] = low


def gelu_parts(u):
    c0, c1 = 0.7978845608028654, 0.044715
    sq = u * u
    t = jnp.tanh(u * (c0 + (c0 * c1) * sq))
    half_up = 0.5 + 0.5 * t
    slope = half_up + (0.5 * u) * (1.0 - t * t) * (c0 + (3.0 * c0 * c1) * sq)
    return u * half_up, slope


def state_of(mine, other, near, first):
    two = [jnp.where(near, mine[first + h], other[first + h]) for h in range(2)]
    st = jnp.concatenate([t[:64] for t in two], axis=1)
    return st, jnp.concatenate([t[64:65] for t in two], axis=1)


def middle_kernel(
    s, meta, bits, x, dy, pq, nd, mine, other, gain, bias, wo, wup, wdown,
    out, dx1, dx, a_low, db, h2, df, gl, du, gs_keep, gs_give, ng,
    x1, xhat, inv, f, dh2, den,
):
    c = pl.program_id(0)
    rows = x.shape[1]
    live = live_of(meta, s, rows)
    col = lanes_of(512)

    @pl.when(c == 0)
    def _():
        for p in range(4):
            st, z = state_of(mine, other, bits[2] == p // 2, 2 * (p % 2))
            zero = jnp.zeros_like(st)
            zb = jnp.broadcast_to(z, st.shape)
            rhs = jnp.concatenate(
                [
                    jnp.where(col < 256, st, zero),
                    jnp.where(col >= 256, st, zero),
                    jnp.where(col < 256, zb, zero),
                    jnp.where(col >= 256, zb, zero),
                ],
                axis=0,
            ).astype(BF)
            both = mm_t(pq[:, 512 * p : 512 * p + 512], rhs) + nd[:, 256 * p : 256 * p + 256]
            lanes = slice(LANES * p, LANES * p + LANES)
            den[:, lanes] = both[:, LANES:]
            f[:, lanes] = both[:, :LANES] / both[:, LANES:]
        a_low[...] = f[...].astype(BF)
        mid = x[0].astype(F32) + live * mm(a_low[...], wo[...])
        x1[...] = mid
        h, xh, iv = norm(mid, gain[...], bias[...])
        h2[...] = h.astype(BF)
        xhat[...] = xh
        inv[...] = jnp.broadcast_to(iv, inv.shape)
        df[...] = (live * dy[0].astype(F32)).astype(BF)

    g, slope = gelu_parts(mm(h2[...], wup[...]))
    g = g.astype(BF)
    gl[...] = g
    d = (slope * mm_t(df[...], wdown[...])).astype(BF)
    du[...] = d
    part = mm(g, wdown[...])
    back = mm_t(d, wup[...])

    @pl.when(c == 0)
    def _():
        x1[...] += live * part
        dh2[...] = back

    @pl.when(c > 0)
    def _():
        x1[...] += live * part
        dh2[...] += back

    @pl.when(c == pl.num_programs(0) - 1)
    def _():
        out[...] = x1[...].astype(BF)
        e = dh2[...]
        xh = xhat[...]
        ng[...] = two_rows(
            jnp.sum(e * xh, axis=0, keepdims=True), jnp.sum(e, axis=0, keepdims=True)
        )
        g1 = dy[0].astype(F32) + norm_grad(e, xh, inv[:, :1], gain[...])
        dx1[...] = g1
        db[...] = (live * g1).astype(BF)
        da = mm_t(db[...], wo[...])
        block = jnp.where(
            lax.broadcasted_iota(jnp.int32, (2 * LANES, LANES), 0) % LANES // 64
            == lax.broadcasted_iota(jnp.int32, (2 * LANES, LANES), 1) // 64,
            -1.0,
            0.0,
        ).astype(BF)
        slot = lanes_of(LANES) % 64
        for p in range(4):
            lanes = slice(LANES * p, LANES * p + LANES)
            dn = da[:, lanes] / den[:, lanes]
            w = dn * f[:, lanes]
            hi = w.astype(BF)
            lo = (w - hi.astype(F32)).astype(BF)
            dd = mm(jnp.concatenate([hi, lo], axis=1), block)
            hi = dd.astype(BF).astype(F32)
            lo = dd - hi
            two = jnp.where((slot == 0) | (slot == 2), hi, jnp.where(slot == 1, lo, 0.0))
            both = jnp.concatenate([dn.astype(BF), two.astype(BF)], axis=1)
            dx[:, 256 * p : 256 * p + 256] = both
            g = mm(both.T, pq[:, 512 * p : 512 * p + 512])
            for near, gs in ((True, gs_keep), (False, gs_give)):

                @pl.when((bits[2] == p // 2) == near)
                def _(gs=gs, g=g):
                    for h in range(2):
                        side, at = slice(256 * h, 256 * h + 256), 128 + 64 * h
                        z = g[at : at + 1, side] + g[at + 1 : at + 2, side]
                        put_state(gs, 2 * (p % 2) + h, g[64 * h : 64 * h + 64, side], z)


def inner_kernel(bits, qs, ks, vv, pq, pk, dx, mine, other, fx, dq, dkl, dvl):
    p = pl.program_id(0)
    rows = pq.shape[0]
    half = rows // 2
    col = lanes_of(512)
    slot = lanes_of(LANES) % 64
    head = head_of(2 * LANES)
    ones = jnp.broadcast_to(jnp.where(slot < 2, 1.0, 0.0), (rows, LANES)).astype(BF)
    v1 = jnp.concatenate([vv[...], ones], axis=1)
    st, z = state_of(mine, other, bits[2] == p // 2, 0)
    zh = z.astype(BF).astype(F32)
    zl = z - zh
    zero = jnp.zeros_like(st)
    row = lax.broadcasted_iota(jnp.int32, (64, 512), 0)
    zr = jnp.where(row < 2, zh, jnp.where(row == 2, zl, 0.0))
    rhs = jnp.concatenate(
        [
            jnp.where(col < 256, st, zero),
            jnp.where(col >= 256, st, zero),
            jnp.where(col < 256, zr, zero),
            jnp.where(col >= 256, zr, zero),
        ],
        axis=0,
    ).astype(BF)
    d = dx[...]
    far = mm(d, rhs)
    eqs, eks = [], []
    top, low = None, None
    for h in range(2):
        cols = slice(256 * h, 256 * h + 256)
        own = jnp.where(head == h, d, jnp.zeros_like(d))
        q, k = pq[:, cols], pk[:, cols]
        a0 = jnp.where(below(half, half, 0), mm_t(own[:half], v1[:half]), 0.0).astype(BF)
        a1 = jnp.where(below(half, rows, half), mm_t(own[half:], v1), 0.0).astype(BF)
        dpq = jnp.concatenate([mm(a0, k[:half]), mm(a1, k)], axis=0) + far[:, cols]
        eqs.append((dpq * q.astype(F32)).astype(BF))
        i0 = lax.broadcasted_iota(jnp.int32, (half, rows), 1)
        up0 = i0 >= lax.broadcasted_iota(jnp.int32, (half, rows), 0)
        up1 = up0[:, :half]
        b0 = jnp.where(up0, mm_t(v1[:half], own), 0.0).astype(BF)
        b1 = jnp.where(up1, mm_t(v1[half:], own[half:]), 0.0).astype(BF)
        dpk = jnp.concatenate([mm(b0, q), mm(b1, q[half:])], axis=0)
        eks.append((dpk * k.astype(F32)).astype(BF))
        c0 = jnp.where(up0, mm_t(k[:half], q), 0.0).astype(BF)
        c1 = jnp.where(up1, mm_t(k[half:], q[half:]), 0.0).astype(BF)
        t, l = mm(c0, own[:, :LANES]), mm(c1, own[half:, :LANES])
        top, low = (t, l) if h == 0 else (top + t, low + l)
    fw = blocks_of(fx[0])
    r = mm(jnp.concatenate(eqs, axis=1), fw)
    dq[...] = (SHRINK * (r[:, :LANES] + 2.0 * qs[...].astype(F32) * r[:, LANES:])).astype(BF)
    r = mm(jnp.concatenate(eks, axis=1), fw)
    dkl[...] = r[:, :LANES] + 2.0 * ks[...].astype(F32) * r[:, LANES:]
    dvl[:half] = top
    dvl[half:] = low


def last_kernel(
    s, bits, x, dx1, gain, ks, vv, pk, mine, other, fx, dq, dkl, dvl, wq, wk, wv,
    grad, dk, dv, ng, dh1,
):
    p = pl.program_id(0)
    rows = pk.shape[0]
    col = lanes_of(512)
    slot = lanes_of(LANES) % 64
    ones = jnp.broadcast_to(jnp.where(slot < 2, 1.0, 0.0), (rows, LANES)).astype(BF)
    v1 = jnp.concatenate([vv[...], ones], axis=1)
    st, z = state_of(mine, other, bits[2] == p // 2, 0)
    zh = z.astype(BF).astype(F32)
    zl = z - zh
    zero = jnp.zeros_like(st)
    row = lax.broadcasted_iota(jnp.int32, (64, 512), 0)
    zr = jnp.where(row == 0, zh, jnp.where(row == 1, zl, 0.0))
    rhs = jnp.concatenate(
        [
            jnp.where(col < 256, st, zero),
            jnp.where(col >= 256, st, zero),
            jnp.where(col < 256, zr, zero),
            jnp.where(col >= 256, zr, zero),
        ],
        axis=0,
    ).astype(BF)
    dpk = mm(v1, rhs)
    ek = (dpk * pk[...].astype(F32)).astype(BF)
    r = mm(ek, blocks_of(fx[0]))
    k = SHRINK * (dkl[...] + r[:, :LANES] + 2.0 * ks[...].astype(F32) * r[:, LANES:])
    k = k.astype(BF)
    v = (dvl[...] + mm_t(pk[...], rhs[:LANES])).astype(BF)
    dk[...], dv[...] = k, v
    w = jnp.concatenate([wq[...], wk[...], wv[...]], axis=1)
    part = mm_t(jnp.concatenate([dq[...], k, v], axis=1), w)

    @pl.when(p == 0)
    def _():
        dh1[...] = part

    @pl.when(p > 0)
    def _():
        dh1[...] += part

    @pl.when(p == pl.num_programs(0) - 1)
    def _():
        _, xh, inv = norm(x[0].astype(F32), gain[...], gain[...])
        e = dh1[...]
        ng[...] = two_rows(
            jnp.sum(e * xh, axis=0, keepdims=True), jnp.sum(e, axis=0, keepdims=True)
        )
        grad[...] = dx1[...] + norm_grad(e, xh, inv, gain[...])


def weight_kernel(c, a0, a1, b0, b1, out):
    out[...] = mm(a0[...].T, b0[...]) + mm(a1[...].T, b1[...])


def late_kernel(c, a0, a1, b0, b1, b2, b3, b4, b5, n0, n1, n2, n3, o0, o1, d0, d1, out):
    a = jnp.concatenate([a0[...].T, a1[...].T], axis=1)
    for n, (first, second) in enumerate(((b0, b1), (b2, b3), (b4, b5))):
        both = jnp.concatenate([first[...], second[...]], axis=0)
        out[:, 512 * n : 512 * n + 512] = mm(a, both)
    out[:, 1536:2048] = mm(o0[...].T, d0[...]) + mm(o1[...].T, d1[...])
    sums = [n0[...] + n1[...], n2[...] + n3[...]]
    out[:, 2048:] = jnp.concatenate(sums + [jnp.zeros((112, out.shape[0]), F32)], axis=0).T


def params(limit=36):
    return pltpu.CompilerParams(vmem_limit_bytes=limit * 2**20)


def full(shape):
    return pl.BlockSpec(shape, lambda p, n=len(shape): (0,) * n)


def of_seq(s, shape):
    return pl.BlockSpec((1,) + shape, lambda p: (s, 0, 0))


def cols(rows, width, first=0):
    return pl.BlockSpec((rows, width), lambda p: (0, first + p))


SMEM = pl.BlockSpec(memory_space=pltpu.SMEM)
HEADS = pl.BlockSpec((2, 72, 256), lambda p: (p % 2, 0, 0))
PAIR = pl.BlockSpec((1, 512, 64), lambda p: (p, 0, 0))


def arr(shape, dtype):
    return jax.ShapeDtypeStruct(shape, dtype)


ANY = pl.BlockSpec(memory_space=pl.ANY)


def call(kernel, grid, ins, outs, scratch=(), flops=0, nbytes=0, scalars=0):
    def run(*args, after=()):
        count, waits = len(ins) + scalars, len(after)

        def waiting(*refs):
            kernel(*refs[:count], *refs[count + waits :])

        return pl.pallas_call(
            waiting,
            grid_spec=pltpu.PrefetchScalarGridSpec(
                num_scalar_prefetch=scalars,
                grid=(grid,),
                in_specs=list(ins) + [ANY] * waits,
                out_specs=[o[0] for o in outs],
                scratch_shapes=list(scratch),
            ),
            out_shape=[arr(*o[1:]) for o in outs],
            compiler_params=params(),
            cost_estimate=pl.CostEstimate(flops=flops, bytes_accessed=nbytes, transcendentals=0),
        )(*args, *after)

    return run


def simple(kernel, after, *parts):
    spec = full(parts[0].shape)
    return call(
        kernel, 1, [spec] * len(parts), [(spec, parts[0].shape, F32)],
        flops=parts[0].size, nbytes=12 * parts[0].size,
    )(*parts, after=after)[0]


def half_of(give):
    return (lambda c: 1 - c[0]) if give else (lambda c: c[0])


def whole(shape):
    return pl.BlockSpec(shape, lambda p, c: (0,) * len(shape))


def up_weights(give, bits, h2, du, after=()):
    rows, n = du[0].shape
    m = h2[0].shape[1] // 2
    at = half_of(give)
    sa = pl.BlockSpec((rows, m), lambda p, c: (0, at(c)))
    sb = pl.BlockSpec((rows, 512), lambda p, c: (0, p))
    return call(
        weight_kernel, n // 512, [sa, sa, sb, sb],
        [(pl.BlockSpec((m, 512), lambda p, c: (0, p)), (m, n), F32)],
        flops=4 * rows * m * n, nbytes=4 * m * n + 4 * rows * n, scalars=1,
    )(bits, *h2, *du, after=after)[0]


def down_weights(give, bits, gl, df, after=()):
    rows, n = df[0].shape
    m = gl[0].shape[1] // 2
    at, grid = half_of(give), m // 512
    sa = pl.BlockSpec((rows, 512), lambda p, c: (0, grid * at(c) + p))
    sb = whole((rows, n))
    return call(
        weight_kernel, grid, [sa, sa, sb, sb],
        [(pl.BlockSpec((512, n), lambda p, c: (p, 0)), (m, n), F32)],
        flops=4 * rows * m * n, nbytes=4 * m * n + 4 * rows * m, scalars=1,
    )(bits, *gl, *df, after=after)[0]


def late_weights(give, bits, h1, dq, dk, dv, ng1, ng2, a, db, after=()):
    rows, n = dk[0].shape
    m = n // 2
    at = half_of(give)
    sa, sb = pl.BlockSpec((rows, m), lambda p, c: (0, at(c))), whole((rows, n))
    sn = pl.BlockSpec((8, m), lambda p, c: (0, at(c)))
    wide = 4 * n + LANES
    return call(
        late_kernel, 1, [sa] * 2 + [sb] * 6 + [sn] * 4 + [sa] * 2 + [sb] * 2,
        [(whole((m, wide)), (m, wide), F32)],
        flops=16 * rows * m * n, nbytes=16 * m * n + 16 * rows * n, scalars=1,
    )(bits, *h1, *dq, *dk, *dv, *ng1, *ng2, *a, *db, after=after)[0]


ORDER = (
    "M0", "f", "M1", "f", "g", "A0", "f", "g", "A1", "f", "g", "f", "g", "N0", "g", "p", "N1",
    "p", "q", "Gu", "u", "Ku", "Gd", "p", "q", "d", "Kd", "u", "I0", "p", "q", "d", "I1",
    "p", "q", "u", "L0", "q", "d", "L1", "Gk", "k", "Kk", "u", "d", "k", "u", "d", "k",
    "u", "d", "k", "u", "d", "k", "u", "d", "k", "u", "d", "k", "u", "d", "k", "k", "k",
)


def body(
    comm,
    inputs,
    lengths,
    norm1_gain,
    norm1_bias,
    qkv_weight,
    features,
    out_weight,
    norm2_gain,
    norm2_bias,
    up_weight,
    down_weight,
    cotangent,
):
    seqs, rows, width = inputs.shape
    wide = up_weight.shape[1]
    first_row = (comm.position() * rows).astype(jnp.int32)
    meta = jnp.concatenate([first_row[None], lengths])
    fx = features.reshape(4, 512, 64)
    bits = comm.bits()
    g1, n1, g2, n2 = (v[None] for v in (norm1_gain, norm1_bias, norm2_gain, norm2_bias))
    vec = full((1, width))
    act = cols(rows, LANES)
    big = cols(rows, 512)
    heads = (4, 72, 256)
    states = [(full(heads), heads, F32)] * 2

    def maps_of(s, after):
        return call(
            functools.partial(map_kernel, s), 4,
            [SMEM, SMEM, of_seq(s, (rows, width)), vec, vec]
            + [cols(width, LANES, 4 * n) for n in range(3)] + [PAIR],
            [(full((rows, width)), (rows, width), BF)]
            + [(act, (rows, width), BF)] * 3
            + [(big, (rows, 2048), BF)] * 2 + states,
            flops=rows * 4_800_000, nbytes=12 * 2**20,
        )(meta, bits, inputs, g1, n1, qkv_weight, qkv_weight, qkv_weight, fx, after=after)

    def locals_of(s, after):
        _, _, _, vv, pq, pk, _, _ = maps[s]
        return call(
            local_kernel, 4, [big, big, act],
            [(cols(rows, 256), (rows, 1024), F32)],
            flops=rows * 6_000_000, nbytes=7 * 2**20,
        )(pq, pk, vv, after=after)[0]

    def middle_of(s, prefix, after):
        pq = maps[s][4]
        return call(
                functools.partial(middle_kernel, s), wide // 512,
                [SMEM, SMEM, of_seq(s, (rows, width)), of_seq(s, (rows, width)), full((rows, 2048)),
                 full((rows, 1024)), full(heads), full(heads), vec, vec, full((width, width)),
                 cols(width, 512), pl.BlockSpec((512, width), lambda p: (p, 0))],
                [(full((rows, width)), (rows, width), BF),
                 (full((rows, width)), (rows, width), F32),
                 (full((rows, 1024)), (rows, 1024), BF),
                 (full((rows, width)), (rows, width), BF),
                 (full((rows, width)), (rows, width), BF),
                 (full((rows, width)), (rows, width), BF),
                 (full((rows, width)), (rows, width), BF),
                 (cols(rows, 512), (rows, wide), BF),
                 (cols(rows, 512), (rows, wide), BF),
                 *states,
                 (full((8, width)), (8, width), F32)],
                scratch=[pltpu.VMEM((rows, width), F32), pltpu.VMEM((rows, width), F32),
                         pltpu.VMEM((rows, LANES), F32)]
                + [pltpu.VMEM((rows, width), F32)] * 3,
                flops=rows * 11_000_000, nbytes=24 * 2**20,
            )(meta, bits, inputs, cotangent, pq, locals_[s], *prefix, g2, n2, out_weight,
              up_weight, down_weight, after=after)

    def inner(s, after):
        _, qs, ks, vv, pq, pk, _, _ = maps[s]
        return call(
            inner_kernel, 4,
            [SMEM, act, act, act, big, big, cols(rows, 256), HEADS, HEADS, PAIR],
            [(act, (rows, width), BF), (act, (rows, width), F32), (act, (rows, width), F32)],
            flops=rows * 20_000_000, nbytes=11 * 2**20,
        )(bits, qs, ks, vv, pq, pk, mids[s][2], *state[s], fx, after=after)

    def last(s, later, after):
        _, qs, ks, vv, pq, pk, _, _ = maps[s]
        return call(
            functools.partial(last_kernel, s), 4,
            [SMEM, of_seq(s, (rows, width)), full((rows, width)), vec, act, act, big, HEADS, HEADS,
             PAIR,
             act, act, act] + [cols(width, LANES, 4 * n) for n in range(3)],
            [(full((rows, width)), (rows, width), F32), (act, (rows, width), BF),
             (act, (rows, width), BF), (full((8, width)), (8, width), F32)],
            scratch=[pltpu.VMEM((rows, width), F32)],
            flops=rows * 6_000_000, nbytes=11 * 2**20,
        )(bits, inputs, mids[s][1], g1, ks, vv, pk, *later, fx, *inners[s],
          qkv_weight, qkv_weight, qkv_weight, after=after)

    maps, locals_, mids, state, inners, lasts, kept, flows = {}, {}, {}, {}, {}, {}, {}, {}

    def of_mids(*index):
        return [[mids[s][n] for s in range(seqs)] for n in index]

    def weights(name, give, after):
        if name == "u":
            return up_weights(give, bits, *of_mids(5, 8), after=after)
        if name == "d":
            return down_weights(give, bits, *of_mids(7, 6), after=after)
        h1 = [maps[s][0] for s in range(seqs)]
        dq = [inners[s][0] for s in range(seqs)]
        dk, dv, ng1 = ([lasts[s][n] for s in range(seqs)] for n in (1, 2, 3))
        return late_weights(give, bits, h1, dq, dk, dv, ng1, *of_mids(11, 3, 4), after=after)

    shapes = {
        "u": ((width, wide),),
        "d": ((wide, width),),
        "k": ((width, 3 * width), (width, width), (width, LANES)),
    }
    orders = {"u": ("x", "y", "z1", "z2"), "d": ("y", "x", "z1", "z2"), "k": None}

    def play(items, token):
        for item in items:
            after = () if token is None else (token,)
            kind, name = item[0], item[-1]
            s = int(name) if name in "01" else None
            if kind == "M":
                maps[s] = maps_of(s, after)
                token = maps[s][7]
                flows["fg"[s]] = comm.carry(maps[s][6], token, bits, False)
                next(flows["fg"[s]])
            elif kind == "A":
                token = locals_[s] = locals_of(s, after)
            elif kind == "N":
                state[s] = next(flows["fg"[s]])
                mids[s] = middle_of(s, state[s], after)
                token = mids[s][10]
                flows["pq"[s]] = comm.carry(mids[s][9], token, bits, True)
                next(flows["pq"[s]])
            elif kind == "I":
                inners[s] = inner(s, after)
                token = inners[s][1]
            elif kind == "L":
                lasts[s] = last(s, next(flows["pq"[s]]), after)
                token = lasts[s][0]
            elif kind == "G":
                token = weights(name, True, after)
                flows[name] = comm.sums(
                    token, functools.partial(kept.get, name), bits, shapes[name], orders[name]
                )
                next(flows[name])
            elif kind == "K":
                token = kept[name] = weights(name, False, after)
            else:
                token = flows[name].send(after)
        return token

    end = (play(ORDER, None),)
    (up_grad,), (down_grad,) = flows["u"].send(end), flows["d"].send(end)
    qkv_grad, outw_grad, small = flows["k"].send(end)
    small = small[:, :16].T
    grad = jnp.stack([lasts[s][0] for s in range(seqs)])
    out = [mids[s][0] for s in range(seqs)]
    return (
        jnp.stack(out),
        grad,
        small[0],
        small[1],
        qkv_grad,
        outw_grad,
        small[8],
        small[9],
        up_grad,
        down_grad,
    )


def solution(mesh):
    comm = AnySlice()
    if dict(mesh.shape) == {"seq": 8, "batch": 4}:
        comm = Slice32()
        mesh = Mesh(mesh.devices.reshape(4, 2, 2, 2), comm.axes)
    return jax.shard_map(
        functools.partial(body, comm),
        mesh=mesh,
        in_specs=(comm.rows, comm.lens) + (P(),) * 9 + (comm.rows,),
        out_specs=(comm.rows, comm.rows) + (P(),) * 8,
        check_vma=False,
    )
```

time: 428 us -> 353 us (0.82)
  the two profiles are of different devices: /device:TPU:0 before, /device:TPU:25 now
where the time goes in v3:
time: 353 us; the launch traced here: 348 us
  waiting for transfers between devices  156 us (44%)
  Pallas kernels  123 us (35%)
  starting transfers between devices  50.2 us (14%)
  local copies, waits for them, and re-layouts  12.8 us (4%)
    ppermute x42, waiting for transfers between devices, swap(): return lax.ppermute(part, name, pairs)  145 us
    pallas_call x62, Pallas kernels, run(): pl.pallas_call(waiting, grid_spec=pltpu.PrefetchScalarGridSpec(num_scalar...  123 us
    ppermute x42, starting transfers between devices, swap(): return lax.ppermute(part, name, pairs)  36.5 us
    ppermute x12, starting transfers between devices, carry(): arrived.append(lax.ppermute(out, 'z', [hop]))  13.8 us
    unnamed x159, local copies, waits for them, and re-layouts  11.5 us
    ppermute x12, waiting for transfers between devices, carry(): arrived.append(lax.ppermute(out, 'z', [hop]))  10.3 us
  transfers between devices with their start and end apart: 54, of which 29 were waited for; matrix products, arithmetic and copies ran while one was open for 1% of the time, Pallas kernels for 24%

profile of v3, /device:TPU:25, one launch (start us, length us, event | category | flops | bytes accessed | tf_op | source)
XLA Modules:
  0.0 347.8 jit_solution(7569376107464485961)
XLA Ops:
  6.7 6.9 %shard_map.195 = (bf16[512,512]{1,0:T(8,128)(2,1)S(1)}, bf16[512,512]{1,0:T(8,128)(2,1)S(1)}, bf16[512,512]{1,0:T(8,128)(2,1)S(1)}, bf16[512,512]{1,0:T(8,128)(2...) custom-call(s32[3]{0:T(128)S(1)} %pad_add_fusion.refs_0_, ...), custom_call_target="tpu_custom_call" | custom-call | flops 2457600000 | bytes 12582912 | tf_op jit(solution)/shard_map/pallas_call | solution.py:663
  16.4 6.9 %shard_map.196 = (bf16[512,512]{1,0:T(8,128)(2,1)S(1)}, bf16[512,512]{1,0:T(8,128)(2,1)S(1)}, bf16[512,512]{1,0:T(8,128)(2,1)S(1)}, bf16[512,512]{1,0:T(8,128)(2...) custom-call(s32[3]{0:T(128)S(1)} %pad_add_fusion.refs_0_, ...), custom_call_target="tpu_custom_call" | custom-call | flops 2457600000 | bytes 12582912 | tf_op jit(solution)/shard_map/pallas_call | solution.py:663
  39.3 7.8 %collective-permute-done.4.refs_5_ = f32[4,72,256]{2,1,0:T(8,128)S(1)} collective-permute-done((f32[4,72,256]{2,1,0:T(8,128)S(1)}, f32[4,72,256]{2,1,0:T(8,128)S(1)}, u32[]{:S(2)}, u32[]{:S(2)}) %collective-permute-start.4) | collective-permute-done | bytes 294944 | tf_op jit(solution)/shard_map/ppermute | solution.py:50
  53.5 13.3 %shard_map.206 = (bf16[512,512]{1,0:T(8,128)(2,1)S(1)}, f32[512,512]{1,0:T(8,128)S(1)}, bf16[512,1024]{1,0:T(8,128)(2,1)S(1)}, bf16[512,512]{1,0:T(8,128)(2,1)S(...) custom-call(s32[3]{0:T(128)S(1)} %pad_add_fusion.refs_0_, ...), custom_call_target="tpu_custom_call" | custom-call | flops 5632000000 | bytes 25165824 | tf_op jit(solution)/shard_map/pallas_call | solution.py:663
  68.5 5.6 %collective-permute-done.9.refs_7_.refs_8_ = f32[4,72,256]{2,1,0:T(8,128)S(1)} collective-permute-done((f32[4,72,256]{2,1,0:T(8,128)S(1)}, f32[4,72,256]{2,1,0:T(8,128)S(1)}, u32[]{:S(2)}, u32[]{:S(2)}) %collective-permute-start.9) | collective-permute-done | bytes 294944 | tf_op jit(solution)/shard_map/ppermute | solution.py:37
  74.0 13.2 %shard_map.208 = (bf16[512,512]{1,0:T(8,128)(2,1)S(1)}, f32[512,512]{1,0:T(8,128)S(1)}, bf16[512,1024]{1,0:T(8,128)(2,1)S(1)}, bf16[512,512]{1,0:T(8,128)(2,1)S(...) custom-call(s32[3]{0:T(128)S(1)} %pad_add_fusion.refs_0_, ...), custom_call_target="tpu_custom_call" | custom-call | flops 5632000000 | bytes 25165824 | tf_op jit(solution)/shard_map/pallas_call | solution.py:663
  92.3 5.5 %collective-permute-start.13 = (f32[256,2048]{1,0:T(8,128)S(1)}, f32[256,2048]{1,0:T(8,128)S(1)}, u32[]{:S(2)}, u32[]{:S(2)}) collective-permute-start(f32[256,2048]{1,0:T(8,128)S(1)} %shard_map.210.refs_5_), channel_id=1, source_target_pairs={{0,1},{1,0},{2,3},{3,2},{4,5},{5,4},{6,7},{7,6},{8,9},{9,8},{10,11... | collective-permute-start | bytes 6291464 | tf_op jit(solution)/shard_map/ppermute | solution.py:37
  103.5 8.1 %collective-permute-done.10.refs_1_.refs_2_ = f32[4,72,256]{2,1,0:T(8,128)S(1)} collective-permute-done((f32[4,72,256]{2,1,0:T(8,128)S(1)}, f32[4,72,256]{2,1,0:T(8,128)S(1)}, u32[]{:S(2)}, u32[]{:S(2)}) %collective-permute-start.10) | collective-permute-done | bytes 294944 | tf_op jit(solution)/shard_map/ppermute | solution.py:37
  127.6 9.0 %shard_map.216 = (bf16[512,512]{1,0:T(8,128)(2,1)S(1)}, f32[512,512]{1,0:T(8,128)S(1)}, f32[512,512]{1,0:T(8,128)S(1)}) custom-call(s32[5]{0:T(128)S(1)} %stack.41.refs_1_.refs_0_, bf16[512,512]{1,0:T(8,128)(2,1)S(1)} %copy-done.74, bf16[512,512]{1,0:T(8,128)(2,1)S(1)} %copy-done.45, bf16[512,512]{1,0:T(8,128)(2,1)S(1)} %copy-done.47, ...), custom_call_target="tpu_custom_call" | custom-call | flops 10240000000 | bytes 11534336 | tf_op jit(solution)/shard_map/pallas_call | solution.py:663
  141.1 9.0 %shard_map.221 = (bf16[512,512]{1,0:T(8,128)(2,1)S(1)}, f32[512,512]{1,0:T(8,128)S(1)}, f32[512,512]{1,0:T(8,128)S(1)}) custom-call(s32[5]{0:T(128)S(1)} %stack.41.refs_1_.refs_0_, bf16[512,512]{1,0:T(8,128)(2,1)S(1)} %copy-done.72, bf16[512,512]{1,0:T(8,128)(2,1)S(1)} %copy-done.39, bf16[512,512]{1,0:T(8,128)(2,1)S(1)} %copy-done.42, ...), custom_call_target="tpu_custom_call" | custom-call | flops 10240000000 | bytes 11534336 | tf_op jit(solution)/shard_map/pallas_call | solution.py:663
  154.1 14.9 %collective-permute-done.18.refs_8_ = f32[4,72,256]{2,1,0:T(8,128)S(1)} collective-permute-done((f32[4,72,256]{2,1,0:T(8,128)S(1)}, f32[4,72,256]{2,1,0:T(8,128)S(1)}, u32[]{:S(2)}, u32[]{:S(2)}) %collective-permute-start.18) | collective-permute-done | bytes 294944 | tf_op jit(solution)/shard_map/ppermute | solution.py:37
  169.0 6.3 %shard_map.225 = (f32[512,512]{1,0:T(8,128)S(1)}, bf16[512,512]{1,0:T(8,128)(2,1)S(1)}, bf16[512,512]{1,0:T(8,128)(2,1)S(1)}, f32[8,512]{1,0:T(8,128)S(1)}) custom-call(s32[5]{0:T(128)S(1)} %stack.41.refs_1_.refs_0_, bf16[2,512,512]{2,1,0:T(8,128)(2,1)S(1)} %copy-done.3, f32[512,512]{1,0:T(8,128)S(1)} %copy-done.31, f32[1,512]{1,0:T(1,128)S(1)} %bitcast.29, ...), custom_call_target="tpu_custom_call" | custom-call | flops 3072000000 | bytes 11534336 | tf_op jit(solution)/shard_map/pallas_call | solution.py:663
  181.8 6.6 %shard_map.228 = (f32[512,512]{1,0:T(8,128)S(1)}, bf16[512,512]{1,0:T(8,128)(2,1)S(1)}, bf16[512,512]{1,0:T(8,128)(2,1)S(1)}, f32[8,512]{1,0:T(8,128)S(1)}) custom-call(s32[5]{0:T(128)S(1)} %stack.41.refs_1_.refs_0_, bf16[2,512,512]{2,1,0:T(8,128)(2,1)S(1)} %copy-done.3, f32[512,512]{1,0:T(8,128)S(1)} %copy-done.29, f32[1,512]{1,0:T(1,128)S(1)} %bitcast.30, ...), custom_call_target="tpu_custom_call" | custom-call | flops 3072000000 | bytes 11534336 | tf_op jit(solution)/shard_map/pallas_call | solution.py:663
  197.8 10.9 %collective-permute-done.26.refs_2_ = f32[64,2048]{1,0:T(8,128)S(1)} collective-permute-done((f32[64,2048]{1,0:T(8,128)}, f32[64,2048]{1,0:T(8,128)S(1)}, u32[]{:S(2)}, u32[]{:S(2)}) %collective-permute-start.26) | collective-permute-done | bytes 524320 | tf_op jit(solution)/shard_map/ppermute | solution.py:37
  218.7 5.0 %collective-permute-done.29.refs_2_ = f32[128,512]{1,0:T(8,128)S(1)} collective-permute-done((f32[128,512]{1,0:T(8,128)S(1)}, f32[128,512]{1,0:T(8,128)S(1)}, u32[]{:S(2)}, u32[]{:S(2)}) %collective-permute-start.29) | collective-permute-done | bytes 262176 | tf_op jit(solution)/shard_map/ppermute | solution.py:37
  229.5 10.3 %collective-permute-done.34.refs_1_ = f32[16,2048]{1,0:T(8,128)S(1)} collective-permute-done((f32[16,2048]{1,0:T(8,128)S(1)}, f32[16,2048]{1,0:T(8,128)S(1)}, u32[]{:S(2)}, u32[]{:S(2)}) %collective-permute-start.34) | collective-permute-done | bytes 131104 | tf_op jit(solution)/shard_map/ppermute | solution.py:37
  239.9 5.5 %collective-permute-done.33.refs_1_ = f32[64,512]{1,0:T(8,128)S(1)} collective-permute-done((f32[64,512]{1,0:T(8,128)S(1)}, f32[64,512]{1,0:T(8,128)S(1)}, u32[]{:S(2)}, u32[]{:S(2)}) %collective-permute-start.33) | collective-permute-done | bytes 131104 | tf_op jit(solution)/shard_map/ppermute | solution.py:37
  252.3 5.8 %collective-permute-done.35.refs_2_ = f32[32,2176]{1,0:T(8,128)S(1)} collective-permute-done((f32[32,2176]{1,0:T(8,128)S(1)}, f32[32,2176]{1,0:T(8,128)S(1)}, u32[]{:S(2)}, u32[]{:S(2)}) %collective-permute-start.35) | collective-permute-done | bytes 278560 | tf_op jit(solution)/shard_map/ppermute | solution.py:37
  258.8 5.0 %collective-permute-done.40.refs_2_ = f32[32,2048]{1,0:T(8,128)S(1)} collective-permute-done((f32[32,2048]{1,0:T(8,128)S(1)}, f32[32,2048]{1,0:T(8,128)S(1)}, u32[]{:S(2)}, u32[]{:S(2)}) %collective-permute-start.40) | collective-permute-done | bytes 262176 | tf_op jit(solution)/shard_map/ppermute | solution.py:37
  270.3 8.0 %collective-permute-done.38.refs_1_ = f32[16,2176]{1,0:T(8,128)S(1)} collective-permute-done((f32[16,2176]{1,0:T(8,128)S(1)}, f32[16,2176]{1,0:T(8,128)S(1)}, u32[]{:S(2)}, u32[]{:S(2)}) %collective-permute-start.38) | collective-permute-done | bytes 139296 | tf_op jit(solution)/shard_map/ppermute | solution.py:37
  283.6 5.3 %collective-permute-done.41.refs_2_ = f32[16,2176]{1,0:T(8,128)S(1)} collective-permute-done((f32[16,2176]{1,0:T(8,128)S(1)}, f32[16,2176]{1,0:T(8,128)S(1)}, u32[]{:S(2)}, u32[]{:S(2)}) %collective-permute-start.41) | collective-permute-done | bytes 139296 | tf_op jit(solution)/shard_map/ppermute | solution.py:37
  289.6 15.2 %collective-permute-done.46.refs_2_ = f32[128,2048]{1,0:T(8,128)S(1)} collective-permute-done((f32[128,2048]{1,0:T(8,128)S(1)}, f32[128,2048]{1,0:T(8,128)S(1)}, u32[]{:S(2)}, u32[]{:S(2)}) %collective-permute-start.46) | collective-permute-done | bytes 1048608 | tf_op jit(solution)/shard_map/ppermute | solution.py:37
  315.5 8.8 %collective-permute-done.49.refs_2_ = f32[64,2176]{1,0:T(8,128)S(1)} collective-permute-done((f32[64,2176]{1,0:T(8,128)S(1)}, f32[64,2176]{1,0:T(8,128)S(1)}, u32[]{:S(2)}, u32[]{:S(2)}) %collective-permute-start.49) | collective-permute-done | bytes 557088 | tf_op jit(solution)/shard_map/ppermute | solution.py:37
  325.5 5.0 %collective-permute-start.51 = (f32[256,2176]{1,0:T(8,128)S(1)}, f32[256,2176]{1,0:T(8,128)S(1)}, u32[]{:S(2)}, u32[]{:S(2)}) collective-permute-start(f32[256,2176]{1,0:T(8,128)S(1)} %shard_map.253.refs_1_.refs_3_), channel_id=1, source_target_pairs={{0,1},{1,0},{2,3},{3,2},{4,5},{5,4},{6,7},{7,6},{8,9},{9,8},{10,11... | collective-permute-start | bytes 6684680 | tf_op jit(solution)/shard_map/ppermute | solution.py:37
  (312 shorter events, 147.1 us)
Async XLA Ops:
  47.9 19.8 %collective-permute-start.8 = (f32[4,72,256]{2,1,0:T(8,128)S(1)}, f32[4,72,256]{2,1,0:T(8,128)S(1)}, u32[]{:S(2)}, u32[]{:S(2)}) collective-permute-start(f32[4,72,256]{2,1,0:T(8,128)S(1)} %shard_map.205.refs_13_), channel_id=1, source_target_pairs={{16,24},{17,25},{18,26},{19,27},{20,28},{21,29},{22,30},{23,31}} | collective-permute-start | bytes 884744 | tf_op jit(solution)/shard_map/ppermute | solution.py:50
  92.3 32.3 %collective-permute-start.13 = (f32[256,2048]{1,0:T(8,128)S(1)}, f32[256,2048]{1,0:T(8,128)S(1)}, u32[]{:S(2)}, u32[]{:S(2)}) collective-permute-start(f32[256,2048]{1,0:T(8,128)S(1)} %shard_map.210.refs_5_), channel_id=1, source_target_pairs={{0,1},{1,0},{2,3},{3,2},{4,5},{5,4},{6,7},{7,6},{8,9},{9,8},{10,11... | collective-permute-start | bytes 6291464 | tf_op jit(solution)/shard_map/ppermute | solution.py:37
  103.3 35.2 %collective-permute-start.15 = (f32[1024,512]{1,0:T(8,128)S(1)}, f32[1024,512]{1,0:T(8,128)S(1)}, u32[]{:S(2)}, u32[]{:S(2)}) collective-permute-start(f32[1024,512]{1,0:T(8,128)S(1)} %shard_map.212.refs_2_.refs_5_), channel_id=1, source_target_pairs={{0,1},{1,0},{2,3},{3,2},{4,5},{5,4},{6,7},{7,6},{8,9},{9,8},{10,11... | collective-permute-start | bytes 6291464 | tf_op jit(solution)/shard_map/ppermute | solution.py:37
  118.8 17.9 %collective-permute-start.12 = (f32[4,72,256]{2,1,0:T(8,128)S(1)}, f32[4,72,256]{2,1,0:T(8,128)S(1)}, u32[]{:S(2)}, u32[]{:S(2)}) collective-permute-start(f32[4,72,256]{2,1,0:T(8,128)S(1)} %shard_map.213.refs_2_), channel_id=1, source_target_pairs={{16,8},{17,9},{18,10},{19,11},{20,12},{21,13},{22,14},{23,15}} | collective-permute-start | bytes 884744 | tf_op jit(solution)/shard_map/ppermute | solution.py:50
  120.9 16.7 %collective-permute-start.17 = (f32[4,72,256]{2,1,0:T(8,128)S(1)}, f32[4,72,256]{2,1,0:T(8,128)S(1)}, u32[]{:S(2)}, u32[]{:S(2)}) collective-permute-start(f32[4,72,256]{2,1,0:T(8,128)S(1)} %shard_map.218.refs_0_), channel_id=1, source_target_pairs={{24,16},{25,17},{26,18},{27,19},{28,20},{29,21},{30,22},{31,23}} | collective-permute-start | bytes 884744 | tf_op jit(solution)/shard_map/ppermute | solution.py:50
  126.4 26.2 %collective-permute-start.19 = (f32[128,2048]{1,0:T(8,128)}, f32[128,2048]{1,0:T(8,128)S(1)}, u32[]{:S(2)}, u32[]{:S(2)}) collective-permute-start(f32[128,2048]{1,0:T(8,128)} %get-tuple-element.136.refs_10_), channel_id=1, source_target_pairs={{0,2},{2,0},{1,3},{3,1},{4,6},{6,4},{5,7},{7,5},{8,10},{10,8},{9,1... | collective-permute-start | bytes 3145736 | tf_op jit(solution)/shard_map/ppermute | solution.py:37
  137.7 14.0 %collective-permute-start.20 = (f32[4,72,256]{2,1,0:T(8,128)S(1)}, f32[4,72,256]{2,1,0:T(8,128)S(1)}, u32[]{:S(2)}, u32[]{:S(2)}) collective-permute-start(f32[4,72,256]{2,1,0:T(8,128)S(1)} %shard_map.219.refs_3_), channel_id=1, source_target_pairs={{16,8},{17,9},{18,10},{19,11},{20,12},{21,13},{22,14},{23,15}} | collective-permute-start | bytes 884744 | tf_op jit(solution)/shard_map/ppermute | solution.py:50
  140.3 36.9 %collective-permute-start.23 = (f32[512,512]{1,0:T(8,128)}, f32[512,512]{1,0:T(8,128)}, u32[]{:S(2)}, u32[]{:S(2)}) collective-permute-start(f32[512,512]{1,0:T(8,128)} %get-tuple-element.142.refs_10_), channel_id=1, source_target_pairs={{0,4},{4,0},{1,5},{5,1},{2,6},{6,2},{3,7},{7,3},{8,12},{12,8},{9,1... | collective-permute-start | bytes 3145736 | tf_op jit(solution)/shard_map/ppermute | solution.py:37
  150.8 18.1 %collective-permute-start.18 = (f32[4,72,256]{2,1,0:T(8,128)S(1)}, f32[4,72,256]{2,1,0:T(8,128)S(1)}, u32[]{:S(2)}, u32[]{:S(2)}) collective-permute-start(f32[4,72,256]{2,1,0:T(8,128)S(1)} %get-tuple-element.145.refs_2_), channel_id=1, source_target_pairs={{0,4},{4,0},{1,5},{5,1},{2,6},{6,2},{3,7},{7,3},{8,12},{12,8},{9,1... | collective-permute-start | bytes 884744 | tf_op jit(solution)/shard_map/ppermute | solution.py:37
  151.7 23.7 %collective-permute-start.21 = (f32[4,72,256]{2,1,0:T(8,128)S(1)}, f32[4,72,256]{2,1,0:T(8,128)S(1)}, u32[]{:S(2)}, u32[]{:S(2)}) collective-permute-start(f32[4,72,256]{2,1,0:T(8,128)S(1)} %shard_map.223.refs_3_), channel_id=1, source_target_pairs={{8,0},{9,1},{10,2},{11,3},{12,4},{13,5},{14,6},{15,7}} | collective-permute-start | bytes 884744 | tf_op jit(solution)/shard_map/ppermute | solution.py:50
  190.4 19.6 %collective-permute-start.24 = (f32[256,2176]{1,0:T(8,128)S(1)}, f32[256,2176]{1,0:T(8,128)S(1)}, u32[]{:S(2)}, u32[]{:S(2)}) collective-permute-start(f32[256,2176]{1,0:T(8,128)S(1)} %shard_map.229.refs_17_), channel_id=1, source_target_pairs={{0,1},{1,0},{2,3},{3,2},{4,5},{5,4},{6,7},{7,6},{8,9},{9,8},{10,11... | collective-permute-start | bytes 6684680 | tf_op jit(solution)/shard_map/ppermute | solution.py:37
  195.0 13.7 %collective-permute-start.26 = (f32[64,2048]{1,0:T(8,128)}, f32[64,2048]{1,0:T(8,128)S(1)}, u32[]{:S(2)}, u32[]{:S(2)}) collective-permute-start(f32[64,2048]{1,0:T(8,128)} %get-tuple-element.149.refs_16_), channel_id=1, source_target_pairs={{0,4},{4,0},{1,5},{5,1},{2,6},{6,2},{3,7},{7,3},{8,12},{12,8},{9,1... | collective-permute-start | bytes 1572872 | tf_op jit(solution)/shard_map/ppermute | solution.py:37
  195.7 13.6 %collective-permute-start.25 = (f32[256,512]{1,0:T(8,128)S(1)}, f32[256,512]{1,0:T(8,128)S(1)}, u32[]{:S(2)}, u32[]{:S(2)}) collective-permute-start(f32[256,512]{1,0:T(8,128)S(1)} %get-tuple-element.157.refs_16_), channel_id=1, source_target_pairs={{0,2},{2,0},{1,3},{3,1},{4,6},{6,4},{5,7},{7,5},{8,10},{10,8},{9,1... | collective-permute-start | bytes 1572872 | tf_op jit(solution)/shard_map/ppermute | solution.py:37
  210.7 13.6 %collective-permute-start.27 = (f32[64,2176]{1,0:T(8,128)S(1)}, f32[64,2176]{1,0:T(8,128)S(1)}, u32[]{:S(2)}, u32[]{:S(2)}) collective-permute-start(f32[64,2176]{1,0:T(8,128)S(1)} %get-tuple-element.178.refs_3_), channel_id=1, source_target_pairs={{0,2},{2,0},{1,3},{3,1},{4,6},{6,4},{5,7},{7,5},{8,10},{10,8},{9,1... | collective-permute-start | bytes 1671176 | tf_op jit(solution)/shard_map/ppermute | solution.py:37
  225.0 20.5 %collective-permute-start.31 = (f32[32,2176]{1,0:T(8,128)S(1)}, f32[32,2176]{1,0:T(8,128)S(1)}, u32[]{:S(2)}, u32[]{:S(2)}) collective-permute-start(f32[32,2176]{1,0:T(8,128)S(1)} %get-tuple-element.186.refs_2_), channel_id=1, source_target_pairs={{0,4},{4,0},{1,5},{5,1},{2,6},{6,2},{3,7},{7,3},{8,12},{12,8},{9,1... | collective-permute-start | bytes 835592 | tf_op jit(solution)/shard_map/ppermute | solution.py:37
  225.9 19.6 %collective-permute-start.32 = (f32[32,2176]{1,0:T(8,128)S(1)}, f32[32,2176]{1,0:T(8,128)S(1)}, u32[]{:S(2)}, u32[]{:S(2)}) collective-permute-start(f32[32,2176]{1,0:T(8,128)S(1)} %get-tuple-element.188), channel_id=1, source_target_pairs={{0,2},{2,0},{1,3},{3,1},{4,6},{6,4},{5,7},{7,5},{8,10},{10,8},{9,1... | collective-permute-start | bytes 835592 | tf_op jit(solution)/shard_map/ppermute | solution.py:37
  227.1 18.3 %collective-permute-start.33 = (f32[64,512]{1,0:T(8,128)S(1)}, f32[64,512]{1,0:T(8,128)S(1)}, u32[]{:S(2)}, u32[]{:S(2)}) collective-permute-start(f32[64,512]{1,0:T(8,128)S(1)} %get-tuple-element.184.refs_5_), channel_id=1, source_target_pairs={{0,16},{16,0},{8,24},{24,8},{1,17},{17,1},{9,25},{25,9},{2,18},{18... | collective-permute-start | bytes 393224 | tf_op jit(solution)/shard_map/ppermute | solution.py:37
  250.2 13.6 %collective-permute-start.40 = (f32[32,2048]{1,0:T(8,128)S(1)}, f32[32,2048]{1,0:T(8,128)S(1)}, u32[]{:S(2)}, u32[]{:S(2)}) collective-permute-start(f32[32,2048]{1,0:T(8,128)S(1)} %shard_map.240.refs_3_.refs_1_), channel_id=1, source_target_pairs={{0,8},{8,0},{16,24},{24,16},{1,9},{9,1},{17,25},{25,17},{2,10},{10... | collective-permute-start | bytes 786440 | tf_op jit(solution)/shard_map/ppermute | solution.py:37
  252.0 17.4 %collective-permute-start.39 = (f32[128,512]{1,0:T(8,128)S(1)}, f32[128,512]{1,0:T(8,128)S(1)}, u32[]{:S(2)}, u32[]{:S(2)}) collective-permute-start(f32[128,512]{1,0:T(8,128)S(1)} %shard_map.241.refs_3_.refs_1_), channel_id=1, source_target_pairs={{0,8},{8,0},{16,24},{24,16},{1,9},{9,1},{17,25},{25,17},{2,10},{10... | collective-permute-start | bytes 786440 | tf_op jit(solution)/shard_map/ppermute | solution.py:37
  264.4 14.0 %collective-permute-start.43 = (f32[64,2048]{1,0:T(8,128)S(1)}, f32[64,2048]{1,0:T(8,128)S(1)}, u32[]{:S(2)}, u32[]{:S(2)}) collective-permute-start(f32[64,2048]{1,0:T(8,128)S(1)} %shard_map.243.refs_3_.refs_1_), channel_id=1, source_target_pairs={{0,4},{4,0},{1,5},{5,1},{2,6},{6,2},{3,7},{7,3},{8,12},{12,8},{9,1... | collective-permute-start | bytes 1572872 | tf_op jit(solution)/shard_map/ppermute | solution.py:37
  279.0 25.7 %collective-permute-start.46 = (f32[128,2048]{1,0:T(8,128)S(1)}, f32[128,2048]{1,0:T(8,128)S(1)}, u32[]{:S(2)}, u32[]{:S(2)}) collective-permute-start(f32[128,2048]{1,0:T(8,128)S(1)} %shard_map.246.refs_3_.refs_1_), channel_id=1, source_target_pairs={{0,2},{2,0},{1,3},{3,1},{4,6},{6,4},{5,7},{7,5},{8,10},{10,8},{9,1... | collective-permute-start | bytes 3145736 | tf_op jit(solution)/shard_map/ppermute | solution.py:37
  282.9 22.5 %collective-permute-start.45 = (f32[512,512]{1,0:T(8,128)S(1)}, f32[512,512]{1,0:T(8,128)S(1)}, u32[]{:S(2)}, u32[]{:S(2)}) collective-permute-start(f32[512,512]{1,0:T(8,128)S(1)} %shard_map.247.refs_3_.refs_1_), channel_id=1, source_target_pairs={{0,4},{4,0},{1,5},{5,1},{2,6},{6,2},{3,7},{7,3},{8,12},{12,8},{9,1... | collective-permute-start | bytes 3145736 | tf_op jit(solution)/shard_map/ppermute | solution.py:37
  289.5 16.6 %collective-permute-start.44 = (f32[32,2176]{1,0:T(8,128)S(1)}, f32[32,2176]{1,0:T(8,128)S(1)}, u32[]{:S(2)}, u32[]{:S(2)}) collective-permute-start(f32[32,2176]{1,0:T(8,128)S(1)} %shard_map.248.refs_3_.refs_1_), channel_id=1, source_target_pairs={{0,8},{8,0},{16,24},{24,16},{1,9},{9,1},{17,25},{25,17},{2,10},{10... | collective-permute-start | bytes 835592 | tf_op jit(solution)/shard_map/ppermute | solution.py:37
  325.5 17.8 %collective-permute-start.51 = (f32[256,2176]{1,0:T(8,128)S(1)}, f32[256,2176]{1,0:T(8,128)S(1)}, u32[]{:S(2)}, u32[]{:S(2)}) collective-permute-start(f32[256,2176]{1,0:T(8,128)S(1)} %shard_map.253.refs_1_.refs_3_), channel_id=1, source_target_pairs={{0,1},{1,0},{2,3},{3,2},{4,5},{5,4},{6,7},{7,6},{8,9},{9,8},{10,11... | collective-permute-start | bytes 6684680 | tf_op jit(solution)/shard_map/ppermute | solution.py:37
  (109 other events, 972.6 us)

commit v4 on v3

--- a/solution.py
+++ b/solution.py
@@ -59,44 +59,7 @@
         yield send
         yield mine, other
 
-    ways = {"x": 1, "y": 2, "z1": 3, "z2": 4}
-
-    def sums(self, give, keep, bits, shapes, order):
-        if order is None:
-            return self.halves_sum(give, keep, bits, shapes)
-        return self.chain_sum(give, keep, bits, shapes, order)
-
-    def chain_sum(self, give, keep, bits, shapes, order):
-        after = yield
-        got = self.swap(give, "c")
-        after = yield give
-        rows, wide = give.shape
-        part = keep()
-        for axis in order:
-            half = part.shape[0] // 2
-            spec = (full((half, wide)), (half, wide), F32)
-            give, part = call(
-                functools.partial(fold_kernel, (self.ways[axis],), 2), 1,
-                [SMEM] + [full(part.shape)] * 2, [spec] * 2, nbytes=16 * part.size,
-            )(bits, part, got, after=after)
-            got = self.swap(give, axis)
-            after = yield give
-        part = simple(add_kernel, after, part, got)
-        got = self.swap(part, order[-1])
-        after = yield part
-        for n in range(len(order) - 1, 0, -1):
-            (part,) = self.join((self.ways[order[n]],), bits, (part, got), after)
-            got = self.swap(part, order[n - 1])
-            after = yield part
-        (part,) = self.join((self.ways[order[0]],), bits, (part, got), after)
-        got = self.swap(part, "c")
-        after = yield part
-        yield call(
-            last_join_kernel, 1, [SMEM] + [full((rows, wide))] * 2,
-            [(full(s), s, F32) for s in shapes], nbytes=16 * rows * wide,
-        )(bits, part, got, after=after)
-
-    def halves_sum(self, give, keep, bits, shapes):
+    def sums(self, give, keep, bits, shapes):
         after = yield
         got = self.swap(give, "c")
         after = yield give
@@ -192,7 +155,7 @@
             out, by = out + shift(out, by), by * 2
         yield out[0], out[1]
 
-    def sums(self, give, keep, bits, shapes, order):
+    def sums(self, give, keep, bits, shapes):
         for _ in range(11):
             yield give
         part = lax.psum(jnp.concatenate([keep(), give], axis=0), self.axes)
@@ -259,9 +222,16 @@
     return jnp.where(row == 0, first, jnp.where(row == 1, second, 0.0))
 
 
-def map_kernel(
-    s, meta, bits, x, gain, bias, wq, wk, wv, fx, h1, qs, ks, vv, pq, pk, keep, give
-):
+def phi(u, f):
+    fw = blocks_of(f)
+    sq = jnp.square(u.astype(F32))
+    hi = sq.astype(BF)
+    lo = (sq - hi.astype(F32)).astype(BF)
+    lhs = jnp.concatenate([u, hi, lo], axis=1)
+    return jnp.exp(mm_t(lhs, jnp.concatenate([fw, fw[:, LANES:]], axis=1))) * SCALE
+
+
+def map_kernel(s, meta, bits, x, gain, bias, wk, wv, fx, h1, ks, vv, pk, keep, give):
     p = pl.program_id(0)
     rows = x.shape[1]
 
@@ -269,33 +239,25 @@
     def _():
         h1[...] = norm(x[0].astype(F32), gain[...], bias[...])[0].astype(BF)
 
-    w = jnp.concatenate([wq[...], wk[...], wv[...]], axis=1)
-    qkv = mm(h1[...], w)
-    q = (SHRINK * qkv[:, :LANES]).astype(BF)
-    k = (SHRINK * qkv[:, LANES : 2 * LANES]).astype(BF)
-    v = qkv[:, 2 * LANES :].astype(BF)
-    qs[...], ks[...], vv[...] = q, k, v
-
-    fw = blocks_of(fx[0])
-    fw = jnp.concatenate([fw, fw[:, LANES:]], axis=1)
-
-    def phi(u):
-        sq = jnp.square(u.astype(F32))
-        hi = sq.astype(BF)
-        lo = (sq - hi.astype(F32)).astype(BF)
-        return jnp.exp(mm_t(jnp.concatenate([u, hi, lo], axis=1), fw)) * SCALE
-
-    pq[...] = phi(q).astype(BF)
-    phk = (phi(k) * live_of(meta, s, rows)).astype(BF)
+    kv = mm(h1[...], jnp.concatenate([wk[...], wv[...]], axis=1))
+    k = (SHRINK * kv[:, :LANES]).astype(BF)
+    v = kv[:, LANES:].astype(BF)
+    ks[...], vv[...] = k, v
+    phk = (phi(k, fx[0]) * live_of(meta, s, rows)).astype(BF)
     pk[...] = phk
-    lhs = jnp.concatenate([v.T, jnp.ones((16, rows), BF)], axis=0)
-    ds = mm(lhs, phk)
+    ds = mm(jnp.concatenate([v.T, jnp.ones((16, rows), BF)], axis=0), phk)
     for near, xs in ((True, keep), (False, give)):
 
         @pl.when((p // 2 == bits[2]) == near)
-        def _():
+        def _(xs=xs):
             put_state(xs, 2 * (p % 2), ds[:64, :256], ds[128:129, :256])
             put_state(xs, 2 * (p % 2) + 1, ds[64:128, 256:], ds[128:129, 256:])
+
+
+def query_kernel(h1, wq, fx, qs, pq):
+    q = (SHRINK * mm(h1[...], wq[...])).astype(BF)
+    qs[...] = q
+    pq[...] = phi(q, fx[0]).astype(BF)
 
 
 def put_state(xs, at, state, total):
@@ -405,6 +367,12 @@
 
 
 def middle_kernel(
+    s, meta, bits, x, dy, pq, nd, mine, other, gain, bias, wo, wup, wdown, *refs
+):
+    middle_body(s, meta, bits, x, dy, pq, nd, mine, other, gain, bias, wo, wup, wdown, *refs[-18:])
+
+
+def middle_body(
     s, meta, bits, x, dy, pq, nd, mine, other, gain, bias, wo, wup, wdown,
     out, dx1, dx, a_low, db, h2, df, gl, du, gs_keep, gs_give, ng,
     x1, xhat, inv, f, dh2, den,
@@ -462,7 +430,7 @@
 
     @pl.when(c == pl.num_programs(0) - 1)
     def _():
-        out[...] = x1[...].astype(BF)
+        out[0] = x1[...].astype(BF)
         e = dh2[...]
         xh = xhat[...]
         ng[...] = two_rows(
@@ -502,8 +470,9 @@
                         put_state(gs, 2 * (p % 2) + h, g[64 * h : 64 * h + 64, side], z)
 
 
-def inner_kernel(bits, qs, ks, vv, pq, pk, dx, mine, other, fx, dq, dkl, dvl):
-    p = pl.program_id(0)
+def inner_kernel(part, bits, qs, ks, vv, pq, pk, dx, mine, other, fx, *outs):
+    p = pl.program_id(0) + 2 * part
+    dq, dkl, dvl = outs[-3:]
     rows = pq.shape[0]
     half = rows // 2
     col = lanes_of(512)
@@ -560,8 +529,9 @@
 
 def last_kernel(
     s, bits, x, dx1, gain, ks, vv, pk, mine, other, fx, dq, dkl, dvl, wq, wk, wv,
-    grad, dk, dv, ng, dh1,
+    *refs,
 ):
+    grad, dk, dv, ng, dh1 = refs[-5:]
     p = pl.program_id(0)
     rows = pk.shape[0]
     col = lanes_of(512)
@@ -608,11 +578,20 @@
         ng[...] = two_rows(
             jnp.sum(e * xh, axis=0, keepdims=True), jnp.sum(e, axis=0, keepdims=True)
         )
-        grad[...] = dx1[...] + norm_grad(e, xh, inv, gain[...])
-
-
-def weight_kernel(c, a0, a1, b0, b1, out):
-    out[...] = mm(a0[...].T, b0[...]) + mm(a1[...].T, b1[...])
+        grad[0] = dx1[...] + norm_grad(e, xh, inv, gain[...])
+
+
+def block_kernel(g0, g1, f0, f1, h0, h1, u0, u1, down, up):
+    p = pl.program_id(0)
+    n = pl.num_programs(0) // 2
+
+    @pl.when(p < n)
+    def _():
+        down[...] = mm(g0[...].T, f0[...]) + mm(g1[...].T, f1[...])
+
+    @pl.when(p >= n)
+    def _():
+        up[...] = mm(h0[...].T, u0[...]) + mm(h1[...].T, u1[...])
 
 
 def late_kernel(c, a0, a1, b0, b1, b2, b3, b4, b5, n0, n1, n2, n3, o0, o1, d0, d1, out):
@@ -625,7 +604,7 @@
     out[:, 2048:] = jnp.concatenate(sums + [jnp.zeros((112, out.shape[0]), F32)], axis=0).T
 
 
-def params(limit=36):
+def params(limit):
     return pltpu.CompilerParams(vmem_limit_bytes=limit * 2**20)
 
 
@@ -653,7 +632,10 @@
 ANY = pl.BlockSpec(memory_space=pl.ANY)
 
 
-def call(kernel, grid, ins, outs, scratch=(), flops=0, nbytes=0, scalars=0):
+def call(
+    kernel, grid, ins, outs, scratch=(), flops=0, nbytes=0, scalars=0, aliases={},
+    grant=16,
+):
     def run(*args, after=()):
         count, waits = len(ins) + scalars, len(after)
 
@@ -670,7 +652,8 @@
                 scratch_shapes=list(scratch),
             ),
             out_shape=[arr(*o[1:]) for o in outs],
-            compiler_params=params(),
+            compiler_params=params(grant),
+            input_output_aliases=aliases,
             cost_estimate=pl.CostEstimate(flops=flops, bytes_accessed=nbytes, transcendentals=0),
         )(*args, *after)
 
@@ -693,30 +676,21 @@
     return pl.BlockSpec(shape, lambda p, c: (0,) * len(shape))
 
 
-def up_weights(give, bits, h2, du, after=()):
-    rows, n = du[0].shape
-    m = h2[0].shape[1] // 2
-    at = half_of(give)
-    sa = pl.BlockSpec((rows, m), lambda p, c: (0, at(c)))
-    sb = pl.BlockSpec((rows, 512), lambda p, c: (0, p))
+def block_weights(gl, df, h2, du, after=()):
+    rows, width = df[0].shape
+    wide = gl[0].shape[1]
+    n = wide // 512
+    one = full((rows, width))
+    first = lambda p: jnp.minimum(p, n - 1)
+    second = lambda p: jnp.maximum(p - n, 0)
+    sg = pl.BlockSpec((rows, 512), lambda p: (0, first(p)))
+    su = pl.BlockSpec((rows, 512), lambda p: (0, second(p)))
     return call(
-        weight_kernel, n // 512, [sa, sa, sb, sb],
-        [(pl.BlockSpec((m, 512), lambda p, c: (0, p)), (m, n), F32)],
-        flops=4 * rows * m * n, nbytes=4 * m * n + 4 * rows * n, scalars=1,
-    )(bits, *h2, *du, after=after)[0]
-
-
-def down_weights(give, bits, gl, df, after=()):
-    rows, n = df[0].shape
-    m = gl[0].shape[1] // 2
-    at, grid = half_of(give), m // 512
-    sa = pl.BlockSpec((rows, 512), lambda p, c: (0, grid * at(c) + p))
-    sb = whole((rows, n))
-    return call(
-        weight_kernel, grid, [sa, sa, sb, sb],
-        [(pl.BlockSpec((512, n), lambda p, c: (p, 0)), (m, n), F32)],
-        flops=4 * rows * m * n, nbytes=4 * m * n + 4 * rows * m, scalars=1,
-    )(bits, *gl, *df, after=after)[0]
+        block_kernel, 2 * n, [sg, sg, one, one, one, one, su, su],
+        [(pl.BlockSpec((512, width), lambda p: (first(p), 0)), (wide, width), F32),
+         (pl.BlockSpec((width, 512), lambda p: (0, second(p))), (width, wide), F32)],
+        flops=8 * rows * width * wide, nbytes=8 * width * wide + 8 * rows * wide,
+    )(*gl, *df, *h2, *du, after=after)
 
 
 def late_weights(give, bits, h1, dq, dk, dv, ng1, ng2, a, db, after=()):
@@ -733,11 +707,13 @@
     )(bits, *h1, *dq, *dk, *dv, *ng1, *ng2, *a, *db, after=after)[0]
 
 
-ORDER = (
-    "M0", "f", "M1", "f", "g", "A0", "f", "g", "A1", "f", "g", "f", "g", "N0", "g", "p", "N1",
-    "p", "q", "Gu", "u", "Ku", "Gd", "p", "q", "d", "Kd", "u", "I0", "p", "q", "d", "I1",
-    "p", "q", "u", "L0", "q", "d", "L1", "Gk", "k", "Kk", "u", "d", "k", "u", "d", "k",
-    "u", "d", "k", "u", "d", "k", "u", "d", "k", "u", "d", "k", "u", "d", "k", "k", "k",
+FRONT = (
+    "M0", "f", "M1", "f", "g", "Q0", "f", "g", "Q1", "f", "g", "A0", "f", "g", "A1", "N0", "g",
+    "p", "N1", "p", "q",
+)
+BACK = (
+    "p", "q", "I0a", "p", "q", "I0b", "I1a", "p", "q", "I1b", "L0", "q", "L1", "Gk", "k", "Kk",
+    "k", "k", "k", "k", "k", "k", "k", "k", "k", "Fk",
 )
 
 
@@ -773,15 +749,22 @@
         return call(
             functools.partial(map_kernel, s), 4,
             [SMEM, SMEM, of_seq(s, (rows, width)), vec, vec]
-            + [cols(width, LANES, 4 * n) for n in range(3)] + [PAIR],
+            + [cols(width, LANES, 4 * n) for n in (1, 2)] + [PAIR],
             [(full((rows, width)), (rows, width), BF)]
-            + [(act, (rows, width), BF)] * 3
-            + [(big, (rows, 2048), BF)] * 2 + states,
-            flops=rows * 4_800_000, nbytes=12 * 2**20,
-        )(meta, bits, inputs, g1, n1, qkv_weight, qkv_weight, qkv_weight, fx, after=after)
+            + [(act, (rows, width), BF)] * 2
+            + [(big, (rows, 2048), BF)] + states,
+            flops=rows * 3_000_000, nbytes=8 * 2**20,
+        )(meta, bits, inputs, g1, n1, qkv_weight, qkv_weight, fx, after=after)
+
+    def queries_of(h1, after):
+        return call(
+            query_kernel, 4, [full((rows, width)), cols(width, LANES), PAIR],
+            [(act, (rows, width), BF), (big, (rows, 2048), BF)],
+            flops=rows * 1_800_000, nbytes=4 * 2**20,
+        )(h1, qkv_weight, fx, after=after)
 
     def locals_of(s, after):
-        _, _, _, vv, pq, pk, _, _ = maps[s]
+        _, _, _, vv, pq, pk = maps[s]
         return call(
             local_kernel, 4, [big, big, act],
             [(cols(rows, 256), (rows, 1024), F32)],
@@ -794,8 +777,8 @@
                 functools.partial(middle_kernel, s), wide // 512,
                 [SMEM, SMEM, of_seq(s, (rows, width)), of_seq(s, (rows, width)), full((rows, 2048)),
                  full((rows, 1024)), full(heads), full(heads), vec, vec, full((width, width)),
-                 cols(width, 512), pl.BlockSpec((512, width), lambda p: (p, 0))],
-                [(full((rows, width)), (rows, width), BF),
+                 cols(width, 512), pl.BlockSpec((512, width), lambda p: (p, 0))] + [ANY] * s,
+                [(of_seq(s, (rows, width)), inputs.shape, BF),
                  (full((rows, width)), (rows, width), F32),
                  (full((rows, 1024)), (rows, 1024), BF),
                  (full((rows, width)), (rows, width), BF),
@@ -809,65 +792,66 @@
                 scratch=[pltpu.VMEM((rows, width), F32), pltpu.VMEM((rows, width), F32),
                          pltpu.VMEM((rows, LANES), F32)]
                 + [pltpu.VMEM((rows, width), F32)] * 3,
-                flops=rows * 11_000_000, nbytes=24 * 2**20,
+                flops=rows * 11_000_000, nbytes=24 * 2**20, grant=24, aliases={13: 0} if s else {},
             )(meta, bits, inputs, cotangent, pq, locals_[s], *prefix, g2, n2, out_weight,
-              up_weight, down_weight, after=after)
-
-    def inner(s, after):
-        _, qs, ks, vv, pq, pk, _, _ = maps[s]
+              up_weight, down_weight, *([mids[0][0]] if s else []), after=after)
+
+    def inner(s, part, after):
+        _, qs, ks, vv, pq, pk = maps[s]
+        here = lambda wide: pl.BlockSpec((rows, wide), lambda p: (0, p + 2 * part))
+        side = pl.BlockSpec((2, 72, 256), lambda p: (p % 2, 0, 0))
+        fxs = pl.BlockSpec((1, 512, 64), lambda p: (p + 2 * part, 0, 0))
+        act, big = here(LANES), here(512)
+        earlier = tuple(inners[s]) if part else ()
         return call(
-            inner_kernel, 4,
-            [SMEM, act, act, act, big, big, cols(rows, 256), HEADS, HEADS, PAIR],
+            functools.partial(inner_kernel, part), 2,
+            [SMEM, act, act, act, big, big, here(256), side, side, fxs] + [ANY] * len(earlier),
             [(act, (rows, width), BF), (act, (rows, width), F32), (act, (rows, width), F32)],
-            flops=rows * 20_000_000, nbytes=11 * 2**20,
-        )(bits, qs, ks, vv, pq, pk, mids[s][2], *state[s], fx, after=after)
+            flops=rows * 10_000_000, nbytes=6 * 2**20,
+            aliases={10 + n: n for n in range(len(earlier))},
+        )(bits, qs, ks, vv, pq, pk, mids[s][2], *state[s], fx, *earlier, after=after)
 
     def last(s, later, after):
-        _, qs, ks, vv, pq, pk, _, _ = maps[s]
+        _, qs, ks, vv, pq, pk = maps[s]
         return call(
             functools.partial(last_kernel, s), 4,
             [SMEM, of_seq(s, (rows, width)), full((rows, width)), vec, act, act, big, HEADS, HEADS,
              PAIR,
-             act, act, act] + [cols(width, LANES, 4 * n) for n in range(3)],
-            [(full((rows, width)), (rows, width), F32), (act, (rows, width), BF),
+             act, act, act] + [cols(width, LANES, 4 * n) for n in range(3)] + [ANY] * s,
+            [(of_seq(s, (rows, width)), inputs.shape, F32), (act, (rows, width), BF),
              (act, (rows, width), BF), (full((8, width)), (8, width), F32)],
             scratch=[pltpu.VMEM((rows, width), F32)],
-            flops=rows * 6_000_000, nbytes=11 * 2**20,
+            flops=rows * 6_000_000, nbytes=11 * 2**20, aliases={16: 0} if s else {},
         )(bits, inputs, mids[s][1], g1, ks, vv, pk, *later, fx, *inners[s],
-          qkv_weight, qkv_weight, qkv_weight, after=after)
+          qkv_weight, qkv_weight, qkv_weight, *([lasts[0][0]] if s else []), after=after)
 
     maps, locals_, mids, state, inners, lasts, kept, flows = {}, {}, {}, {}, {}, {}, {}, {}
+    ends = {}
 
     def of_mids(*index):
         return [[mids[s][n] for s in range(seqs)] for n in index]
 
     def weights(name, give, after):
-        if name == "u":
-            return up_weights(give, bits, *of_mids(5, 8), after=after)
-        if name == "d":
-            return down_weights(give, bits, *of_mids(7, 6), after=after)
         h1 = [maps[s][0] for s in range(seqs)]
         dq = [inners[s][0] for s in range(seqs)]
         dk, dv, ng1 = ([lasts[s][n] for s in range(seqs)] for n in (1, 2, 3))
         return late_weights(give, bits, h1, dq, dk, dv, ng1, *of_mids(11, 3, 4), after=after)
 
-    shapes = {
-        "u": ((width, wide),),
-        "d": ((wide, width),),
-        "k": ((width, 3 * width), (width, width), (width, LANES)),
-    }
-    orders = {"u": ("x", "y", "z1", "z2"), "d": ("y", "x", "z1", "z2"), "k": None}
+    shapes = ((width, 3 * width), (width, width), (width, LANES))
 
     def play(items, token):
         for item in items:
             after = () if token is None else (token,)
             kind, name = item[0], item[-1]
-            s = int(name) if name in "01" else None
+            s = int(item[1]) if item[1:2] in ("0", "1") else None
             if kind == "M":
-                maps[s] = maps_of(s, after)
-                token = maps[s][7]
-                flows["fg"[s]] = comm.carry(maps[s][6], token, bits, False)
+                h1, ks, vv, pk, keep, token = maps_of(s, after)
+                maps[s] = [h1, None, ks, vv, None, pk]
+                flows["fg"[s]] = comm.carry(keep, token, bits, False)
                 next(flows["fg"[s]])
+            elif kind == "Q":
+                maps[s][1], maps[s][4] = queries_of(maps[s][0], after)
+                token = maps[s][1]
             elif kind == "A":
                 token = locals_[s] = locals_of(s, after)
             elif kind == "N":
@@ -877,7 +861,7 @@
                 flows["pq"[s]] = comm.carry(mids[s][9], token, bits, True)
                 next(flows["pq"[s]])
             elif kind == "I":
-                inners[s] = inner(s, after)
+                inners[s] = inner(s, int(name == "b"), after)
                 token = inners[s][1]
             elif kind == "L":
                 lasts[s] = last(s, next(flows["pq"[s]]), after)
@@ -885,23 +869,35 @@
             elif kind == "G":
                 token = weights(name, True, after)
                 flows[name] = comm.sums(
-                    token, functools.partial(kept.get, name), bits, shapes[name], orders[name]
+                    token, functools.partial(kept.get, name), bits, shapes
                 )
                 next(flows[name])
             elif kind == "K":
                 token = kept[name] = weights(name, False, after)
+            elif kind == "F":
+                ends[name] = flows[name].send(after)
+                token = ends[name][0]
             else:
                 token = flows[name].send(after)
         return token
 
-    end = (play(ORDER, None),)
-    (up_grad,), (down_grad,) = flows["u"].send(end), flows["d"].send(end)
-    qkv_grad, outw_grad, small = flows["k"].send(end)
-    small = small[:, :16].T
-    grad = jnp.stack([lasts[s][0] for s in range(seqs)])
-    out = [mids[s][0] for s in range(seqs)]
+    token = play(FRONT, None)
+    parts = block_weights(*of_mids(7, 6, 5, 8), after=(token,))
+    down_grad, up_grad = comm.whole_sum(tuple(parts))
+
+    def rest():
+        play(BACK, parts[1])
+        qkv_grad, outw_grad, small = ends["k"]
+        return qkv_grad, outw_grad, small[:, :16].T, lasts[seqs - 1][0]
+
+    def nothing():
+        shaped = [(width, 3 * width), (width, width), (16, width)]
+        return *(jnp.zeros(s, F32) for s in shaped), cotangent.astype(F32)
+
+    qkv_grad, outw_grad, small, grad = lax.cond(jnp.max(lengths) > 0, rest, nothing)
+    out = mids[seqs - 1][0]
     return (
-        jnp.stack(out),
+        out,
         grad,
         small[0],
         small[1],

time: 353 us -> 337 us (0.955)
  the two profiles are of different devices: /device:TPU:25 before, /device:TPU:0 now
where the time goes in v4:
time: 337 us; the launch traced here: 339 us
  waiting for transfers between devices  133 us (39%)
  Pallas kernels  127 us (38%)
  starting transfers between devices  44.7 us (13%)
  between operations  15.3 us (5%)
  local copies, waits for them, and re-layouts  13.4 us (4%)
  other arithmetic  3.98 us (1%)
    pallas_call x43, Pallas kernels, run(): pl.pallas_call(waiting, grid_spec=pltpu.PrefetchScalarGridSpec(num_scalar...  127 us
    ppermute x22, waiting for transfers between devices, swap(): return lax.ppermute(part, name, pairs)  121 us
    ppermute x22, starting transfers between devices, swap(): return lax.ppermute(part, name, pairs)  29 us
    ppermute x12, starting transfers between devices, carry(): arrived.append(lax.ppermute(out, 'z', [hop]))  15.7 us
    ppermute x12, waiting for transfers between devices, carry(): arrived.append(lax.ppermute(out, 'z', [hop]))  12.7 us
    unnamed x65, local copies, waits for them, and re-layouts  12.3 us
  transfers between devices with their start and end apart: 35, of which 24 were waited for; matrix products, arithmetic and copies ran while one was open for 1% of the time, Pallas kernels for 25%

profile of v4, /device:TPU:0, one launch (start us, length us, event | category | flops | bytes accessed | tf_op | source)
XLA Modules:
  0.0 338.5 jit_solution(4158318295307526786)
XLA Ops:
  10.0 6.9 %shard_map.198 = (bf16[512,512]{1,0:T(8,128)(2,1)S(1)}, bf16[512,512]{1,0:T(8,128)(2,1)}, bf16[512,512]{1,0:T(8,128)(2,1)S(1)}, bf16[512,2048]{1,0:T(8,128)(2,1)...) custom-call(s32[3]{0:T(128)S(1)} %pad_add_fusion.refs_0_, s32[5]{0:T(128)S(1)} %stack.23.refs_1_.refs_0_, ...), custom_call_target="tpu_custom_call" | custom-call | flops 1536000000 | bytes 8388608 | tf_op jit(solution)/shard_map/pallas_call | solution.py:645
  19.9 6.2 %shard_map.199 = (bf16[512,512]{1,0:T(8,128)(2,1)S(1)}, bf16[512,512]{1,0:T(8,128)(2,1)}, bf16[512,512]{1,0:T(8,128)(2,1)S(1)}, bf16[512,2048]{1,0:T(8,128)(2,1)...) custom-call(s32[3]{0:T(128)S(1)} %pad_add_fusion.refs_0_, s32[5]{0:T(128)S(1)} %stack.23.refs_1_.refs_0_, ...), custom_call_target="tpu_custom_call" | custom-call | flops 1536000000 | bytes 8388608 | tf_op jit(solution)/shard_map/pallas_call | solution.py:645
  58.3 14.4 %shard_map.211 = (bf16[2,512,512]{2,1,0:T(8,128)(2,1)}, f32[512,512]{1,0:T(8,128)}, bf16[512,1024]{1,0:T(8,128)(2,1)}, bf16[512,512]{1,0:T(8,128)(2,1)}, bf16[51...) custom-call(s32[3]{0:T(128)S(1)} %pad_add_fusion.refs_0_, ...), custom_call_target="tpu_custom_call" | custom-call | flops 5632000000 | bytes 25165824 | tf_op jit(solution)/shard_map/pallas_call | solution.py:645
  74.9 5.2 %collective-permute-done.30.refs_7_ = f32[4,72,256]{2,1,0:T(8,128)S(1)} collective-permute-done((f32[4,72,256]{2,1,0:T(8,128)S(1)}, f32[4,72,256]{2,1,0:T(8,128)S(1)}, u32[]{:S(2)}, u32[]{:S(2)}) %collective-permute-start.30) | collective-permute-done | bytes 294944 | tf_op jit(solution)/shard_map/ppermute | solution.py:37
  80.1 14.5 %shard_map.213 = (bf16[2,512,512]{2,1,0:T(8,128)(2,1)}, f32[512,512]{1,0:T(8,128)}, bf16[512,1024]{1,0:T(8,128)(2,1)}, bf16[512,512]{1,0:T(8,128)(2,1)}, bf16[51...) custom-call(s32[3]{0:T(128)S(1)} %pad_add_fusion.refs_0_, ...), custom_call_target="tpu_custom_call", output_to_operand_aliasing={{0}: (13, {})} | custom-call | flops 5632000000 | bytes 25165824 | tf_op jit(solution)/shard_map/pallas_call | solution.py:645
  94.6 22.1 %shard_map.215 = (f32[2048,512]{1,0:T(8,128)S(1)}, f32[512,2048]{1,0:T(8,128)}) custom-call(bf16[512,2048]{1,0:T(8,128)(2,1)S(1)} %get-tuple-element.250.refs_0_, bf16[512,2048]{1,0:T(8,128)(2,1)S(1)} %get-tuple-element.251.refs_1_, bf16[512,512]{1,0:T(8,128)(2,1)S(1)} %get-tuple-element.252.refs_2_, bf16[512,512]{1,0:T(8,128)(2,1)S(1)} %get-tuple-element.253.refs_3_, ...), custom_call_target="tpu_custom_call" | custom-call | flops 4294967296 | bytes 16777216 | tf_op jit(solution)/shard_map/pallas_call | solution.py:645
  120.3 6.5 %collective-permute-done.31.refs_1_ = f32[4,72,256]{2,1,0:T(8,128)S(1)} collective-permute-done((f32[4,72,256]{2,1,0:T(8,128)S(1)}, f32[4,72,256]{2,1,0:T(8,128)S(1)}, u32[]{:S(2)}, u32[]{:S(2)}) %collective-permute-start.31) | collective-permute-done | bytes 294944 | tf_op jit(solution)/shard_map/ppermute | solution.py:37
  132.1 9.8 %collective-permute-done.33 = f32[4,72,256]{2,1,0:T(8,128)} collective-permute-done((f32[4,72,256]{2,1,0:T(8,128)S(1)}, f32[4,72,256]{2,1,0:T(8,128)}, u32[]{:S(2)}, u32[]{:S(2)}) %collective-permute-start.33) | collective-permute-done | bytes 294944 | tf_op jit(solution)/shard_map/ppermute | solution.py:37
  141.9 182.7 %conditional.1 = (f32[512,1536]{1,0:T(8,128)}, f32[512,512]{1,0:T(8,128)}, f32[16,512]{0,1:T(8,128)}, f32[2,512,512]{2,1,0:T(8,128)}, bf16[1,512]{0,1:T(8,128)(2...) conditional(s32[]{:T(128)} %convert_element_type.6, ...), branch_computations={%region_1.2_spmd, %region_2.3_spmd} | conditional | flops 28772802560 | bytes 228324928 | solution.py:897
  145.2 5.1 %branch_1_fun.27 = (bf16[512,512]{1,0:T(8,128)(2,1)S(1)}, f32[512,512]{1,0:T(8,128)S(1)}, f32[512,512]{1,0:T(8,128)S(1)}) custom-call(s32[5]{0:T(128)S(1)} %get-tuple-element.85.refs_0_, bf16[512,512]{1,0:T(8,128)(2,1)S(1)} %copy-done.37, bf16[512,512]{1,0:T(8,128)(2,1)S(1)} %copy-done.30, bf16[512,512]{1,0:T(8,128)(2,1)S(1)} %copy-done.32, ...), custom_call_target="tpu_custom_call" | custom-call | flops 5120000000 | bytes 6291456 | tf_op jit(solution)/shard_map/cond/branch_1_fun/pallas_call | solution.py:645
  152.6 4.7 %branch_1_fun.30 = (bf16[512,512]{1,0:T(8,128)(2,1)S(1)}, f32[512,512]{1,0:T(8,128)S(1)}, f32[512,512]{1,0:T(8,128)S(1)}) custom-call(s32[5]{0:T(128)S(1)} %get-tuple-element.85.refs_0_, bf16[512,512]{1,0:T(8,128)(2,1)S(1)} %copy-done.37, bf16[512,512]{1,0:T(8,128)(2,1)S(1)} %copy-done.30, ...), custom_call_target="tpu_custom_call", output_to_operand_aliasing={{0}: (10, {}), {1}: (11, {}), {2}: (12, {})} | custom-call | flops 5120000000 | bytes 6291456 | tf_op jit(solution)/shard_map/cond/branch_1_fun/pallas_call | solution.py:645
  162.1 11.5 %collective-permute-done.3.refs_5_ = f32[4,72,256]{2,1,0:T(8,128)S(1)} collective-permute-done((f32[4,72,256]{2,1,0:T(8,128)S(1)}, f32[4,72,256]{2,1,0:T(8,128)S(1)}, u32[]{:S(2)}, u32[]{:S(2)}) %collective-permute-start.3) | collective-permute-done | bytes 294944 | tf_op jit(solution)/shard_map/cond/branch_1_fun/ppermute | solution.py:50
  181.4 7.2 %branch_1_fun.35 = (f32[2,512,512]{2,1,0:T(8,128)}, bf16[512,512]{1,0:T(8,128)(2,1)S(1)}, bf16[512,512]{1,0:T(8,128)(2,1)S(1)}, f32[8,512]{1,0:T(8,128)S(1)}) custom-call(s32[5]{0:T(128)S(1)} %get-tuple-element.85.refs_0_, bf16[2,512,512]{2,1,0:T(8,128)(2,1)S(1)} %copy-done.10, f32[512,512]{1,0:T(8,128)S(1)} %copy-done.28, ...), custom_call_target="tpu_custom_call" | custom-call | flops 3072000000 | bytes 11534336 | tf_op jit(solution)/shard_map/cond/branch_1_fun/pallas_call | solution.py:645
  190.9 7.3 %collective-permute-done.6.refs_8_ = f32[4,72,256]{2,1,0:T(8,128)S(1)} collective-permute-done((f32[4,72,256]{2,1,0:T(8,128)S(1)}, f32[4,72,256]{2,1,0:T(8,128)S(1)}, u32[]{:S(2)}, u32[]{:S(2)}) %collective-permute-start.6) | collective-permute-done | bytes 294944 | tf_op jit(solution)/shard_map/cond/branch_1_fun/ppermute | solution.py:37
  198.2 7.2 %branch_1_fun.37 = (f32[2,512,512]{2,1,0:T(8,128)}, bf16[512,512]{1,0:T(8,128)(2,1)S(1)}, bf16[512,512]{1,0:T(8,128)(2,1)S(1)}, f32[8,512]{1,0:T(8,128)S(1)}) custom-call(s32[5]{0:T(128)S(1)} %get-tuple-element.85.refs_0_, bf16[2,512,512]{2,1,0:T(8,128)(2,1)S(1)} %copy-done.10, f32[512,512]{1,0:T(8,128)S(1)} %copy-done.29, ...), custom_call_target="tpu_custom_call", output_to_operand_aliasing={{0}: (16, {})} | custom-call | flops 3072000000 | bytes 11534336 | tf_op jit(solution)/shard_map/cond/branch_1_fun/pallas_call | solution.py:645
  214.5 12.6 %collective-permute-done.9.refs_4_ = f32[64,2176]{1,0:T(8,128)S(1)} collective-permute-done((f32[64,2176]{1,0:T(8,128)S(1)}, f32[64,2176]{1,0:T(8,128)S(1)}, u32[]{:S(2)}, u32[]{:S(2)}) %collective-permute-start.9) | collective-permute-done | bytes 557088 | tf_op jit(solution)/shard_map/cond/branch_1_fun/ppermute | solution.py:37
  231.1 6.1 %collective-permute-done.11.refs_4_ = f32[32,2176]{1,0:T(8,128)S(1)} collective-permute-done((f32[32,2176]{1,0:T(8,128)S(1)}, f32[32,2176]{1,0:T(8,128)S(1)}, u32[]{:S(2)}, u32[]{:S(2)}) %collective-permute-start.11) | collective-permute-done | bytes 278560 | tf_op jit(solution)/shard_map/cond/branch_1_fun/ppermute | solution.py:37
  242.3 6.3 %collective-permute-done.12.refs_2_ = f32[32,2176]{1,0:T(8,128)S(1)} collective-permute-done((f32[32,2176]{1,0:T(8,128)S(1)}, f32[32,2176]{1,0:T(8,128)S(1)}, u32[]{:S(2)}, u32[]{:S(2)}) %collective-permute-start.12) | collective-permute-done | bytes 278560 | tf_op jit(solution)/shard_map/cond/branch_1_fun/ppermute | solution.py:37
  252.0 12.1 %collective-permute-done.13.refs_1_ = f32[16,2176]{1,0:T(8,128)S(1)} collective-permute-done((f32[16,2176]{1,0:T(8,128)S(1)}, f32[16,2176]{1,0:T(8,128)S(1)}, u32[]{:S(2)}, u32[]{:S(2)}) %collective-permute-start.13) | collective-permute-done | bytes 139296 | tf_op jit(solution)/shard_map/cond/branch_1_fun/ppermute | solution.py:37
  264.1 7.9 %collective-permute-done.14.refs_2_ = f32[16,2176]{1,0:T(8,128)S(1)} collective-permute-done((f32[16,2176]{1,0:T(8,128)S(1)}, f32[16,2176]{1,0:T(8,128)S(1)}, u32[]{:S(2)}, u32[]{:S(2)}) %collective-permute-start.14) | collective-permute-done | bytes 139296 | tf_op jit(solution)/shard_map/cond/branch_1_fun/ppermute | solution.py:37
  272.7 11.1 %collective-permute-done.15.refs_2_ = f32[32,2176]{1,0:T(8,128)S(1)} collective-permute-done((f32[32,2176]{1,0:T(8,128)S(1)}, f32[32,2176]{1,0:T(8,128)S(1)}, u32[]{:S(2)}, u32[]{:S(2)}) %collective-permute-start.15) | collective-permute-done | bytes 278560 | tf_op jit(solution)/shard_map/cond/branch_1_fun/ppermute | solution.py:37
  287.0 8.6 %collective-permute-done.17.refs_4_ = f32[32,2176]{1,0:T(8,128)S(1)} collective-permute-done((f32[32,2176]{1,0:T(8,128)S(1)}, f32[32,2176]{1,0:T(8,128)S(1)}, u32[]{:S(2)}, u32[]{:S(2)}) %collective-permute-start.17) | collective-permute-done | bytes 278560 | tf_op jit(solution)/shard_map/cond/branch_1_fun/ppermute | solution.py:37
  302.0 11.0 %collective-permute-done.18.refs_2_ = f32[64,2176]{1,0:T(8,128)S(1)} collective-permute-done((f32[64,2176]{1,0:T(8,128)S(1)}, f32[64,2176]{1,0:T(8,128)S(1)}, u32[]{:S(2)}, u32[]{:S(2)}) %collective-permute-start.18) | collective-permute-done | bytes 557088 | tf_op jit(solution)/shard_map/cond/branch_1_fun/ppermute | solution.py:37
  324.6 4.8 %copy.66 = f32[512,2048]{1,0:T(8,128)} copy(f32[512,2048]{1,0:T(8,128)} %get-tuple-element.338) | data formatting | bytes 8388608
  (216 shorter events, 113.6 us)
Async XLA Ops:
  7.2 317.4 %all-reduce.3.cloned.1.call-start = ((), (), s32[]{:S(2)}) async-start(), calls=%async_computation | async-start | bytes 16777216 | tf_op jit(solution)/shard_map/psum | solution.py:40
  16.9 10.0 %collective-permute-start.22 = (f32[4,72,256]{2,1,0:T(8,128)S(1)}, f32[4,72,256]{2,1,0:T(8,128)S(1)}, u32[]{:S(2)}, u32[]{:S(2)}) collective-permute-start(f32[4,72,256]{2,1,0:T(8,128)S(1)} %get-tuple-element.227.refs_8_), channel_id=1, source_target_pairs={{0,4},{4,0},{1,5},{5,1},{2,6},{6,2},{3,7},{7,3},{8,12},{12,8},{9,1... | collective-permute-start | bytes 884744 | tf_op jit(solution)/shard_map/ppermute | solution.py:37
  27.0 9.1 %collective-permute-start.23 = (f32[4,72,256]{2,1,0:T(8,128)S(1)}, f32[4,72,256]{2,1,0:T(8,128)S(1)}, u32[]{:S(2)}, u32[]{:S(2)}) collective-permute-start(f32[4,72,256]{2,1,0:T(8,128)S(1)} %shard_map.200.refs_0_), channel_id=1, source_target_pairs={{0,8},{1,9},{2,10},{3,11},{4,12},{5,13},{6,14},{7,15}} | collective-permute-start | bytes 884744 | tf_op jit(solution)/shard_map/ppermute | solution.py:50
  36.1 8.6 %collective-permute-start.25 = (f32[4,72,256]{2,1,0:T(8,128)S(1)}, f32[4,72,256]{2,1,0:T(8,128)S(1)}, u32[]{:S(2)}, u32[]{:S(2)}) collective-permute-start(f32[4,72,256]{2,1,0:T(8,128)S(1)} %shard_map.202.refs_2_), channel_id=1, source_target_pairs={{8,16},{9,17},{10,18},{11,19},{12,20},{13,21},{14,22},{15,23}} | collective-permute-start | bytes 884744 | tf_op jit(solution)/shard_map/ppermute | solution.py:50
  53.0 19.6 %collective-permute-start.28 = (f32[4,72,256]{2,1,0:T(8,128)S(1)}, f32[4,72,256]{2,1,0:T(8,128)S(1)}, u32[]{:S(2)}, u32[]{:S(2)}) collective-permute-start(f32[4,72,256]{2,1,0:T(8,128)S(1)} %shard_map.209.refs_3_), channel_id=1, source_target_pairs={{16,24},{17,25},{18,26},{19,27},{20,28},{21,29},{22,30},{23,31}} | collective-permute-start | bytes 884744 | tf_op jit(solution)/shard_map/ppermute | solution.py:50
  118.8 8.1 %collective-permute-start.31 = (f32[4,72,256]{2,1,0:T(8,128)S(1)}, f32[4,72,256]{2,1,0:T(8,128)S(1)}, u32[]{:S(2)}, u32[]{:S(2)}) collective-permute-start(f32[4,72,256]{2,1,0:T(8,128)S(1)} %get-tuple-element.243.refs_6_.refs_14_), channel_id=1, source_target_pairs={{0,4},{4,0},{1,5},{5,1},{2,6},{6,2},{3,7},{7,3},{8,12},{12,8},{9,1... | collective-permute-start | bytes 884744 | tf_op jit(solution)/shard_map/ppermute | solution.py:37
  128.2 13.6 %collective-permute-start.33 = (f32[4,72,256]{2,1,0:T(8,128)S(1)}, f32[4,72,256]{2,1,0:T(8,128)}, u32[]{:S(2)}, u32[]{:S(2)}) collective-permute-start(f32[4,72,256]{2,1,0:T(8,128)S(1)} %get-tuple-element.249.refs_2_.refs_8_), channel_id=1, source_target_pairs={{0,4},{4,0},{1,5},{5,1},{2,6},{6,2},{3,7},{7,3},{8,12},{12,8},{9,1... | collective-permute-start | bytes 884744 | tf_op jit(solution)/shard_map/ppermute | solution.py:37
  142.0 8.3 %collective-permute-start.1 = (f32[4,72,256]{2,1,0:T(8,128)S(1)}, f32[4,72,256]{2,1,0:T(8,128)S(1)}, u32[]{:S(2)}, u32[]{:S(2)}) collective-permute-start(f32[4,72,256]{2,1,0:T(8,128)S(1)} %branch_1_fun.25.refs_2_), channel_id=1, source_target_pairs={{16,8},{17,9},{18,10},{19,11},{20,12},{21,13},{22,14},{23,15}} | collective-permute-start | bytes 884744 | tf_op jit(solution)/shard_map/cond/branch_1_fun/ppermute | solution.py:50
  150.3 23.3 %collective-permute-start.3 = (f32[4,72,256]{2,1,0:T(8,128)S(1)}, f32[4,72,256]{2,1,0:T(8,128)S(1)}, u32[]{:S(2)}, u32[]{:S(2)}) collective-permute-start(f32[4,72,256]{2,1,0:T(8,128)S(1)} %branch_1_fun.28.refs_2_), channel_id=1, source_target_pairs={{8,0},{9,1},{10,2},{11,3},{12,4},{13,5},{14,6},{15,7}} | collective-permute-start | bytes 884744 | tf_op jit(solution)/shard_map/cond/branch_1_fun/ppermute | solution.py:50
  151.8 23.5 %collective-permute-start.2 = (f32[4,72,256]{2,1,0:T(8,128)S(1)}, f32[4,72,256]{2,1,0:T(8,128)S(1)}, u32[]{:S(2)}, u32[]{:S(2)}) collective-permute-start(f32[4,72,256]{2,1,0:T(8,128)S(1)} %branch_1_fun.29.refs_13_), channel_id=1, source_target_pairs={{16,8},{17,9},{18,10},{19,11},{20,12},{21,13},{22,14},{23,15}} | collective-permute-start | bytes 884744 | tf_op jit(solution)/shard_map/cond/branch_1_fun/ppermute | solution.py:50
  175.4 13.3 %collective-permute-start.5 = (f32[4,72,256]{2,1,0:T(8,128)S(1)}, f32[4,72,256]{2,1,0:T(8,128)S(1)}, u32[]{:S(2)}, u32[]{:S(2)}) collective-permute-start(f32[4,72,256]{2,1,0:T(8,128)S(1)} %branch_1_fun.33.refs_13_), channel_id=1, source_target_pairs={{8,0},{9,1},{10,2},{11,3},{12,4},{13,5},{14,6},{15,7}} | collective-permute-start | bytes 884744 | tf_op jit(solution)/shard_map/cond/branch_1_fun/ppermute | solution.py:50
  189.8 8.4 %collective-permute-start.6 = (f32[4,72,256]{2,1,0:T(8,128)S(1)}, f32[4,72,256]{2,1,0:T(8,128)S(1)}, u32[]{:S(2)}, u32[]{:S(2)}) collective-permute-start(f32[4,72,256]{2,1,0:T(8,128)S(1)} %get-tuple-element.133.refs_17_), channel_id=1, source_target_pairs={{0,4},{4,0},{1,5},{5,1},{2,6},{6,2},{3,7},{7,3},{8,12},{12,8},{9,1... | collective-permute-start | bytes 884744 | tf_op jit(solution)/shard_map/cond/branch_1_fun/ppermute | solution.py:37
  212.4 14.7 %collective-permute-start.9 = (f32[64,2176]{1,0:T(8,128)S(1)}, f32[64,2176]{1,0:T(8,128)S(1)}, u32[]{:S(2)}, u32[]{:S(2)}) collective-permute-start(f32[64,2176]{1,0:T(8,128)S(1)} %get-tuple-element.150), channel_id=1, source_target_pairs={{0,4},{4,0},{1,5},{5,1},{2,6},{6,2},{3,7},{7,3},{8,12},{12,8},{9,1... | collective-permute-start | bytes 1671176 | tf_op jit(solution)/shard_map/cond/branch_1_fun/ppermute | solution.py:37
  212.8 14.4 %collective-permute-start.8 = (f32[64,2176]{1,0:T(8,128)S(1)}, f32[64,2176]{1,0:T(8,128)S(1)}, u32[]{:S(2)}, u32[]{:S(2)}) collective-permute-start(f32[64,2176]{1,0:T(8,128)S(1)} %get-tuple-element.148.refs_5_), channel_id=1, source_target_pairs={{0,2},{2,0},{1,3},{3,1},{4,6},{6,4},{5,7},{7,5},{8,10},{10,8},{9,1... | collective-permute-start | bytes 1671176 | tf_op jit(solution)/shard_map/cond/branch_1_fun/ppermute | solution.py:37
  227.9 9.3 %collective-permute-start.11 = (f32[32,2176]{1,0:T(8,128)S(1)}, f32[32,2176]{1,0:T(8,128)S(1)}, u32[]{:S(2)}, u32[]{:S(2)}) collective-permute-start(f32[32,2176]{1,0:T(8,128)S(1)} %get-tuple-element.154), channel_id=1, source_target_pairs={{0,2},{2,0},{1,3},{3,1},{4,6},{6,4},{5,7},{7,5},{8,10},{10,8},{9,1... | collective-permute-start | bytes 835592 | tf_op jit(solution)/shard_map/cond/branch_1_fun/ppermute | solution.py:37
  229.6 10.1 %collective-permute-start.10 = (f32[32,2176]{1,0:T(8,128)S(1)}, f32[32,2176]{1,0:T(8,128)S(1)}, u32[]{:S(2)}, u32[]{:S(2)}) collective-permute-start(f32[32,2176]{1,0:T(8,128)S(1)} %get-tuple-element.152.refs_5_), channel_id=1, source_target_pairs={{0,4},{4,0},{1,5},{5,1},{2,6},{6,2},{3,7},{7,3},{8,12},{12,8},{9,1... | collective-permute-start | bytes 835592 | tf_op jit(solution)/shard_map/cond/branch_1_fun/ppermute | solution.py:37
  240.4 8.2 %collective-permute-start.12 = (f32[32,2176]{1,0:T(8,128)S(1)}, f32[32,2176]{1,0:T(8,128)S(1)}, u32[]{:S(2)}, u32[]{:S(2)}) collective-permute-start(f32[32,2176]{1,0:T(8,128)S(1)} %get-tuple-element.156.refs_3_), channel_id=1, source_target_pairs={{0,8},{8,0},{16,24},{24,16},{1,9},{9,1},{17,25},{25,17},{2,10},{10... | collective-permute-start | bytes 835592 | tf_op jit(solution)/shard_map/cond/branch_1_fun/ppermute | solution.py:37
  249.1 14.9 %collective-permute-start.13 = (f32[16,2176]{1,0:T(8,128)S(1)}, f32[16,2176]{1,0:T(8,128)S(1)}, u32[]{:S(2)}, u32[]{:S(2)}) collective-permute-start(f32[16,2176]{1,0:T(8,128)S(1)} %get-tuple-element.158.refs_2_), channel_id=1, source_target_pairs={{0,16},{16,0},{8,24},{24,8},{1,17},{17,1},{9,25},{25,9},{2,18},{18... | collective-permute-start | bytes 417800 | tf_op jit(solution)/shard_map/cond/branch_1_fun/ppermute | solution.py:37
  264.1 8.0 %collective-permute-start.14 = (f32[16,2176]{1,0:T(8,128)S(1)}, f32[16,2176]{1,0:T(8,128)S(1)}, u32[]{:S(2)}, u32[]{:S(2)}) collective-permute-start(f32[16,2176]{1,0:T(8,128)S(1)} %branch_1_fun.44.refs_1_.refs_3_), channel_id=1, source_target_pairs={{0,16},{16,0},{8,24},{24,8},{1,17},{17,1},{9,25},{25,9},{2,18},{18... | collective-permute-start | bytes 417800 | tf_op jit(solution)/shard_map/cond/branch_1_fun/ppermute | solution.py:37
  272.6 11.2 %collective-permute-start.15 = (f32[32,2176]{1,0:T(8,128)S(1)}, f32[32,2176]{1,0:T(8,128)S(1)}, u32[]{:S(2)}, u32[]{:S(2)}) collective-permute-start(f32[32,2176]{1,0:T(8,128)S(1)} %branch_1_fun.45.refs_1_.refs_3_), channel_id=1, source_target_pairs={{0,8},{8,0},{16,24},{24,16},{1,9},{9,1},{17,25},{25,17},{2,10},{10... | collective-permute-start | bytes 835592 | tf_op jit(solution)/shard_map/cond/branch_1_fun/ppermute | solution.py:37
  284.5 11.1 %collective-permute-start.17 = (f32[32,2176]{1,0:T(8,128)S(1)}, f32[32,2176]{1,0:T(8,128)S(1)}, u32[]{:S(2)}, u32[]{:S(2)}) collective-permute-start(f32[32,2176]{1,0:T(8,128)S(1)} %get-tuple-element.290.refs_3_), channel_id=1, source_target_pairs={{0,2},{2,0},{1,3},{3,1},{4,6},{6,4},{5,7},{7,5},{8,10},{10,8},{9,1... | collective-permute-start | bytes 835592 | tf_op jit(solution)/shard_map/cond/branch_1_fun/ppermute | solution.py:37
  286.9 12.4 %collective-permute-start.16 = (f32[32,2176]{1,0:T(8,128)S(1)}, f32[32,2176]{1,0:T(8,128)S(1)}, u32[]{:S(2)}, u32[]{:S(2)}) collective-permute-start(f32[32,2176]{1,0:T(8,128)S(1)} %get-tuple-element.291.refs_1_.refs_5_), channel_id=1, source_target_pairs={{0,4},{4,0},{1,5},{5,1},{2,6},{6,2},{3,7},{7,3},{8,12},{12,8},{9,1... | collective-permute-start | bytes 835592 | tf_op jit(solution)/shard_map/cond/branch_1_fun/ppermute | solution.py:37
  300.0 13.1 %collective-permute-start.18 = (f32[64,2176]{1,0:T(8,128)S(1)}, f32[64,2176]{1,0:T(8,128)S(1)}, u32[]{:S(2)}, u32[]{:S(2)}) collective-permute-start(f32[64,2176]{1,0:T(8,128)S(1)} %get-tuple-element.159.refs_1_.refs_5_), channel_id=1, source_target_pairs={{0,2},{2,0},{1,3},{3,1},{4,6},{6,4},{5,7},{7,5},{8,10},{10,8},{9,1... | collective-permute-start | bytes 1671176 | tf_op jit(solution)/shard_map/cond/branch_1_fun/ppermute | solution.py:37
  302.0 11.2 %collective-permute-start.19 = (f32[64,2176]{1,0:T(8,128)S(1)}, f32[64,2176]{1,0:T(8,128)S(1)}, u32[]{:S(2)}, u32[]{:S(2)}) collective-permute-start(f32[64,2176]{1,0:T(8,128)S(1)} %get-tuple-element.160.refs_3_), channel_id=1, source_target_pairs={{0,4},{4,0},{1,5},{5,1},{2,6},{6,2},{3,7},{7,3},{8,12},{12,8},{9,1... | collective-permute-start | bytes 1671176 | tf_op jit(solution)/shard_map/cond/branch_1_fun/ppermute | solution.py:37
  (69 other events, 621.8 us)
Sparse Core Ops, SparseCore 0:
  118.9 202.0 all-reduce.2

commit v5 on v4

--- a/solution.py
+++ b/solution.py
@@ -583,25 +583,28 @@
 
 def block_kernel(g0, g1, f0, f1, h0, h1, u0, u1, down, up):
     p = pl.program_id(0)
-    n = pl.num_programs(0) // 2
-
-    @pl.when(p < n)
+
+    @pl.when(p < 4)
     def _():
         down[...] = mm(g0[...].T, f0[...]) + mm(g1[...].T, f1[...])
 
-    @pl.when(p >= n)
+    @pl.when(p >= 4)
     def _():
         up[...] = mm(h0[...].T, u0[...]) + mm(h1[...].T, u1[...])
 
 
-def late_kernel(c, a0, a1, b0, b1, b2, b3, b4, b5, n0, n1, n2, n3, o0, o1, d0, d1, out):
+def early_kernel(c, a0, a1, b0, b1, a2, a3, b2, b3, out):
+    out[:, :512] = mm(a0[...].T, b0[...]) + mm(a1[...].T, b1[...])
+    out[:, 512:] = mm(a2[...].T, b2[...]) + mm(a3[...].T, b3[...])
+
+
+def late_kernel(c, a0, a1, b0, b1, b2, b3, b4, b5, n0, n1, n2, n3, out):
     a = jnp.concatenate([a0[...].T, a1[...].T], axis=1)
     for n, (first, second) in enumerate(((b0, b1), (b2, b3), (b4, b5))):
         both = jnp.concatenate([first[...], second[...]], axis=0)
         out[:, 512 * n : 512 * n + 512] = mm(a, both)
-    out[:, 1536:2048] = mm(o0[...].T, d0[...]) + mm(o1[...].T, d1[...])
     sums = [n0[...] + n1[...], n2[...] + n3[...]]
-    out[:, 2048:] = jnp.concatenate(sums + [jnp.zeros((112, out.shape[0]), F32)], axis=0).T
+    out[:, 1536:] = jnp.concatenate(sums + [jnp.zeros((112, out.shape[0]), F32)], axis=0).T
 
 
 def params(limit):
@@ -686,34 +689,47 @@
     sg = pl.BlockSpec((rows, 512), lambda p: (0, first(p)))
     su = pl.BlockSpec((rows, 512), lambda p: (0, second(p)))
     return call(
-        block_kernel, 2 * n, [sg, sg, one, one, one, one, su, su],
+        block_kernel, 2 * n - 1, [sg, sg, one, one, one, one, su, su],
         [(pl.BlockSpec((512, width), lambda p: (first(p), 0)), (wide, width), F32),
-         (pl.BlockSpec((width, 512), lambda p: (0, second(p))), (width, wide), F32)],
+         (pl.BlockSpec((width, 512), lambda p: (0, second(p))), (width, wide - 512), F32)],
         flops=8 * rows * width * wide, nbytes=8 * width * wide + 8 * rows * wide,
     )(*gl, *df, *h2, *du, after=after)
 
 
-def late_weights(give, bits, h1, dq, dk, dv, ng1, ng2, a, db, after=()):
+def early_weights(give, bits, h2, du, a, db, after=()):
+    rows, n = db[0].shape
+    m = n // 2
+    at, end = half_of(give), du[0].shape[1] // 512 - 1
+    sa, sb = pl.BlockSpec((rows, m), lambda p, c: (0, at(c))), whole((rows, n))
+    sd = pl.BlockSpec((rows, 512), lambda p, c: (0, end))
+    return call(
+        early_kernel, 1, [sa, sa, sd, sd, sa, sa, sb, sb],
+        [(whole((m, 2 * n)), (m, 2 * n), F32)],
+        flops=8 * rows * m * n, nbytes=8 * m * n + 8 * rows * n, scalars=1,
+    )(bits, *h2, *du, *a, *db, after=after)[0]
+
+
+def late_weights(give, bits, h1, dq, dk, dv, ng1, ng2, after=()):
     rows, n = dk[0].shape
     m = n // 2
     at = half_of(give)
     sa, sb = pl.BlockSpec((rows, m), lambda p, c: (0, at(c))), whole((rows, n))
     sn = pl.BlockSpec((8, m), lambda p, c: (0, at(c)))
-    wide = 4 * n + LANES
+    wide = 3 * n + LANES
     return call(
-        late_kernel, 1, [sa] * 2 + [sb] * 6 + [sn] * 4 + [sa] * 2 + [sb] * 2,
-        [(whole((m, wide)), (m, wide), F32)],
-        flops=16 * rows * m * n, nbytes=16 * m * n + 16 * rows * n, scalars=1,
-    )(bits, *h1, *dq, *dk, *dv, *ng1, *ng2, *a, *db, after=after)[0]
+        late_kernel, 1, [sa] * 2 + [sb] * 6 + [sn] * 4, [(whole((m, wide)), (m, wide), F32)],
+        flops=12 * rows * m * n, nbytes=12 * m * n + 12 * rows * n, scalars=1,
+    )(bits, *h1, *dq, *dk, *dv, *ng1, *ng2, after=after)[0]
 
 
 FRONT = (
-    "M0", "f", "M1", "f", "g", "Q0", "f", "g", "Q1", "f", "g", "A0", "f", "g", "A1", "N0", "g",
-    "p", "N1", "p", "q",
+    "M0", "f", "M1", "f", "g", "Q0", "f", "g", "Q1", "f", "g", "A0", "f", "g", "A1", "g", "N0",
+    "p", "N1", "q", "p",
 )
 BACK = (
-    "p", "q", "I0a", "p", "q", "I0b", "I1a", "p", "q", "I1b", "L0", "q", "L1", "Gk", "k", "Kk",
-    "k", "k", "k", "k", "k", "k", "k", "k", "k", "Fk",
+    "p", "q", "Ge", "e", "I0a", "Ke", "p", "q", "e", "I0b", "I1a", "p", "q", "e", "I1b", "e",
+    "L0", "q", "e", "L1", "Gk", "k", "Kk", "e", "k", "e", "k", "e", "k", "e", "k", "e", "k", "Fe",
+    "k", "k", "k", "k", "Fk",
 )
 
 
@@ -774,10 +790,10 @@
     def middle_of(s, prefix, after):
         pq = maps[s][4]
         return call(
-                functools.partial(middle_kernel, s), wide // 512,
+                functools.partial(middle_kernel, s), wide // 1024,
                 [SMEM, SMEM, of_seq(s, (rows, width)), of_seq(s, (rows, width)), full((rows, 2048)),
                  full((rows, 1024)), full(heads), full(heads), vec, vec, full((width, width)),
-                 cols(width, 512), pl.BlockSpec((512, width), lambda p: (p, 0))] + [ANY] * s,
+                 cols(width, 1024), pl.BlockSpec((1024, width), lambda p: (p, 0))] + [ANY] * s,
                 [(of_seq(s, (rows, width)), inputs.shape, BF),
                  (full((rows, width)), (rows, width), F32),
                  (full((rows, 1024)), (rows, 1024), BF),
@@ -785,14 +801,14 @@
                  (full((rows, width)), (rows, width), BF),
                  (full((rows, width)), (rows, width), BF),
                  (full((rows, width)), (rows, width), BF),
-                 (cols(rows, 512), (rows, wide), BF),
-                 (cols(rows, 512), (rows, wide), BF),
+                 (cols(rows, 1024), (rows, wide), BF),
+                 (cols(rows, 1024), (rows, wide), BF),
                  *states,
                  (full((8, width)), (8, width), F32)],
                 scratch=[pltpu.VMEM((rows, width), F32), pltpu.VMEM((rows, width), F32),
                          pltpu.VMEM((rows, LANES), F32)]
                 + [pltpu.VMEM((rows, width), F32)] * 3,
-                flops=rows * 11_000_000, nbytes=24 * 2**20, grant=24, aliases={13: 0} if s else {},
+                flops=rows * 11_000_000, nbytes=24 * 2**20, grant=30, aliases={13: 0} if s else {},
             )(meta, bits, inputs, cotangent, pq, locals_[s], *prefix, g2, n2, out_weight,
               up_weight, down_weight, *([mids[0][0]] if s else []), after=after)
 
@@ -832,12 +848,17 @@
         return [[mids[s][n] for s in range(seqs)] for n in index]
 
     def weights(name, give, after):
+        if name == "e":
+            return early_weights(give, bits, *of_mids(5, 8, 3, 4), after=after)
         h1 = [maps[s][0] for s in range(seqs)]
         dq = [inners[s][0] for s in range(seqs)]
         dk, dv, ng1 = ([lasts[s][n] for s in range(seqs)] for n in (1, 2, 3))
-        return late_weights(give, bits, h1, dq, dk, dv, ng1, *of_mids(11, 3, 4), after=after)
-
-    shapes = ((width, 3 * width), (width, width), (width, LANES))
+        return late_weights(give, bits, h1, dq, dk, dv, ng1, *of_mids(11), after=after)
+
+    shapes = {
+        "e": ((width, 512), (width, width)),
+        "k": ((width, 3 * width), (width, LANES)),
+    }
 
     def play(items, token):
         for item in items:
@@ -869,7 +890,7 @@
             elif kind == "G":
                 token = weights(name, True, after)
                 flows[name] = comm.sums(
-                    token, functools.partial(kept.get, name), bits, shapes
+                    token, functools.partial(kept.get, name), bits, shapes[name]
                 )
                 next(flows[name])
             elif kind == "K":
@@ -887,14 +908,15 @@
 
     def rest():
         play(BACK, parts[1])
-        qkv_grad, outw_grad, small = ends["k"]
-        return qkv_grad, outw_grad, small[:, :16].T, lasts[seqs - 1][0]
+        qkv_grad, small = ends["k"]
+        return *ends["e"], qkv_grad, small[:, :16].T, lasts[seqs - 1][0]
 
     def nothing():
-        shaped = [(width, 3 * width), (width, width), (16, width)]
+        shaped = [(width, 512), (width, width), (width, 3 * width), (16, width)]
         return *(jnp.zeros(s, F32) for s in shaped), cotangent.astype(F32)
 
-    qkv_grad, outw_grad, small, grad = lax.cond(jnp.max(lengths) > 0, rest, nothing)
+    up_end, outw_grad, qkv_grad, small, grad = lax.cond(jnp.max(lengths) > 0, rest, nothing)
+    up_grad = jnp.concatenate([up_grad, up_end], axis=1)
     out = mids[seqs - 1][0]
     return (
         out,

time: 337 us -> 325 us (0.964); the launches traced: 339 us -> 320 us
  waiting for transfers between devices: 133 us -> 118 us
  local copies, waits for them, and re-layouts: 13.4 us -> 7.11 us
  Pallas kernels: 127 us -> 121 us
  starting transfers between devices: 44.7 us -> 48.8 us
  other arithmetic: 3.98 us -> 7.9 us
    ppermute x22 -> x36, waiting for transfers between devices: 121 us -> 95.3 us  [swap(): return lax.ppermute(part, name, pairs)]
    ppermute x12, waiting for transfers between devices: 12.7 us -> 22.8 us  [carry(): arrived.append(lax.ppermute(out, 'z', [hop]))]
    unnamed x65 -> x78, local copies, waits for them, and re-layouts: 12.3 us -> 6.11 us
    pallas_call x43 -> x55, Pallas kernels: 127 us -> 121 us  [run(): pl.pallas_call(waiting, grid_spec=pltpu.PrefetchScalarGridSpec(num_scalar...]
    concatenate x0 -> x1, other arithmetic: none -> 4.43 us  [body(): up_grad = jnp.concatenate([up_grad, up_end], axis=1)]
    ppermute x22 -> x36, starting transfers between devices: 29 us -> 32.3 us  [swap(): return lax.ppermute(part, name, pairs)]
  transfers between devices with their start and end apart: 35 -> 49, of which waited for: 24 -> 27; matrix products, arithmetic and copies ran while one was open for 1% -> 1% of each run, Pallas kernels for 25% -> 33%
where the time goes in v5:
time: 325 us; the launch traced here: 320 us
  Pallas kernels  121 us (37%)
  waiting for transfers between devices  118 us (36%)
  starting transfers between devices  48.8 us (15%)
  between operations  15.6 us (5%)
  other arithmetic  7.9 us (2%)
  local copies, waits for them, and re-layouts  7.11 us (2%)
    pallas_call x55, Pallas kernels, run(): pl.pallas_call(waiting, grid_spec=pltpu.PrefetchScalarGridSpec(num_scalar...  121 us
    ppermute x36, waiting for transfers between devices, swap(): return lax.ppermute(part, name, pairs)  95.3 us
    ppermute x36, starting transfers between devices, swap(): return lax.ppermute(part, name, pairs)  32.3 us
    ppermute x12, waiting for transfers between devices, carry(): arrived.append(lax.ppermute(out, 'z', [hop]))  22.8 us
    ppermute x12, starting transfers between devices, carry(): arrived.append(lax.ppermute(out, 'z', [hop]))  16.5 us
  transfers between devices with their start and end apart: 49, of which 27 were waited for; matrix products, arithmetic and copies ran while one was open for 1% of the time, Pallas kernels for 33%

profile of v5, /device:TPU:0, one launch (start us, length us, event | category | flops | bytes accessed | tf_op | source)
XLA Modules:
  0.0 319.7 jit_solution(11071886257229027141)
XLA Ops:
  10.0 6.8 %shard_map.198 = (bf16[512,512]{1,0:T(8,128)(2,1)S(1)}, bf16[512,512]{1,0:T(8,128)(2,1)}, bf16[512,512]{1,0:T(8,128)(2,1)S(1)}, bf16[512,2048]{1,0:T(8,128)(2,1)...) custom-call(s32[3]{0:T(128)S(1)} %pad_add_fusion.refs_0_, s32[5]{0:T(128)S(1)} %stack.23.refs_1_.refs_0_, ...), custom_call_target="tpu_custom_call" | custom-call | flops 1536000000 | bytes 8388608 | tf_op jit(solution)/shard_map/pallas_call | solution.py:648
  19.9 6.2 %shard_map.199 = (bf16[512,512]{1,0:T(8,128)(2,1)S(1)}, bf16[512,512]{1,0:T(8,128)(2,1)}, bf16[512,512]{1,0:T(8,128)(2,1)S(1)}, bf16[512,2048]{1,0:T(8,128)(2,1)...) custom-call(s32[3]{0:T(128)S(1)} %pad_add_fusion.refs_0_, s32[5]{0:T(128)S(1)} %stack.23.refs_1_.refs_0_, ...), custom_call_target="tpu_custom_call" | custom-call | flops 1536000000 | bytes 8388608 | tf_op jit(solution)/shard_map/pallas_call | solution.py:648
  61.1 12.9 %shard_map.212 = (bf16[2,512,512]{2,1,0:T(8,128)(2,1)}, f32[512,512]{1,0:T(8,128)}, bf16[512,1024]{1,0:T(8,128)(2,1)}, bf16[512,512]{1,0:T(8,128)(2,1)}, bf16[51...) custom-call(s32[3]{0:T(128)S(1)} %pad_add_fusion.refs_0_, ...), custom_call_target="tpu_custom_call" | custom-call | flops 5632000000 | bytes 25165824 | tf_op jit(solution)/shard_map/pallas_call | solution.py:648
  76.6 13.2 %shard_map.213 = (bf16[2,512,512]{2,1,0:T(8,128)(2,1)}, f32[512,512]{1,0:T(8,128)}, bf16[512,1024]{1,0:T(8,128)(2,1)}, bf16[512,512]{1,0:T(8,128)(2,1)}, bf16[51...) custom-call(s32[3]{0:T(128)S(1)} %pad_add_fusion.refs_0_, ...), custom_call_target="tpu_custom_call", output_to_operand_aliasing={{0}: (13, {})} | custom-call | flops 5632000000 | bytes 25165824 | tf_op jit(solution)/shard_map/pallas_call | solution.py:648
  89.9 7.0 %shard_map.215 = (f32[2048,512]{1,0:T(8,128)S(1)}, f32[512,1536]{1,0:T(8,128)}) custom-call(bf16[512,2048]{1,0:T(8,128)(2,1)S(1)} %get-tuple-element.278.refs_0_, bf16[512,2048]{1,0:T(8,128)(2,1)S(1)} %get-tuple-element.279.refs_1_, bf16[512,512]{1,0:T(8,128)(2,1)S(1)} %get-tuple-element.280.refs_2_, bf16[512,512]{1,0:T(8,128)(2,1)S(1)} %get-tuple-element.281.refs_3_, ...), custom_call_target="tpu_custom_call" | custom-call | flops 4294967296 | bytes 16777216 | tf_op jit(solution)/shard_map/pallas_call | solution.py:648
  101.7 5.5 %collective-permute-done.47 = f32[4,72,256]{2,1,0:T(8,128)} collective-permute-done((f32[4,72,256]{2,1,0:T(8,128)S(1)}, f32[4,72,256]{2,1,0:T(8,128)}, u32[]{:S(2)}, u32[]{:S(2)}) %collective-permute-start.47) | collective-permute-done | bytes 294944 | tf_op jit(solution)/shard_map/ppermute | solution.py:37
  107.2 198.7 %conditional.1 = (f32[512,512]{1,0:T(8,128)S(1)}, f32[512,512]{1,0:T(8,128)}, f32[512,1536]{1,0:T(8,128)}, f32[16,512]{0,1:T(8,128)}, f32[2,512,512]{2,1,0:T(8,1...) conditional(s32[]{:T(128)} %convert_element_type.6, ...), branch_computations={%region_1.2_spmd, %region_2.3_spmd} | conditional | flops 29309861888 | bytes 275151072 | solution.py:918
  115.2 4.9 %branch_1_fun.40 = (bf16[512,512]{1,0:T(8,128)(2,1)S(1)}, f32[512,512]{1,0:T(8,128)S(1)}, f32[512,512]{1,0:T(8,128)S(1)}) custom-call(s32[5]{0:T(128)S(1)} %get-tuple-element.93.refs_0_, bf16[512,512]{1,0:T(8,128)(2,1)S(1)} %copy-done.49, bf16[512,512]{1,0:T(8,128)(2,1)S(1)} %copy-done.42, bf16[512,512]{1,0:T(8,128)(2,1)S(1)} %copy-done.44, ...), custom_call_target="tpu_custom_call" | custom-call | flops 5120000000 | bytes 6291456 | tf_op jit(solution)/shard_map/cond/branch_1_fun/pallas_call | solution.py:648
  126.2 4.7 %branch_1_fun.45 = (bf16[512,512]{1,0:T(8,128)(2,1)S(1)}, f32[512,512]{1,0:T(8,128)S(1)}, f32[512,512]{1,0:T(8,128)S(1)}) custom-call(s32[5]{0:T(128)S(1)} %get-tuple-element.93.refs_0_, bf16[512,512]{1,0:T(8,128)(2,1)S(1)} %copy-done.49, bf16[512,512]{1,0:T(8,128)(2,1)S(1)} %copy-done.42, ...), custom_call_target="tpu_custom_call", output_to_operand_aliasing={{0}: (10, {}), {1}: (11, {}), {2}: (12, {})} | custom-call | flops 5120000000 | bytes 6291456 | tf_op jit(solution)/shard_map/cond/branch_1_fun/pallas_call | solution.py:648
  131.0 4.7 %branch_1_fun.46 = (bf16[512,512]{1,0:T(8,128)(2,1)S(1)}, f32[512,512]{1,0:T(8,128)S(1)}, f32[512,512]{1,0:T(8,128)S(1)}) custom-call(s32[5]{0:T(128)S(1)} %get-tuple-element.93.refs_0_, bf16[512,512]{1,0:T(8,128)(2,1)S(1)} %copy-done.51, bf16[512,512]{1,0:T(8,128)(2,1)S(1)} %copy-done.45, bf16[512,512]{1,0:T(8,128)(2,1)S(1)} %copy-done.47, ...), custom_call_target="tpu_custom_call" | custom-call | flops 5120000000 | bytes 6291456 | tf_op jit(solution)/shard_map/cond/branch_1_fun/pallas_call | solution.py:648
  135.7 20.9 %collective-permute-done.6.refs_5_ = f32[4,72,256]{2,1,0:T(8,128)S(1)} collective-permute-done((f32[4,72,256]{2,1,0:T(8,128)S(1)}, f32[4,72,256]{2,1,0:T(8,128)S(1)}, u32[]{:S(2)}, u32[]{:S(2)}) %collective-permute-start.6) | collective-permute-done | bytes 294944 | tf_op jit(solution)/shard_map/cond/branch_1_fun/ppermute | solution.py:50
  163.5 4.9 %branch_1_fun.50 = (bf16[512,512]{1,0:T(8,128)(2,1)S(1)}, f32[512,512]{1,0:T(8,128)S(1)}, f32[512,512]{1,0:T(8,128)S(1)}) custom-call(s32[5]{0:T(128)S(1)} %get-tuple-element.93.refs_0_, bf16[512,512]{1,0:T(8,128)(2,1)S(1)} %copy-done.51, bf16[512,512]{1,0:T(8,128)(2,1)S(1)} %copy-done.45, ...), custom_call_target="tpu_custom_call", output_to_operand_aliasing={{0}: (10, {}), {1}: (11, {}), {2}: (12, {})} | custom-call | flops 5120000000 | bytes 6291456 | tf_op jit(solution)/shard_map/cond/branch_1_fun/pallas_call | solution.py:648
  168.5 5.3 %collective-permute-done.7.refs_2_ = f32[32,1024]{1,0:T(8,128)S(1)} collective-permute-done((f32[32,1024]{1,0:T(8,128)S(1)}, f32[32,1024]{1,0:T(8,128)S(1)}, u32[]{:S(2)}, u32[]{:S(2)}) %collective-permute-start.7) | collective-permute-done | bytes 131104 | tf_op jit(solution)/shard_map/cond/branch_1_fun/ppermute | solution.py:37
  174.4 7.2 %branch_1_fun.52 = (f32[2,512,512]{2,1,0:T(8,128)}, bf16[512,512]{1,0:T(8,128)(2,1)S(1)}, bf16[512,512]{1,0:T(8,128)(2,1)S(1)}, f32[8,512]{1,0:T(8,128)S(1)}) custom-call(s32[5]{0:T(128)S(1)} %get-tuple-element.93.refs_0_, bf16[2,512,512]{2,1,0:T(8,128)(2,1)S(1)} %get-tuple-element.145.refs_1_, f32[512,512]{1,0:T(8,128)S(1)} %copy-done.40, ...), custom_call_target="tpu_custom_call" | custom-call | flops 3072000000 | bytes 11534336 | tf_op jit(solution)/shard_map/cond/branch_1_fun/pallas_call | solution.py:648
  183.7 4.1 %collective-permute-done.9.refs_2_ = f32[32,1024]{1,0:T(8,128)S(1)} collective-permute-done((f32[32,1024]{1,0:T(8,128)S(1)}, f32[32,1024]{1,0:T(8,128)S(1)}, u32[]{:S(2)}, u32[]{:S(2)}) %collective-permute-start.9) | collective-permute-done | bytes 131104 | tf_op jit(solution)/shard_map/cond/branch_1_fun/ppermute | solution.py:37
  191.6 7.2 %branch_1_fun.55 = (f32[2,512,512]{2,1,0:T(8,128)}, bf16[512,512]{1,0:T(8,128)(2,1)S(1)}, bf16[512,512]{1,0:T(8,128)(2,1)S(1)}, f32[8,512]{1,0:T(8,128)S(1)}) custom-call(s32[5]{0:T(128)S(1)} %get-tuple-element.93.refs_0_, bf16[2,512,512]{2,1,0:T(8,128)(2,1)S(1)} %get-tuple-element.145.refs_1_, ...), custom_call_target="tpu_custom_call", output_to_operand_aliasing={{0}: (16, {})} | custom-call | flops 3072000000 | bytes 11534336 | tf_op jit(solution)/shard_map/cond/branch_1_fun/pallas_call | solution.py:648
  215.3 4.1 %collective-permute-done.18.refs_4_ = f32[64,1664]{1,0:T(8,128)S(1)} collective-permute-done((f32[64,1664]{1,0:T(8,128)S(1)}, f32[64,1664]{1,0:T(8,128)S(1)}, u32[]{:S(2)}, u32[]{:S(2)}) %collective-permute-start.18) | collective-permute-done | bytes 426016 | tf_op jit(solution)/shard_map/cond/branch_1_fun/ppermute | solution.py:37
  225.0 4.2 %collective-permute-done.22.refs_4_ = f32[32,1664]{1,0:T(8,128)S(1)} collective-permute-done((f32[32,1664]{1,0:T(8,128)S(1)}, f32[32,1664]{1,0:T(8,128)S(1)}, u32[]{:S(2)}, u32[]{:S(2)}) %collective-permute-start.22) | collective-permute-done | bytes 213024 | tf_op jit(solution)/shard_map/cond/branch_1_fun/ppermute | solution.py:37
  238.3 6.9 %collective-permute-done.25.refs_2_ = f32[32,1664]{1,0:T(8,128)S(1)} collective-permute-done((f32[32,1664]{1,0:T(8,128)S(1)}, f32[32,1664]{1,0:T(8,128)S(1)}, u32[]{:S(2)}, u32[]{:S(2)}) %collective-permute-start.25) | collective-permute-done | bytes 213024 | tf_op jit(solution)/shard_map/cond/branch_1_fun/ppermute | solution.py:37
  247.5 7.6 %collective-permute-done.27.refs_1_ = f32[16,1664]{1,0:T(8,128)S(1)} collective-permute-done((f32[16,1664]{1,0:T(8,128)S(1)}, f32[16,1664]{1,0:T(8,128)S(1)}, u32[]{:S(2)}, u32[]{:S(2)}) %collective-permute-start.27) | collective-permute-done | bytes 106528 | tf_op jit(solution)/shard_map/cond/branch_1_fun/ppermute | solution.py:37
  256.9 8.0 %collective-permute-done.28.refs_2_ = f32[16,1664]{1,0:T(8,128)S(1)} collective-permute-done((f32[16,1664]{1,0:T(8,128)S(1)}, f32[16,1664]{1,0:T(8,128)S(1)}, u32[]{:S(2)}, u32[]{:S(2)}) %collective-permute-start.28) | collective-permute-done | bytes 106528 | tf_op jit(solution)/shard_map/cond/branch_1_fun/ppermute | solution.py:37
  265.5 12.0 %collective-permute-done.29.refs_2_ = f32[32,1664]{1,0:T(8,128)S(1)} collective-permute-done((f32[32,1664]{1,0:T(8,128)S(1)}, f32[32,1664]{1,0:T(8,128)S(1)}, u32[]{:S(2)}, u32[]{:S(2)}) %collective-permute-start.29) | collective-permute-done | bytes 213024 | tf_op jit(solution)/shard_map/cond/branch_1_fun/ppermute | solution.py:37
  287.2 8.5 %collective-permute-done.32.refs_2_ = f32[64,1664]{1,0:T(8,128)S(1)} collective-permute-done((f32[64,1664]{1,0:T(8,128)S(1)}, f32[64,1664]{1,0:T(8,128)S(1)}, u32[]{:S(2)}, u32[]{:S(2)}) %collective-permute-start.32) | collective-permute-done | bytes 426016 | tf_op jit(solution)/shard_map/cond/branch_1_fun/ppermute | solution.py:37
  306.0 4.4 %pad_maximum_fusion = f32[512,2048]{1,0:T(8,128)} fusion(f32[512,512]{1,0:T(8,128)S(1)} %get-tuple-element.307, f32[512,1536]{1,0:T(8,128)} %get-tuple-element.309), kind=kLoop, calls=%fused_computation.1 | loop fusion | flops 1048576 | bytes 8388608 | tf_op jit(solution)/shard_map/concatenate | solution.py:919
  (285 shorter events, 131.7 us)
Async XLA Ops:
  7.2 298.8 %all-reduce.3.cloned.1.call-start = ((), (), s32[]{:S(2)}) async-start(), calls=%async_computation | async-start | bytes 14680064 | tf_op jit(solution)/shard_map/psum | solution.py:40
  16.9 10.0 %collective-permute-start.36 = (f32[4,72,256]{2,1,0:T(8,128)S(1)}, f32[4,72,256]{2,1,0:T(8,128)S(1)}, u32[]{:S(2)}, u32[]{:S(2)}) collective-permute-start(f32[4,72,256]{2,1,0:T(8,128)S(1)} %get-tuple-element.255.refs_8_), channel_id=1, source_target_pairs={{0,4},{4,0},{1,5},{5,1},{2,6},{6,2},{3,7},{7,3},{8,12},{12,8},{9,1... | collective-permute-start | bytes 884744 | tf_op jit(solution)/shard_map/ppermute | solution.py:37
  27.0 9.1 %collective-permute-start.37 = (f32[4,72,256]{2,1,0:T(8,128)S(1)}, f32[4,72,256]{2,1,0:T(8,128)S(1)}, u32[]{:S(2)}, u32[]{:S(2)}) collective-permute-start(f32[4,72,256]{2,1,0:T(8,128)S(1)} %shard_map.200.refs_0_), channel_id=1, source_target_pairs={{0,8},{1,9},{2,10},{3,11},{4,12},{5,13},{6,14},{7,15}} | collective-permute-start | bytes 884744 | tf_op jit(solution)/shard_map/ppermute | solution.py:50
  58.8 17.8 %collective-permute-start.43 = (f32[4,72,256]{2,1,0:T(8,128)S(1)}, f32[4,72,256]{2,1,0:T(8,128)S(1)}, u32[]{:S(2)}, u32[]{:S(2)}) collective-permute-start(f32[4,72,256]{2,1,0:T(8,128)S(1)} %get-tuple-element.271.refs_13_), channel_id=1, source_target_pairs={{0,4},{4,0},{1,5},{5,1},{2,6},{6,2},{3,7},{7,3},{8,12},{12,8},{9,1... | collective-permute-start | bytes 884744 | tf_op jit(solution)/shard_map/ppermute | solution.py:37
  74.0 15.8 %collective-permute-start.45 = (f32[4,72,256]{2,1,0:T(8,128)S(1)}, f32[4,72,256]{2,1,0:T(8,128)S(1)}, u32[]{:S(2)}, u32[]{:S(2)}) collective-permute-start(f32[4,72,256]{2,1,0:T(8,128)S(1)} %get-tuple-element.274.refs_14_), channel_id=1, source_target_pairs={{0,4},{4,0},{1,5},{5,1},{2,6},{6,2},{3,7},{7,3},{8,12},{12,8},{9,1... | collective-permute-start | bytes 884744 | tf_op jit(solution)/shard_map/ppermute | solution.py:37
  113.7 9.9 %collective-permute-start = (f32[256,1024]{1,0:T(8,128)S(1)}, f32[256,1024]{1,0:T(8,128)S(1)}, u32[]{:S(2)}, u32[]{:S(2)}) collective-permute-start(f32[256,1024]{1,0:T(8,128)S(1)} %branch_1_fun.39.refs_10_), channel_id=1, source_target_pairs={{0,1},{1,0},{2,3},{3,2},{4,5},{5,4},{6,7},{7,6},{8,9},{9,8},{10,11... | collective-permute-start | bytes 3145736 | tf_op jit(solution)/shard_map/cond/branch_1_fun/ppermute | solution.py:37
  113.7 9.1 %collective-permute-start.1 = (f32[4,72,256]{2,1,0:T(8,128)S(1)}, f32[4,72,256]{2,1,0:T(8,128)S(1)}, u32[]{:S(2)}, u32[]{:S(2)}) collective-permute-start(f32[4,72,256]{2,1,0:T(8,128)S(1)} %branch_1_fun.38.refs_9_.refs_0_), channel_id=1, source_target_pairs={{24,16},{25,17},{26,18},{27,19},{28,20},{29,21},{30,22},{31,23}} | collective-permute-start | bytes 884744 | tf_op jit(solution)/shard_map/cond/branch_1_fun/ppermute | solution.py:50
  121.6 35.1 %collective-permute-start.6 = (f32[4,72,256]{2,1,0:T(8,128)S(1)}, f32[4,72,256]{2,1,0:T(8,128)S(1)}, u32[]{:S(2)}, u32[]{:S(2)}) collective-permute-start(f32[4,72,256]{2,1,0:T(8,128)S(1)} %branch_1_fun.42.refs_2_), channel_id=1, source_target_pairs={{8,0},{9,1},{10,2},{11,3},{12,4},{13,5},{14,6},{15,7}} | collective-permute-start | bytes 884744 | tf_op jit(solution)/shard_map/cond/branch_1_fun/ppermute | solution.py:50
  122.9 34.8 %collective-permute-start.5 = (f32[4,72,256]{2,1,0:T(8,128)S(1)}, f32[4,72,256]{2,1,0:T(8,128)S(1)}, u32[]{:S(2)}, u32[]{:S(2)}) collective-permute-start(f32[4,72,256]{2,1,0:T(8,128)S(1)} %branch_1_fun.43.refs_3_), channel_id=1, source_target_pairs={{16,8},{17,9},{18,10},{19,11},{20,12},{21,13},{22,14},{23,15}} | collective-permute-start | bytes 884744 | tf_op jit(solution)/shard_map/cond/branch_1_fun/ppermute | solution.py:50
  124.3 34.8 %collective-permute-start.4 = (f32[64,1024]{1,0:T(8,128)S(1)}, f32[64,1024]{1,0:T(8,128)S(1)}, u32[]{:S(2)}, u32[]{:S(2)}) collective-permute-start(f32[64,1024]{1,0:T(8,128)S(1)} %get-tuple-element.120), channel_id=1, source_target_pairs={{0,4},{4,0},{1,5},{5,1},{2,6},{6,2},{3,7},{7,3},{8,12},{12,8},{9,1... | collective-permute-start | bytes 786440 | tf_op jit(solution)/shard_map/cond/branch_1_fun/ppermute | solution.py:37
  124.4 34.8 %collective-permute-start.3 = (f32[64,1024]{1,0:T(8,128)S(1)}, f32[64,1024]{1,0:T(8,128)S(1)}, u32[]{:S(2)}, u32[]{:S(2)}) collective-permute-start(f32[64,1024]{1,0:T(8,128)S(1)} %get-tuple-element.118.refs_13_), channel_id=1, source_target_pairs={{0,2},{2,0},{1,3},{3,1},{4,6},{6,4},{5,7},{7,5},{8,10},{10,8},{9,1... | collective-permute-start | bytes 786440 | tf_op jit(solution)/shard_map/cond/branch_1_fun/ppermute | solution.py:37
  157.7 16.7 %collective-permute-start.11 = (f32[4,72,256]{2,1,0:T(8,128)S(1)}, f32[4,72,256]{2,1,0:T(8,128)S(1)}, u32[]{:S(2)}, u32[]{:S(2)}) collective-permute-start(f32[4,72,256]{2,1,0:T(8,128)S(1)} %get-tuple-element.135.refs_2_), channel_id=1, source_target_pairs={{0,4},{4,0},{1,5},{5,1},{2,6},{6,2},{3,7},{7,3},{8,12},{12,8},{9,1... | collective-permute-start | bytes 884744 | tf_op jit(solution)/shard_map/cond/branch_1_fun/ppermute | solution.py:37
  157.8 23.8 %collective-permute-start.10 = (f32[4,72,256]{2,1,0:T(8,128)S(1)}, f32[4,72,256]{2,1,0:T(8,128)S(1)}, u32[]{:S(2)}, u32[]{:S(2)}) collective-permute-start(f32[4,72,256]{2,1,0:T(8,128)S(1)} %branch_1_fun.48.refs_5_), channel_id=1, source_target_pairs={{8,0},{9,1},{10,2},{11,3},{12,4},{13,5},{14,6},{15,7}} | collective-permute-start | bytes 884744 | tf_op jit(solution)/shard_map/cond/branch_1_fun/ppermute | solution.py:50
  161.5 12.2 %collective-permute-start.7 = (f32[32,1024]{1,0:T(8,128)S(1)}, f32[32,1024]{1,0:T(8,128)S(1)}, u32[]{:S(2)}, u32[]{:S(2)}) collective-permute-start(f32[32,1024]{1,0:T(8,128)S(1)} %get-tuple-element.137.refs_13_), channel_id=1, source_target_pairs={{0,4},{4,0},{1,5},{5,1},{2,6},{6,2},{3,7},{7,3},{8,12},{12,8},{9,1... | collective-permute-start | bytes 393224 | tf_op jit(solution)/shard_map/cond/branch_1_fun/ppermute | solution.py:37
  206.6 12.8 %collective-permute-start.18 = (f32[64,1664]{1,0:T(8,128)S(1)}, f32[64,1664]{1,0:T(8,128)S(1)}, u32[]{:S(2)}, u32[]{:S(2)}) collective-permute-start(f32[64,1664]{1,0:T(8,128)S(1)} %get-tuple-element.174), channel_id=1, source_target_pairs={{0,4},{4,0},{1,5},{5,1},{2,6},{6,2},{3,7},{7,3},{8,12},{12,8},{9,1... | collective-permute-start | bytes 1277960 | tf_op jit(solution)/shard_map/cond/branch_1_fun/ppermute | solution.py:37
  208.1 11.5 %collective-permute-start.17 = (f32[64,1664]{1,0:T(8,128)S(1)}, f32[64,1664]{1,0:T(8,128)S(1)}, u32[]{:S(2)}, u32[]{:S(2)}) collective-permute-start(f32[64,1664]{1,0:T(8,128)S(1)} %get-tuple-element.171.refs_3_), channel_id=1, source_target_pairs={{0,2},{2,0},{1,3},{3,1},{4,6},{6,4},{5,7},{7,5},{8,10},{10,8},{9,1... | collective-permute-start | bytes 1277960 | tf_op jit(solution)/shard_map/cond/branch_1_fun/ppermute | solution.py:37
  220.2 9.0 %collective-permute-start.22 = (f32[32,1664]{1,0:T(8,128)S(1)}, f32[32,1664]{1,0:T(8,128)S(1)}, u32[]{:S(2)}, u32[]{:S(2)}) collective-permute-start(f32[32,1664]{1,0:T(8,128)S(1)} %get-tuple-element.178), channel_id=1, source_target_pairs={{0,2},{2,0},{1,3},{3,1},{4,6},{6,4},{5,7},{7,5},{8,10},{10,8},{9,1... | collective-permute-start | bytes 638984 | tf_op jit(solution)/shard_map/cond/branch_1_fun/ppermute | solution.py:37
  221.8 10.0 %collective-permute-start.21 = (f32[32,1664]{1,0:T(8,128)S(1)}, f32[32,1664]{1,0:T(8,128)S(1)}, u32[]{:S(2)}, u32[]{:S(2)}) collective-permute-start(f32[32,1664]{1,0:T(8,128)S(1)} %get-tuple-element.175.refs_3_), channel_id=1, source_target_pairs={{0,4},{4,0},{1,5},{5,1},{2,6},{6,2},{3,7},{7,3},{8,12},{12,8},{9,1... | collective-permute-start | bytes 638984 | tf_op jit(solution)/shard_map/cond/branch_1_fun/ppermute | solution.py:37
  223.5 10.1 %collective-permute-start.20 = (f32[32,1024]{1,0:T(8,128)S(1)}, f32[32,1024]{1,0:T(8,128)S(1)}, u32[]{:S(2)}, u32[]{:S(2)}) collective-permute-start(f32[32,1024]{1,0:T(8,128)S(1)} %get-tuple-element.327.refs_3_), channel_id=1, source_target_pairs={{0,2},{2,0},{1,3},{3,1},{4,6},{6,4},{5,7},{7,5},{8,10},{10,8},{9,1... | collective-permute-start | bytes 393224 | tf_op jit(solution)/shard_map/cond/branch_1_fun/ppermute | solution.py:37
  224.1 12.5 %collective-permute-start.19 = (f32[32,1024]{1,0:T(8,128)S(1)}, f32[32,1024]{1,0:T(8,128)S(1)}, u32[]{:S(2)}, u32[]{:S(2)}) collective-permute-start(f32[32,1024]{1,0:T(8,128)S(1)} %get-tuple-element.328.refs_5_.refs_1_), channel_id=1, source_target_pairs={{0,4},{4,0},{1,5},{5,1},{2,6},{6,2},{3,7},{7,3},{8,12},{12,8},{9,1... | collective-permute-start | bytes 393224 | tf_op jit(solution)/shard_map/cond/branch_1_fun/ppermute | solution.py:37
  255.1 9.7 %collective-permute-start.28 = (f32[16,1664]{1,0:T(8,128)S(1)}, f32[16,1664]{1,0:T(8,128)S(1)}, u32[]{:S(2)}, u32[]{:S(2)}) collective-permute-start(f32[16,1664]{1,0:T(8,128)S(1)} %branch_1_fun.67.refs_3_.refs_1_), channel_id=1, source_target_pairs={{0,16},{16,0},{8,24},{24,8},{1,17},{17,1},{9,25},{25,9},{2,18},{18... | collective-permute-start | bytes 319496 | tf_op jit(solution)/shard_map/cond/branch_1_fun/ppermute | solution.py:37
  265.4 12.1 %collective-permute-start.29 = (f32[32,1664]{1,0:T(8,128)S(1)}, f32[32,1664]{1,0:T(8,128)S(1)}, u32[]{:S(2)}, u32[]{:S(2)}) collective-permute-start(f32[32,1664]{1,0:T(8,128)S(1)} %branch_1_fun.69.refs_1_.refs_3_), channel_id=1, source_target_pairs={{0,8},{8,0},{16,24},{24,16},{1,9},{9,1},{17,25},{25,17},{2,10},{10... | collective-permute-start | bytes 638984 | tf_op jit(solution)/shard_map/cond/branch_1_fun/ppermute | solution.py:37
  286.0 9.7 %collective-permute-start.32 = (f32[64,1664]{1,0:T(8,128)S(1)}, f32[64,1664]{1,0:T(8,128)S(1)}, u32[]{:S(2)}, u32[]{:S(2)}) collective-permute-start(f32[64,1664]{1,0:T(8,128)S(1)} %get-tuple-element.187.refs_1_.refs_5_), channel_id=1, source_target_pairs={{0,2},{2,0},{1,3},{3,1},{4,6},{6,4},{5,7},{7,5},{8,10},{10,8},{9,1... | collective-permute-start | bytes 1277960 | tf_op jit(solution)/shard_map/cond/branch_1_fun/ppermute | solution.py:37
  286.8 9.3 %collective-permute-start.33 = (f32[64,1664]{1,0:T(8,128)S(1)}, f32[64,1664]{1,0:T(8,128)S(1)}, u32[]{:S(2)}, u32[]{:S(2)}) collective-permute-start(f32[64,1664]{1,0:T(8,128)S(1)} %get-tuple-element.188.refs_3_), channel_id=1, source_target_pairs={{0,4},{4,0},{1,5},{5,1},{2,6},{6,2},{3,7},{7,3},{8,12},{12,8},{9,1... | collective-permute-start | bytes 1277960 | tf_op jit(solution)/shard_map/cond/branch_1_fun/ppermute | solution.py:37
  (97 other events, 828.4 us)
Sparse Core Ops, SparseCore 0:
  99.1 198.4 all-reduce.2

commit v6 on v5

--- a/solution.py
+++ b/solution.py
@@ -23,6 +23,9 @@
         "z1": ("z", [(0, 1), (1, 0), (2, 3), (3, 2)]),
         "z2": ("z", [(0, 2), (2, 0), (1, 3), (3, 1)]),
     }
+
+    def late_rows(self, width):
+        return width // 2
 
     def position(self):
         return lax.axis_index("z") * 2 + lax.axis_index("y")
@@ -110,11 +113,13 @@
             [SMEM] + [full(a.shape)] * 4, [(full((rows, wide)), (rows, wide), F32)],
             nbytes=8 * rows * wide,
         )(bits, a, got_a, b, got_b, after=after)[0]
+        yield part
+
+    def close(self, part, bits, shapes, after=()):
         got = self.swap(part, "c")
-        after = yield part
-        yield call(
-            last_join_kernel, 1, [SMEM] + [full((rows, wide))] * 2,
-            [(full(s), s, F32) for s in shapes], nbytes=16 * rows * wide,
+        return call(
+            last_join_kernel, 1, [SMEM] + [full(part.shape)] * 2,
+            [(full(s), s, F32) for s in shapes], nbytes=16 * part.size,
         )(bits, part, got, after=after)
 
     def join(self, ways, bits, parts, after):
@@ -132,6 +137,9 @@
     rows = P("batch", "seq", None)
     lens = P("batch")
 
+    def late_rows(self, width):
+        return width
+
     def position(self):
         return lax.axis_index("seq")
 
@@ -156,16 +164,17 @@
         yield out[0], out[1]
 
     def sums(self, give, keep, bits, shapes):
-        for _ in range(11):
+        for _ in range(10):
             yield give
-        part = lax.psum(jnp.concatenate([keep(), give], axis=0), self.axes)
+        yield jnp.concatenate([keep(), give], axis=0)
+
+    def close(self, part, bits, shapes, after=()):
+        part = lax.psum(part, self.axes)
         outs, at = [], 0
         for shape in shapes:
             outs.append(part[:, at : at + shape[1]])
             at += shape[1]
-        yield outs
-
-
+        return outs
 LANES = 128
 BF = jnp.bfloat16
 F32 = jnp.float32
@@ -728,8 +737,8 @@
 )
 BACK = (
     "p", "q", "Ge", "e", "I0a", "Ke", "p", "q", "e", "I0b", "I1a", "p", "q", "e", "I1b", "e",
-    "L0", "q", "e", "L1", "Gk", "k", "Kk", "e", "k", "e", "k", "e", "k", "e", "k", "e", "k", "Fe",
-    "k", "k", "k", "k", "Fk",
+    "L0", "q", "e", "L1", "Gk", "k", "Kk", "e", "k", "e", "k", "e", "k", "e", "k", "k", "Fe", "k",
+    "k", "k", "Fk",
 )
 
 
@@ -896,8 +905,7 @@
             elif kind == "K":
                 token = kept[name] = weights(name, False, after)
             elif kind == "F":
-                ends[name] = flows[name].send(after)
-                token = ends[name][0]
+                token = ends[name] = flows[name].send(after)
             else:
                 token = flows[name].send(after)
         return token
@@ -908,15 +916,17 @@
 
     def rest():
         play(BACK, parts[1])
-        qkv_grad, small = ends["k"]
-        return *ends["e"], qkv_grad, small[:, :16].T, lasts[seqs - 1][0]
+        up_end, outw_grad = comm.close(ends["e"], bits, shapes["e"])
+        return up_end, outw_grad, ends["k"], lasts[seqs - 1][0]
 
     def nothing():
-        shaped = [(width, 512), (width, width), (width, 3 * width), (16, width)]
+        shaped = [(width, 512), (width, width), (comm.late_rows(width), 3 * width + LANES)]
         return *(jnp.zeros(s, F32) for s in shaped), cotangent.astype(F32)
 
-    up_end, outw_grad, qkv_grad, small, grad = lax.cond(jnp.max(lengths) > 0, rest, nothing)
+    up_end, outw_grad, late, grad = lax.cond(jnp.max(lengths) > 0, rest, nothing)
     up_grad = jnp.concatenate([up_grad, up_end], axis=1)
+    qkv_grad, small = comm.close(late, bits, shapes["k"], after=(up_grad,))
+    small = small[:, :16].T
     out = mids[seqs - 1][0]
     return (
         out,

time: 325 us -> 313 us (0.963)
  waiting for transfers between devices: 118 us -> 109 us
  local copies, waits for them, and re-layouts: 7.11 us -> 15.6 us
  Pallas kernels: 121 us -> 114 us
  other arithmetic: 7.9 us -> 1.4 us
    ppermute x36, waiting for transfers between devices: 95.3 us -> 85.2 us  [swap(): return lax.ppermute(part, name, pairs)]
    pallas_call x55, Pallas kernels: 121 us -> 114 us  [run(): pl.pallas_call(waiting, grid_spec=pltpu.PrefetchScalarGridSpec(num_scalar...]
    unnamed x78 -> x79, local copies, waits for them, and re-layouts: 6.11 us -> 10.8 us
    concatenate x1 -> x0, other arithmetic: 4.43 us -> none  [body(): up_grad = jnp.concatenate([up_grad, up_end], axis=1)]
    cond x68, local copies, waits for them, and re-layouts: 0.14 us -> 3.44 us
  transfers between devices with their start and end apart: 49 -> 49, of which waited for: 27 -> 26; matrix products, arithmetic and copies ran while one was open for 1% -> 1% of each run, Pallas kernels for 33% -> 32%
where the time goes in v6:
time: 313 us; the launch traced here: 307 us
  Pallas kernels  114 us (36%)
  waiting for transfers between devices  109 us (35%)
  starting transfers between devices  51 us (16%)
  local copies, waits for them, and re-layouts  15.6 us (5%)
  between operations  15.6 us (5%)
    pallas_call x55, Pallas kernels, run(): pl.pallas_call(waiting, grid_spec=pltpu.PrefetchScalarGridSpec(num_scalar...  114 us
    ppermute x36, waiting for transfers between devices, swap(): return lax.ppermute(part, name, pairs)  85.2 us
    ppermute x36, starting transfers between devices, swap(): return lax.ppermute(part, name, pairs)  35.1 us
    ppermute x12, waiting for transfers between devices, carry(): arrived.append(lax.ppermute(out, 'z', [hop]))  22.7 us
    ppermute x12, starting transfers between devices, carry(): arrived.append(lax.ppermute(out, 'z', [hop]))  15.8 us
    unnamed x79, local copies, waits for them, and re-layouts  10.8 us
  transfers between devices with their start and end apart: 49, of which 26 were waited for; matrix products, arithmetic and copies ran while one was open for 1% of the time, Pallas kernels for 32%

profile of v6, /device:TPU:0, one launch (start us, length us, event | category | flops | bytes accessed | tf_op | source)
XLA Modules:
  0.0 307.4 jit_solution(6610201624839429508)
XLA Ops:
  10.1 6.8 %shard_map.198 = (bf16[512,512]{1,0:T(8,128)(2,1)S(1)}, bf16[512,512]{1,0:T(8,128)(2,1)}, bf16[512,512]{1,0:T(8,128)(2,1)S(1)}, bf16[512,2048]{1,0:T(8,128)(2,1)...) custom-call(s32[3]{0:T(128)S(1)} %pad_add_fusion.refs_0_, s32[5]{0:T(128)S(1)} %stack.23.refs_1_.refs_0_, ...), custom_call_target="tpu_custom_call" | custom-call | flops 1536000000 | bytes 8388608 | tf_op jit(solution)/shard_map/pallas_call | solution.py:657
  19.9 6.2 %shard_map.199 = (bf16[512,512]{1,0:T(8,128)(2,1)S(1)}, bf16[512,512]{1,0:T(8,128)(2,1)}, bf16[512,512]{1,0:T(8,128)(2,1)S(1)}, bf16[512,2048]{1,0:T(8,128)(2,1)...) custom-call(s32[3]{0:T(128)S(1)} %pad_add_fusion.refs_0_, s32[5]{0:T(128)S(1)} %stack.23.refs_1_.refs_0_, ...), custom_call_target="tpu_custom_call" | custom-call | flops 1536000000 | bytes 8388608 | tf_op jit(solution)/shard_map/pallas_call | solution.py:657
  61.1 13.0 %shard_map.212 = (bf16[2,512,512]{2,1,0:T(8,128)(2,1)}, f32[512,512]{1,0:T(8,128)}, bf16[512,1024]{1,0:T(8,128)(2,1)}, bf16[512,512]{1,0:T(8,128)(2,1)}, bf16[51...) custom-call(s32[3]{0:T(128)S(1)} %pad_add_fusion.refs_0_, ...), custom_call_target="tpu_custom_call" | custom-call | flops 5632000000 | bytes 25165824 | tf_op jit(solution)/shard_map/pallas_call | solution.py:657
  76.7 13.2 %shard_map.213 = (bf16[2,512,512]{2,1,0:T(8,128)(2,1)}, f32[512,512]{1,0:T(8,128)}, bf16[512,1024]{1,0:T(8,128)(2,1)}, bf16[512,512]{1,0:T(8,128)(2,1)}, bf16[51...) custom-call(s32[3]{0:T(128)S(1)} %pad_add_fusion.refs_0_, ...), custom_call_target="tpu_custom_call", output_to_operand_aliasing={{0}: (13, {})} | custom-call | flops 5632000000 | bytes 25165824 | tf_op jit(solution)/shard_map/pallas_call | solution.py:657
  90.0 7.0 %shard_map.215 = (f32[2048,512]{1,0:T(8,128)S(1)}, f32[512,1536]{1,0:T(8,128)}) custom-call(bf16[512,2048]{1,0:T(8,128)(2,1)S(1)} %get-tuple-element.266.refs_0_, bf16[512,2048]{1,0:T(8,128)(2,1)S(1)} %get-tuple-element.267.refs_1_, bf16[512,512]{1,0:T(8,128)(2,1)S(1)} %get-tuple-element.268.refs_2_, bf16[512,512]{1,0:T(8,128)(2,1)S(1)} %get-tuple-element.269.refs_3_, ...), custom_call_target="tpu_custom_call" | custom-call | flops 4294967296 | bytes 16777216 | tf_op jit(solution)/shard_map/pallas_call | solution.py:657
  101.1 5.4 %collective-permute-done.46 = f32[4,72,256]{2,1,0:T(8,128)S(1)} collective-permute-done((f32[4,72,256]{2,1,0:T(8,128)S(1)}, f32[4,72,256]{2,1,0:T(8,128)S(1)}, u32[]{:S(2)}, u32[]{:S(2)}) %collective-permute-start.46) | collective-permute-done | bytes 294944 | tf_op jit(solution)/shard_map/ppermute | solution.py:40
  106.5 182.0 %conditional.1 = (f32[512,512]{1,0:T(8,128)S(1)}, f32[512,512]{1,0:T(8,128)S(1)}, f32[256,1664]{1,0:T(8,128)S(1)}, f32[2,512,512]{2,1,0:T(8,128)}) conditional(s32[]{:T(128)} %convert_element_type.6, bf16[2,512,512]{2,1,0:T(8,128)(2,1)} %refs_3_.3, (f32[4,72,256]{2,1,0:T(8,128)S(1)}, f32[4,72,256]{2,1,0:T(8,128)S(1)}, f32[512,1536]{1,0:T(8,128)}, ...), branch_computations={%region_1.2_spmd, %region_2.3_spmd} | conditional | flops 29309859840 | bytes 265496704 | solution.py:926
  114.6 4.9 %branch_1_fun.39 = (bf16[512,512]{1,0:T(8,128)(2,1)S(1)}, f32[512,512]{1,0:T(8,128)S(1)}, f32[512,512]{1,0:T(8,128)S(1)}) custom-call(s32[5]{0:T(128)S(1)} %get-tuple-element.85.refs_0_, bf16[512,512]{1,0:T(8,128)(2,1)S(1)} %copy-done.53, bf16[512,512]{1,0:T(8,128)(2,1)S(1)} %copy-done.46, bf16[512,512]{1,0:T(8,128)(2,1)S(1)} %copy-done.48, ...), custom_call_target="tpu_custom_call" | custom-call | flops 5120000000 | bytes 6291456 | tf_op jit(solution)/shard_map/cond/branch_1_fun/pallas_call | solution.py:657
  125.2 4.7 %branch_1_fun.44 = (bf16[512,512]{1,0:T(8,128)(2,1)S(1)}, f32[512,512]{1,0:T(8,128)S(1)}, f32[512,512]{1,0:T(8,128)S(1)}) custom-call(s32[5]{0:T(128)S(1)} %get-tuple-element.85.refs_0_, bf16[512,512]{1,0:T(8,128)(2,1)S(1)} %copy-done.53, bf16[512,512]{1,0:T(8,128)(2,1)S(1)} %copy-done.46, ...), custom_call_target="tpu_custom_call", output_to_operand_aliasing={{0}: (10, {}), {1}: (11, {}), {2}: (12, {})} | custom-call | flops 5120000000 | bytes 6291456 | tf_op jit(solution)/shard_map/cond/branch_1_fun/pallas_call | solution.py:657
  130.0 4.7 %branch_1_fun.45 = (bf16[512,512]{1,0:T(8,128)(2,1)S(1)}, f32[512,512]{1,0:T(8,128)S(1)}, f32[512,512]{1,0:T(8,128)S(1)}) custom-call(s32[5]{0:T(128)S(1)} %get-tuple-element.85.refs_0_, bf16[512,512]{1,0:T(8,128)(2,1)S(1)} %copy-done.55, bf16[512,512]{1,0:T(8,128)(2,1)S(1)} %copy-done.49, bf16[512,512]{1,0:T(8,128)(2,1)S(1)} %copy-done.51, ...), custom_call_target="tpu_custom_call" | custom-call | flops 5120000000 | bytes 6291456 | tf_op jit(solution)/shard_map/cond/branch_1_fun/pallas_call | solution.py:657
  134.7 20.7 %collective-permute-done.6.refs_5_ = f32[4,72,256]{2,1,0:T(8,128)S(1)} collective-permute-done((f32[4,72,256]{2,1,0:T(8,128)S(1)}, f32[4,72,256]{2,1,0:T(8,128)S(1)}, u32[]{:S(2)}, u32[]{:S(2)}) %collective-permute-start.6) | collective-permute-done | bytes 294944 | tf_op jit(solution)/shard_map/cond/branch_1_fun/ppermute | solution.py:53
  161.8 4.9 %branch_1_fun.49 = (bf16[512,512]{1,0:T(8,128)(2,1)S(1)}, f32[512,512]{1,0:T(8,128)S(1)}, f32[512,512]{1,0:T(8,128)S(1)}) custom-call(s32[5]{0:T(128)S(1)} %get-tuple-element.85.refs_0_, bf16[512,512]{1,0:T(8,128)(2,1)S(1)} %copy-done.55, bf16[512,512]{1,0:T(8,128)(2,1)S(1)} %copy-done.49, ...), custom_call_target="tpu_custom_call", output_to_operand_aliasing={{0}: (10, {}), {1}: (11, {}), {2}: (12, {})} | custom-call | flops 5120000000 | bytes 6291456 | tf_op jit(solution)/shard_map/cond/branch_1_fun/pallas_call | solution.py:657
  169.9 6.3 %branch_1_fun.51 = (f32[2,512,512]{2,1,0:T(8,128)S(1)}, bf16[512,512]{1,0:T(8,128)(2,1)S(1)}, bf16[512,512]{1,0:T(8,128)(2,1)S(1)}, f32[8,512]{1,0:T(8,128)S(1)}) custom-call(s32[5]{0:T(128)S(1)} %get-tuple-element.85.refs_0_, bf16[2,512,512]{2,1,0:T(8,128)(2,1)S(1)} %copy-done.17, f32[512,512]{1,0:T(8,128)S(1)} %copy-done.43, ...), custom_call_target="tpu_custom_call" | custom-call | flops 3072000000 | bytes 11534336 | tf_op jit(solution)/shard_map/cond/branch_1_fun/pallas_call | solution.py:657
  183.7 6.3 %branch_1_fun.54 = (f32[2,512,512]{2,1,0:T(8,128)S(1)}, bf16[512,512]{1,0:T(8,128)(2,1)S(1)}, bf16[512,512]{1,0:T(8,128)(2,1)S(1)}, f32[8,512]{1,0:T(8,128)S(1)}) custom-call(s32[5]{0:T(128)S(1)} %get-tuple-element.85.refs_0_, bf16[2,512,512]{2,1,0:T(8,128)(2,1)S(1)} %copy-done.17, f32[512,512]{1,0:T(8,128)S(1)} %copy-done.44, ...), custom_call_target="tpu_custom_call", output_to_operand_aliasing={{0}: (16, {})} | custom-call | flops 3072000000 | bytes 11534336 | tf_op jit(solution)/shard_map/cond/branch_1_fun/pallas_call | solution.py:657
  191.6 4.5 %collective-permute-start.12 = (f32[16,1024]{1,0:T(8,128)S(1)}, f32[16,1024]{1,0:T(8,128)S(1)}, u32[]{:S(2)}, u32[]{:S(2)}) collective-permute-start(f32[16,1024]{1,0:T(8,128)S(1)} %get-tuple-element.147.refs_17_), channel_id=1, source_target_pairs={{0,16},{16,0},{8,24},{24,8},{1,17},{17,1},{9,25},{25,9},{2,18},{18... | collective-permute-start | bytes 196616 | tf_op jit(solution)/shard_map/cond/branch_1_fun/ppermute | solution.py:40
  203.4 4.1 %collective-permute-done.14.refs_2_ = f32[16,1024]{1,0:T(8,128)S(1)} collective-permute-done((f32[16,1024]{1,0:T(8,128)S(1)}, f32[16,1024]{1,0:T(8,128)S(1)}, u32[]{:S(2)}, u32[]{:S(2)}) %collective-permute-start.14) | collective-permute-done | bytes 65568 | tf_op jit(solution)/shard_map/cond/branch_1_fun/ppermute | solution.py:40
  208.2 6.8 %collective-permute-done.18.refs_4_ = f32[64,1664]{1,0:T(8,128)S(1)} collective-permute-done((f32[64,1664]{1,0:T(8,128)S(1)}, f32[64,1664]{1,0:T(8,128)S(1)}, u32[]{:S(2)}, u32[]{:S(2)}) %collective-permute-start.18) | collective-permute-done | bytes 426016 | tf_op jit(solution)/shard_map/cond/branch_1_fun/ppermute | solution.py:40
  217.9 4.3 %collective-permute-done.22.refs_4_ = f32[32,1664]{1,0:T(8,128)S(1)} collective-permute-done((f32[32,1664]{1,0:T(8,128)S(1)}, f32[32,1664]{1,0:T(8,128)S(1)}, u32[]{:S(2)}, u32[]{:S(2)}) %collective-permute-start.22) | collective-permute-done | bytes 213024 | tf_op jit(solution)/shard_map/cond/branch_1_fun/ppermute | solution.py:40
  225.7 5.1 %collective-permute-done.20.refs_4_ = f32[32,1024]{1,0:T(8,128)S(1)} collective-permute-done((f32[32,1024]{1,0:T(8,128)S(1)}, f32[32,1024]{1,0:T(8,128)S(1)}, u32[]{:S(2)}, u32[]{:S(2)}) %collective-permute-start.20) | collective-permute-done | bytes 131104 | tf_op jit(solution)/shard_map/cond/branch_1_fun/ppermute | solution.py:40
  236.2 10.2 %collective-permute-done.26.refs_1_ = f32[16,1664]{1,0:T(8,128)S(1)} collective-permute-done((f32[16,1664]{1,0:T(8,128)S(1)}, f32[16,1664]{1,0:T(8,128)S(1)}, u32[]{:S(2)}, u32[]{:S(2)}) %collective-permute-start.26) | collective-permute-done | bytes 106528 | tf_op jit(solution)/shard_map/cond/branch_1_fun/ppermute | solution.py:40
  247.2 5.2 %collective-permute-done.28.refs_2_ = f32[16,1664]{1,0:T(8,128)S(1)} collective-permute-done((f32[16,1664]{1,0:T(8,128)S(1)}, f32[16,1664]{1,0:T(8,128)S(1)}, u32[]{:S(2)}, u32[]{:S(2)}) %collective-permute-start.28) | collective-permute-done | bytes 106528 | tf_op jit(solution)/shard_map/cond/branch_1_fun/ppermute | solution.py:40
  253.1 10.3 %collective-permute-done.29.refs_2_ = f32[32,1664]{1,0:T(8,128)S(1)} collective-permute-done((f32[32,1664]{1,0:T(8,128)S(1)}, f32[32,1664]{1,0:T(8,128)S(1)}, u32[]{:S(2)}, u32[]{:S(2)}) %collective-permute-start.29) | collective-permute-done | bytes 213024 | tf_op jit(solution)/shard_map/cond/branch_1_fun/ppermute | solution.py:40
  266.2 10.2 %collective-permute-done.31.refs_4_ = f32[32,1664]{1,0:T(8,128)S(1)} collective-permute-done((f32[32,1664]{1,0:T(8,128)S(1)}, f32[32,1664]{1,0:T(8,128)S(1)}, u32[]{:S(2)}, u32[]{:S(2)}) %collective-permute-start.31) | collective-permute-done | bytes 213024 | tf_op jit(solution)/shard_map/cond/branch_1_fun/ppermute | solution.py:40
  279.3 6.8 %collective-permute-done.32.refs_2_ = f32[64,1664]{1,0:T(8,128)S(1)} collective-permute-done((f32[64,1664]{1,0:T(8,128)S(1)}, f32[64,1664]{1,0:T(8,128)S(1)}, u32[]{:S(2)}, u32[]{:S(2)}) %collective-permute-start.32) | collective-permute-done | bytes 426016 | tf_op jit(solution)/shard_map/cond/branch_1_fun/ppermute | solution.py:40
  (286 shorter events, 119.0 us)
Async XLA Ops:
  7.2 284.1 %all-reduce.3.cloned.1.call-start = ((), (), s32[]{:S(2)}) async-start(), calls=%async_computation | async-start | bytes 14680064 | tf_op jit(solution)/shard_map/psum | solution.py:43
  16.9 10.0 %collective-permute-start.35 = (f32[4,72,256]{2,1,0:T(8,128)S(1)}, f32[4,72,256]{2,1,0:T(8,128)S(1)}, u32[]{:S(2)}, u32[]{:S(2)}) collective-permute-start(f32[4,72,256]{2,1,0:T(8,128)S(1)} %get-tuple-element.243.refs_8_), channel_id=1, source_target_pairs={{0,4},{4,0},{1,5},{5,1},{2,6},{6,2},{3,7},{7,3},{8,12},{12,8},{9,1... | collective-permute-start | bytes 884744 | tf_op jit(solution)/shard_map/ppermute | solution.py:40
  58.8 17.8 %collective-permute-start.42 = (f32[4,72,256]{2,1,0:T(8,128)S(1)}, f32[4,72,256]{2,1,0:T(8,128)S(1)}, u32[]{:S(2)}, u32[]{:S(2)}) collective-permute-start(f32[4,72,256]{2,1,0:T(8,128)S(1)} %get-tuple-element.259.refs_13_), channel_id=1, source_target_pairs={{0,4},{4,0},{1,5},{5,1},{2,6},{6,2},{3,7},{7,3},{8,12},{12,8},{9,1... | collective-permute-start | bytes 884744 | tf_op jit(solution)/shard_map/ppermute | solution.py:40
  74.1 15.8 %collective-permute-start.44 = (f32[4,72,256]{2,1,0:T(8,128)S(1)}, f32[4,72,256]{2,1,0:T(8,128)S(1)}, u32[]{:S(2)}, u32[]{:S(2)}) collective-permute-start(f32[4,72,256]{2,1,0:T(8,128)S(1)} %get-tuple-element.262.refs_14_), channel_id=1, source_target_pairs={{0,4},{4,0},{1,5},{5,1},{2,6},{6,2},{3,7},{7,3},{8,12},{12,8},{9,1... | collective-permute-start | bytes 884744 | tf_op jit(solution)/shard_map/ppermute | solution.py:40
  113.0 9.9 %collective-permute-start = (f32[256,1024]{1,0:T(8,128)S(1)}, f32[256,1024]{1,0:T(8,128)S(1)}, u32[]{:S(2)}, u32[]{:S(2)}) collective-permute-start(f32[256,1024]{1,0:T(8,128)S(1)} %branch_1_fun.38.refs_10_), channel_id=1, source_target_pairs={{0,1},{1,0},{2,3},{3,2},{4,5},{5,4},{6,7},{7,6},{8,9},{9,8},{10,11... | collective-permute-start | bytes 3145736 | tf_op jit(solution)/shard_map/cond/branch_1_fun/ppermute | solution.py:40
  113.1 9.1 %collective-permute-start.1 = (f32[4,72,256]{2,1,0:T(8,128)S(1)}, f32[4,72,256]{2,1,0:T(8,128)S(1)}, u32[]{:S(2)}, u32[]{:S(2)}) collective-permute-start(f32[4,72,256]{2,1,0:T(8,128)S(1)} %branch_1_fun.37.refs_9_.refs_0_), channel_id=1, source_target_pairs={{24,16},{25,17},{26,18},{27,19},{28,20},{29,21},{30,22},{31,23}} | collective-permute-start | bytes 884744 | tf_op jit(solution)/shard_map/cond/branch_1_fun/ppermute | solution.py:53
  120.9 34.6 %collective-permute-start.6 = (f32[4,72,256]{2,1,0:T(8,128)S(1)}, f32[4,72,256]{2,1,0:T(8,128)S(1)}, u32[]{:S(2)}, u32[]{:S(2)}) collective-permute-start(f32[4,72,256]{2,1,0:T(8,128)S(1)} %branch_1_fun.41.refs_2_), channel_id=1, source_target_pairs={{8,0},{9,1},{10,2},{11,3},{12,4},{13,5},{14,6},{15,7}} | collective-permute-start | bytes 884744 | tf_op jit(solution)/shard_map/cond/branch_1_fun/ppermute | solution.py:53
  122.2 33.9 %collective-permute-start.5 = (f32[4,72,256]{2,1,0:T(8,128)S(1)}, f32[4,72,256]{2,1,0:T(8,128)S(1)}, u32[]{:S(2)}, u32[]{:S(2)}) collective-permute-start(f32[4,72,256]{2,1,0:T(8,128)S(1)} %branch_1_fun.42.refs_3_), channel_id=1, source_target_pairs={{16,8},{17,9},{18,10},{19,11},{20,12},{21,13},{22,14},{23,15}} | collective-permute-start | bytes 884744 | tf_op jit(solution)/shard_map/cond/branch_1_fun/ppermute | solution.py:53
  123.6 33.9 %collective-permute-start.4 = (f32[64,1024]{1,0:T(8,128)S(1)}, f32[64,1024]{1,0:T(8,128)S(1)}, u32[]{:S(2)}, u32[]{:S(2)}) collective-permute-start(f32[64,1024]{1,0:T(8,128)S(1)} %get-tuple-element.112), channel_id=1, source_target_pairs={{0,4},{4,0},{1,5},{5,1},{2,6},{6,2},{3,7},{7,3},{8,12},{12,8},{9,1... | collective-permute-start | bytes 786440 | tf_op jit(solution)/shard_map/cond/branch_1_fun/ppermute | solution.py:40
  123.7 33.9 %collective-permute-start.3 = (f32[64,1024]{1,0:T(8,128)S(1)}, f32[64,1024]{1,0:T(8,128)S(1)}, u32[]{:S(2)}, u32[]{:S(2)}) collective-permute-start(f32[64,1024]{1,0:T(8,128)S(1)} %get-tuple-element.110.refs_13_), channel_id=1, source_target_pairs={{0,2},{2,0},{1,3},{3,1},{4,6},{6,4},{5,7},{7,5},{8,10},{10,8},{9,1... | collective-permute-start | bytes 786440 | tf_op jit(solution)/shard_map/cond/branch_1_fun/ppermute | solution.py:40
  156.1 13.8 %collective-permute-start.11 = (f32[4,72,256]{2,1,0:T(8,128)S(1)}, f32[4,72,256]{2,1,0:T(8,128)S(1)}, u32[]{:S(2)}, u32[]{:S(2)}) collective-permute-start(f32[4,72,256]{2,1,0:T(8,128)S(1)} %get-tuple-element.127.refs_2_), channel_id=1, source_target_pairs={{0,4},{4,0},{1,5},{5,1},{2,6},{6,2},{3,7},{7,3},{8,12},{12,8},{9,1... | collective-permute-start | bytes 884744 | tf_op jit(solution)/shard_map/cond/branch_1_fun/ppermute | solution.py:40
  156.2 20.0 %collective-permute-start.10 = (f32[4,72,256]{2,1,0:T(8,128)S(1)}, f32[4,72,256]{2,1,0:T(8,128)S(1)}, u32[]{:S(2)}, u32[]{:S(2)}) collective-permute-start(f32[4,72,256]{2,1,0:T(8,128)S(1)} %branch_1_fun.47.refs_5_), channel_id=1, source_target_pairs={{8,0},{9,1},{10,2},{11,3},{12,4},{13,5},{14,6},{15,7}} | collective-permute-start | bytes 884744 | tf_op jit(solution)/shard_map/cond/branch_1_fun/ppermute | solution.py:53
  159.8 9.5 %collective-permute-start.7 = (f32[32,1024]{1,0:T(8,128)S(1)}, f32[32,1024]{1,0:T(8,128)S(1)}, u32[]{:S(2)}, u32[]{:S(2)}) collective-permute-start(f32[32,1024]{1,0:T(8,128)S(1)} %get-tuple-element.129.refs_13_), channel_id=1, source_target_pairs={{0,4},{4,0},{1,5},{5,1},{2,6},{6,2},{3,7},{7,3},{8,12},{12,8},{9,1... | collective-permute-start | bytes 393224 | tf_op jit(solution)/shard_map/cond/branch_1_fun/ppermute | solution.py:40
  200.6 14.3 %collective-permute-start.18 = (f32[64,1664]{1,0:T(8,128)S(1)}, f32[64,1664]{1,0:T(8,128)S(1)}, u32[]{:S(2)}, u32[]{:S(2)}) collective-permute-start(f32[64,1664]{1,0:T(8,128)S(1)} %get-tuple-element.166), channel_id=1, source_target_pairs={{0,4},{4,0},{1,5},{5,1},{2,6},{6,2},{3,7},{7,3},{8,12},{12,8},{9,1... | collective-permute-start | bytes 1277960 | tf_op jit(solution)/shard_map/cond/branch_1_fun/ppermute | solution.py:40
  201.8 13.2 %collective-permute-start.17 = (f32[64,1664]{1,0:T(8,128)S(1)}, f32[64,1664]{1,0:T(8,128)S(1)}, u32[]{:S(2)}, u32[]{:S(2)}) collective-permute-start(f32[64,1664]{1,0:T(8,128)S(1)} %get-tuple-element.163.refs_3_), channel_id=1, source_target_pairs={{0,2},{2,0},{1,3},{3,1},{4,6},{6,4},{5,7},{7,5},{8,10},{10,8},{9,1... | collective-permute-start | bytes 1277960 | tf_op jit(solution)/shard_map/cond/branch_1_fun/ppermute | solution.py:40
  208.1 9.2 %collective-permute-start.16 = (f32[32,1024]{1,0:T(8,128)S(1)}, f32[32,1024]{1,0:T(8,128)S(1)}, u32[]{:S(2)}, u32[]{:S(2)}) collective-permute-start(f32[32,1024]{1,0:T(8,128)S(1)} %branch_1_fun.59.refs_5_.refs_1_), channel_id=1, source_target_pairs={{0,8},{8,0},{16,24},{24,16},{1,9},{9,1},{17,25},{25,17},{2,10},{10... | collective-permute-start | bytes 393224 | tf_op jit(solution)/shard_map/cond/branch_1_fun/ppermute | solution.py:40
  222.9 12.5 %collective-permute-start.25 = (f32[32,1664]{1,0:T(8,128)S(1)}, f32[32,1664]{1,0:T(8,128)S(1)}, u32[]{:S(2)}, u32[]{:S(2)}) collective-permute-start(f32[32,1664]{1,0:T(8,128)S(1)} %get-tuple-element.171.refs_5_), channel_id=1, source_target_pairs={{0,8},{8,0},{16,24},{24,16},{1,9},{9,1},{17,25},{25,17},{2,10},{10... | collective-permute-start | bytes 638984 | tf_op jit(solution)/shard_map/cond/branch_1_fun/ppermute | solution.py:40
  233.5 13.0 %collective-permute-start.24 = (f32[64,1024]{1,0:T(8,128)S(1)}, f32[64,1024]{1,0:T(8,128)S(1)}, u32[]{:S(2)}, u32[]{:S(2)}) collective-permute-start(f32[64,1024]{1,0:T(8,128)S(1)} %get-tuple-element.173.refs_3_), channel_id=1, source_target_pairs={{0,4},{4,0},{1,5},{5,1},{2,6},{6,2},{3,7},{7,3},{8,12},{12,8},{9,1... | collective-permute-start | bytes 786440 | tf_op jit(solution)/shard_map/cond/branch_1_fun/ppermute | solution.py:40
  234.4 12.1 %collective-permute-start.23 = (f32[64,1024]{1,0:T(8,128)S(1)}, f32[64,1024]{1,0:T(8,128)S(1)}, u32[]{:S(2)}, u32[]{:S(2)}) collective-permute-start(f32[64,1024]{1,0:T(8,128)S(1)} %get-tuple-element.172.refs_3_.refs_1_), channel_id=1, source_target_pairs={{0,2},{2,0},{1,3},{3,1},{4,6},{6,4},{5,7},{7,5},{8,10},{10,8},{9,1... | collective-permute-start | bytes 786440 | tf_op jit(solution)/shard_map/cond/branch_1_fun/ppermute | solution.py:40
  235.9 10.5 %collective-permute-start.26 = (f32[16,1664]{1,0:T(8,128)S(1)}, f32[16,1664]{1,0:T(8,128)S(1)}, u32[]{:S(2)}, u32[]{:S(2)}) collective-permute-start(f32[16,1664]{1,0:T(8,128)S(1)} %get-tuple-element.176.refs_2_), channel_id=1, source_target_pairs={{0,16},{16,0},{8,24},{24,8},{1,17},{17,1},{9,25},{25,9},{2,18},{18... | collective-permute-start | bytes 319496 | tf_op jit(solution)/shard_map/cond/branch_1_fun/ppermute | solution.py:40
  253.0 10.4 %collective-permute-start.29 = (f32[32,1664]{1,0:T(8,128)S(1)}, f32[32,1664]{1,0:T(8,128)S(1)}, u32[]{:S(2)}, u32[]{:S(2)}) collective-permute-start(f32[32,1664]{1,0:T(8,128)S(1)} %branch_1_fun.68.refs_1_.refs_3_), channel_id=1, source_target_pairs={{0,8},{8,0},{16,24},{24,16},{1,9},{9,1},{17,25},{25,17},{2,10},{10... | collective-permute-start | bytes 638984 | tf_op jit(solution)/shard_map/cond/branch_1_fun/ppermute | solution.py:40
  253.0 34.5 %collective-permute-start.27 = (f32[256,1024]{1,0:T(8,128)S(1)}, f32[256,1024]{1,0:T(8,128)S(1)}, u32[]{:S(2)}, u32[]{:S(2)}) collective-permute-start(f32[256,1024]{1,0:T(8,128)S(1)} %branch_1_fun.66.refs_1_.refs_3_), channel_id=1, source_target_pairs={{0,1},{1,0},{2,3},{3,2},{4,5},{5,4},{6,7},{7,6},{8,9},{9,8},{10,11... | collective-permute-start | bytes 3145736 | tf_op jit(solution)/shard_map/cond/branch_1_fun/ppermute | solution.py:40
  264.0 12.3 %collective-permute-start.31 = (f32[32,1664]{1,0:T(8,128)S(1)}, f32[32,1664]{1,0:T(8,128)S(1)}, u32[]{:S(2)}, u32[]{:S(2)}) collective-permute-start(f32[32,1664]{1,0:T(8,128)S(1)} %get-tuple-element.301.refs_3_), channel_id=1, source_target_pairs={{0,2},{2,0},{1,3},{3,1},{4,6},{6,4},{5,7},{7,5},{8,10},{10,8},{9,1... | collective-permute-start | bytes 638984 | tf_op jit(solution)/shard_map/cond/branch_1_fun/ppermute | solution.py:40
  265.4 11.8 %collective-permute-start.30 = (f32[32,1664]{1,0:T(8,128)S(1)}, f32[32,1664]{1,0:T(8,128)S(1)}, u32[]{:S(2)}, u32[]{:S(2)}) collective-permute-start(f32[32,1664]{1,0:T(8,128)S(1)} %get-tuple-element.302.refs_1_.refs_5_), channel_id=1, source_target_pairs={{0,4},{4,0},{1,5},{5,1},{2,6},{6,2},{3,7},{7,3},{8,12},{12,8},{9,1... | collective-permute-start | bytes 638984 | tf_op jit(solution)/shard_map/cond/branch_1_fun/ppermute | solution.py:40
  (97 other events, 824.3 us)
Sparse Core Ops, SparseCore 0:
  99.2 192.0 all-reduce.2

commit v7 on v6

--- a/solution.py
+++ b/solution.py
@@ -590,16 +590,21 @@
         grad[0] = dx1[...] + norm_grad(e, xh, inv, gain[...])
 
 
-def block_kernel(g0, g1, f0, f1, h0, h1, u0, u1, down, up):
+def block_kernel(g0, g1, f0, f1, h0, h1, u0, u1, down, up, turned):
     p = pl.program_id(0)
+    rows = h0.shape[0]
 
     @pl.when(p < 4)
     def _():
         down[...] = mm(g0[...].T, f0[...]) + mm(g1[...].T, f1[...])
 
+    @pl.when(p == 4)
+    def _():
+        turned[:, :rows], turned[:, rows:] = h0[...].T, h1[...].T
+
     @pl.when(p >= 4)
     def _():
-        up[...] = mm(h0[...].T, u0[...]) + mm(h1[...].T, u1[...])
+        up[...] = mm(turned[:, :rows], u0[...]) + mm(turned[:, rows:], u1[...])
 
 
 def early_kernel(c, a0, a1, b0, b1, a2, a3, b2, b3, out):
@@ -701,6 +706,7 @@
         block_kernel, 2 * n - 1, [sg, sg, one, one, one, one, su, su],
         [(pl.BlockSpec((512, width), lambda p: (first(p), 0)), (wide, width), F32),
          (pl.BlockSpec((width, 512), lambda p: (0, second(p))), (width, wide - 512), F32)],
+        scratch=[pltpu.VMEM((width, 2 * rows), BF)],
         flops=8 * rows * width * wide, nbytes=8 * width * wide + 8 * rows * wide,
     )(*gl, *df, *h2, *du, after=after)
 

time: 313 us -> 313 us (level)
  no operation moved by 1% of the time
where the time goes in v7:
time: 313 us; the launch traced here: 308 us
  Pallas kernels  114 us (36%)
  waiting for transfers between devices  110 us (35%)
  starting transfers between devices  49.3 us (16%)
  local copies, waits for them, and re-layouts  15.6 us (5%)
  between operations  15.6 us (5%)
    pallas_call x55, Pallas kernels, run(): pl.pallas_call(waiting, grid_spec=pltpu.PrefetchScalarGridSpec(num_scalar...  114 us
    ppermute x36, waiting for transfers between devices, swap(): return lax.ppermute(part, name, pairs)  86.6 us
    ppermute x36, starting transfers between devices, swap(): return lax.ppermute(part, name, pairs)  33.4 us
    ppermute x12, waiting for transfers between devices, carry(): arrived.append(lax.ppermute(out, 'z', [hop]))  22.8 us
    ppermute x12, starting transfers between devices, carry(): arrived.append(lax.ppermute(out, 'z', [hop]))  15.8 us
    unnamed x79, local copies, waits for them, and re-layouts  10.8 us
  transfers between devices with their start and end apart: 49, of which 26 were waited for; matrix products, arithmetic and copies ran while one was open for 1% of the time, Pallas kernels for 32%

profile of v7, /device:TPU:0, one launch (start us, length us, event | category | flops | bytes accessed | tf_op | source)
XLA Modules:
  0.0 307.5 jit_solution(13827272001534951554)
XLA Ops:
  10.1 6.8 %shard_map.198 = (bf16[512,512]{1,0:T(8,128)(2,1)S(1)}, bf16[512,512]{1,0:T(8,128)(2,1)}, bf16[512,512]{1,0:T(8,128)(2,1)S(1)}, bf16[512,2048]{1,0:T(8,128)(2,1)...) custom-call(s32[3]{0:T(128)S(1)} %pad_add_fusion.refs_0_, s32[5]{0:T(128)S(1)} %stack.23.refs_1_.refs_0_, ...), custom_call_target="tpu_custom_call" | custom-call | flops 1536000000 | bytes 8388608 | tf_op jit(solution)/shard_map/pallas_call | solution.py:662
  19.9 6.2 %shard_map.199 = (bf16[512,512]{1,0:T(8,128)(2,1)S(1)}, bf16[512,512]{1,0:T(8,128)(2,1)}, bf16[512,512]{1,0:T(8,128)(2,1)S(1)}, bf16[512,2048]{1,0:T(8,128)(2,1)...) custom-call(s32[3]{0:T(128)S(1)} %pad_add_fusion.refs_0_, s32[5]{0:T(128)S(1)} %stack.23.refs_1_.refs_0_, ...), custom_call_target="tpu_custom_call" | custom-call | flops 1536000000 | bytes 8388608 | tf_op jit(solution)/shard_map/pallas_call | solution.py:662
  47.1 3.7 %shard_map.207.refs_6_.refs_5_ = f32[512,1024]{1,0:T(8,128)S(1)} custom-call(bf16[512,2048]{1,0:T(8,128)(2,1)S(1)} %get-tuple-element.254.refs_0_.refs_4_, bf16[512,2048]{1,0:T(8,128)(2,1)S(1)} %get-tuple-element.255.refs_1_, bf16[512,512]{1,0:T(8,128)(2,1)S(1)} %get-tuple-element.256.refs_2_, f32[4,72,256]{2,1,0:T(8,128)S(1)} %shard_map.206.refs_3_), custom_call_target="tpu_custom_call" | custom-call | flops 3072000000 | bytes 7340032 | tf_op jit(solution)/shard_map/pallas_call | solution.py:662
  61.1 13.0 %shard_map.212 = (bf16[2,512,512]{2,1,0:T(8,128)(2,1)}, f32[512,512]{1,0:T(8,128)}, bf16[512,1024]{1,0:T(8,128)(2,1)}, bf16[512,512]{1,0:T(8,128)(2,1)}, bf16[51...) custom-call(s32[3]{0:T(128)S(1)} %pad_add_fusion.refs_0_, ...), custom_call_target="tpu_custom_call" | custom-call | flops 5632000000 | bytes 25165824 | tf_op jit(solution)/shard_map/pallas_call | solution.py:662
  76.7 13.2 %shard_map.213 = (bf16[2,512,512]{2,1,0:T(8,128)(2,1)}, f32[512,512]{1,0:T(8,128)}, bf16[512,1024]{1,0:T(8,128)(2,1)}, bf16[512,512]{1,0:T(8,128)(2,1)}, bf16[51...) custom-call(s32[3]{0:T(128)S(1)} %pad_add_fusion.refs_0_, ...), custom_call_target="tpu_custom_call", output_to_operand_aliasing={{0}: (13, {})} | custom-call | flops 5632000000 | bytes 25165824 | tf_op jit(solution)/shard_map/pallas_call | solution.py:662
  90.0 7.3 %shard_map.215 = (f32[2048,512]{1,0:T(8,128)S(1)}, f32[512,1536]{1,0:T(8,128)}) custom-call(bf16[512,2048]{1,0:T(8,128)(2,1)S(1)} %get-tuple-element.266.refs_0_, bf16[512,2048]{1,0:T(8,128)(2,1)S(1)} %get-tuple-element.267.refs_1_, bf16[512,512]{1,0:T(8,128)(2,1)S(1)} %get-tuple-element.268.refs_2_, bf16[512,512]{1,0:T(8,128)(2,1)S(1)} %get-tuple-element.269.refs_3_, ...), custom_call_target="tpu_custom_call" | custom-call | flops 4294967296 | bytes 16777216 | tf_op jit(solution)/shard_map/pallas_call | solution.py:662
  101.4 5.4 %collective-permute-done.46 = f32[4,72,256]{2,1,0:T(8,128)S(1)} collective-permute-done((f32[4,72,256]{2,1,0:T(8,128)S(1)}, f32[4,72,256]{2,1,0:T(8,128)S(1)}, u32[]{:S(2)}, u32[]{:S(2)}) %collective-permute-start.46) | collective-permute-done | bytes 294944 | tf_op jit(solution)/shard_map/ppermute | solution.py:40
  106.8 181.8 %conditional.1 = (f32[512,512]{1,0:T(8,128)S(1)}, f32[512,512]{1,0:T(8,128)S(1)}, f32[256,1664]{1,0:T(8,128)S(1)}, f32[2,512,512]{2,1,0:T(8,128)}) conditional(s32[]{:T(128)} %convert_element_type.6, bf16[2,512,512]{2,1,0:T(8,128)(2,1)} %refs_3_.3, (f32[4,72,256]{2,1,0:T(8,128)S(1)}, f32[4,72,256]{2,1,0:T(8,128)S(1)}, f32[512,1536]{1,0:T(8,128)}, ...), branch_computations={%region_1.2_spmd, %region_2.3_spmd} | conditional | flops 29309859840 | bytes 265496704 | solution.py:932
  114.9 4.9 %branch_1_fun.39 = (bf16[512,512]{1,0:T(8,128)(2,1)S(1)}, f32[512,512]{1,0:T(8,128)S(1)}, f32[512,512]{1,0:T(8,128)S(1)}) custom-call(s32[5]{0:T(128)S(1)} %get-tuple-element.85.refs_0_, bf16[512,512]{1,0:T(8,128)(2,1)S(1)} %copy-done.53, bf16[512,512]{1,0:T(8,128)(2,1)S(1)} %copy-done.46, bf16[512,512]{1,0:T(8,128)(2,1)S(1)} %copy-done.48, ...), custom_call_target="tpu_custom_call" | custom-call | flops 5120000000 | bytes 6291456 | tf_op jit(solution)/shard_map/cond/branch_1_fun/pallas_call | solution.py:662
  125.5 4.7 %branch_1_fun.44 = (bf16[512,512]{1,0:T(8,128)(2,1)S(1)}, f32[512,512]{1,0:T(8,128)S(1)}, f32[512,512]{1,0:T(8,128)S(1)}) custom-call(s32[5]{0:T(128)S(1)} %get-tuple-element.85.refs_0_, bf16[512,512]{1,0:T(8,128)(2,1)S(1)} %copy-done.53, bf16[512,512]{1,0:T(8,128)(2,1)S(1)} %copy-done.46, ...), custom_call_target="tpu_custom_call", output_to_operand_aliasing={{0}: (10, {}), {1}: (11, {}), {2}: (12, {})} | custom-call | flops 5120000000 | bytes 6291456 | tf_op jit(solution)/shard_map/cond/branch_1_fun/pallas_call | solution.py:662
  130.3 4.7 %branch_1_fun.45 = (bf16[512,512]{1,0:T(8,128)(2,1)S(1)}, f32[512,512]{1,0:T(8,128)S(1)}, f32[512,512]{1,0:T(8,128)S(1)}) custom-call(s32[5]{0:T(128)S(1)} %get-tuple-element.85.refs_0_, bf16[512,512]{1,0:T(8,128)(2,1)S(1)} %copy-done.55, bf16[512,512]{1,0:T(8,128)(2,1)S(1)} %copy-done.49, bf16[512,512]{1,0:T(8,128)(2,1)S(1)} %copy-done.51, ...), custom_call_target="tpu_custom_call" | custom-call | flops 5120000000 | bytes 6291456 | tf_op jit(solution)/shard_map/cond/branch_1_fun/pallas_call | solution.py:662
  135.0 20.8 %collective-permute-done.6.refs_5_ = f32[4,72,256]{2,1,0:T(8,128)S(1)} collective-permute-done((f32[4,72,256]{2,1,0:T(8,128)S(1)}, f32[4,72,256]{2,1,0:T(8,128)S(1)}, u32[]{:S(2)}, u32[]{:S(2)}) %collective-permute-start.6) | collective-permute-done | bytes 294944 | tf_op jit(solution)/shard_map/cond/branch_1_fun/ppermute | solution.py:53
  162.1 4.9 %branch_1_fun.49 = (bf16[512,512]{1,0:T(8,128)(2,1)S(1)}, f32[512,512]{1,0:T(8,128)S(1)}, f32[512,512]{1,0:T(8,128)S(1)}) custom-call(s32[5]{0:T(128)S(1)} %get-tuple-element.85.refs_0_, bf16[512,512]{1,0:T(8,128)(2,1)S(1)} %copy-done.55, bf16[512,512]{1,0:T(8,128)(2,1)S(1)} %copy-done.49, ...), custom_call_target="tpu_custom_call", output_to_operand_aliasing={{0}: (10, {}), {1}: (11, {}), {2}: (12, {})} | custom-call | flops 5120000000 | bytes 6291456 | tf_op jit(solution)/shard_map/cond/branch_1_fun/pallas_call | solution.py:662
  171.2 6.3 %branch_1_fun.51 = (f32[2,512,512]{2,1,0:T(8,128)S(1)}, bf16[512,512]{1,0:T(8,128)(2,1)S(1)}, bf16[512,512]{1,0:T(8,128)(2,1)S(1)}, f32[8,512]{1,0:T(8,128)S(1)}) custom-call(s32[5]{0:T(128)S(1)} %get-tuple-element.85.refs_0_, bf16[2,512,512]{2,1,0:T(8,128)(2,1)S(1)} %copy-done.17, f32[512,512]{1,0:T(8,128)S(1)} %copy-done.43, ...), custom_call_target="tpu_custom_call" | custom-call | flops 3072000000 | bytes 11534336 | tf_op jit(solution)/shard_map/cond/branch_1_fun/pallas_call | solution.py:662
  185.0 6.3 %branch_1_fun.54 = (f32[2,512,512]{2,1,0:T(8,128)S(1)}, bf16[512,512]{1,0:T(8,128)(2,1)S(1)}, bf16[512,512]{1,0:T(8,128)(2,1)S(1)}, f32[8,512]{1,0:T(8,128)S(1)}) custom-call(s32[5]{0:T(128)S(1)} %get-tuple-element.85.refs_0_, bf16[2,512,512]{2,1,0:T(8,128)(2,1)S(1)} %copy-done.17, f32[512,512]{1,0:T(8,128)S(1)} %copy-done.44, ...), custom_call_target="tpu_custom_call", output_to_operand_aliasing={{0}: (16, {})} | custom-call | flops 3072000000 | bytes 11534336 | tf_op jit(solution)/shard_map/cond/branch_1_fun/pallas_call | solution.py:662
  203.7 4.2 %collective-permute-done.14.refs_2_ = f32[16,1024]{1,0:T(8,128)S(1)} collective-permute-done((f32[16,1024]{1,0:T(8,128)S(1)}, f32[16,1024]{1,0:T(8,128)S(1)}, u32[]{:S(2)}, u32[]{:S(2)}) %collective-permute-start.14) | collective-permute-done | bytes 65568 | tf_op jit(solution)/shard_map/cond/branch_1_fun/ppermute | solution.py:40
  208.6 6.8 %collective-permute-done.18.refs_4_ = f32[64,1664]{1,0:T(8,128)S(1)} collective-permute-done((f32[64,1664]{1,0:T(8,128)S(1)}, f32[64,1664]{1,0:T(8,128)S(1)}, u32[]{:S(2)}, u32[]{:S(2)}) %collective-permute-start.18) | collective-permute-done | bytes 426016 | tf_op jit(solution)/shard_map/cond/branch_1_fun/ppermute | solution.py:40
  218.3 4.3 %collective-permute-done.22.refs_4_ = f32[32,1664]{1,0:T(8,128)S(1)} collective-permute-done((f32[32,1664]{1,0:T(8,128)S(1)}, f32[32,1664]{1,0:T(8,128)S(1)}, u32[]{:S(2)}, u32[]{:S(2)}) %collective-permute-start.22) | collective-permute-done | bytes 213024 | tf_op jit(solution)/shard_map/cond/branch_1_fun/ppermute | solution.py:40
  226.1 4.9 %collective-permute-done.20.refs_4_ = f32[32,1024]{1,0:T(8,128)S(1)} collective-permute-done((f32[32,1024]{1,0:T(8,128)S(1)}, f32[32,1024]{1,0:T(8,128)S(1)}, u32[]{:S(2)}, u32[]{:S(2)}) %collective-permute-start.20) | collective-permute-done | bytes 131104 | tf_op jit(solution)/shard_map/cond/branch_1_fun/ppermute | solution.py:40
  236.6 9.9 %collective-permute-done.26.refs_1_ = f32[16,1664]{1,0:T(8,128)S(1)} collective-permute-done((f32[16,1664]{1,0:T(8,128)S(1)}, f32[16,1664]{1,0:T(8,128)S(1)}, u32[]{:S(2)}, u32[]{:S(2)}) %collective-permute-start.26) | collective-permute-done | bytes 106528 | tf_op jit(solution)/shard_map/cond/branch_1_fun/ppermute | solution.py:40
  247.3 5.2 %collective-permute-done.28.refs_2_ = f32[16,1664]{1,0:T(8,128)S(1)} collective-permute-done((f32[16,1664]{1,0:T(8,128)S(1)}, f32[16,1664]{1,0:T(8,128)S(1)}, u32[]{:S(2)}, u32[]{:S(2)}) %collective-permute-start.28) | collective-permute-done | bytes 106528 | tf_op jit(solution)/shard_map/cond/branch_1_fun/ppermute | solution.py:40
  253.2 10.3 %collective-permute-done.29.refs_2_ = f32[32,1664]{1,0:T(8,128)S(1)} collective-permute-done((f32[32,1664]{1,0:T(8,128)S(1)}, f32[32,1664]{1,0:T(8,128)S(1)}, u32[]{:S(2)}, u32[]{:S(2)}) %collective-permute-start.29) | collective-permute-done | bytes 213024 | tf_op jit(solution)/shard_map/cond/branch_1_fun/ppermute | solution.py:40
  266.6 9.2 %collective-permute-done.31.refs_4_ = f32[32,1664]{1,0:T(8,128)S(1)} collective-permute-done((f32[32,1664]{1,0:T(8,128)S(1)}, f32[32,1664]{1,0:T(8,128)S(1)}, u32[]{:S(2)}, u32[]{:S(2)}) %collective-permute-start.31) | collective-permute-done | bytes 213024 | tf_op jit(solution)/shard_map/cond/branch_1_fun/ppermute | solution.py:40
  279.5 7.1 %collective-permute-done.32.refs_2_ = f32[64,1664]{1,0:T(8,128)S(1)} collective-permute-done((f32[64,1664]{1,0:T(8,128)S(1)}, f32[64,1664]{1,0:T(8,128)S(1)}, u32[]{:S(2)}, u32[]{:S(2)}) %collective-permute-start.32) | collective-permute-done | bytes 426016 | tf_op jit(solution)/shard_map/cond/branch_1_fun/ppermute | solution.py:40
  (286 shorter events, 120.5 us)
Async XLA Ops:
  7.2 284.2 %all-reduce.3.cloned.1.call-start = ((), (), s32[]{:S(2)}) async-start(), calls=%async_computation | async-start | bytes 14680064 | tf_op jit(solution)/shard_map/psum | solution.py:43
  16.9 10.0 %collective-permute-start.35 = (f32[4,72,256]{2,1,0:T(8,128)S(1)}, f32[4,72,256]{2,1,0:T(8,128)S(1)}, u32[]{:S(2)}, u32[]{:S(2)}) collective-permute-start(f32[4,72,256]{2,1,0:T(8,128)S(1)} %get-tuple-element.243.refs_8_), channel_id=1, source_target_pairs={{0,4},{4,0},{1,5},{5,1},{2,6},{6,2},{3,7},{7,3},{8,12},{12,8},{9,1... | collective-permute-start | bytes 884744 | tf_op jit(solution)/shard_map/ppermute | solution.py:40
  58.8 17.8 %collective-permute-start.42 = (f32[4,72,256]{2,1,0:T(8,128)S(1)}, f32[4,72,256]{2,1,0:T(8,128)S(1)}, u32[]{:S(2)}, u32[]{:S(2)}) collective-permute-start(f32[4,72,256]{2,1,0:T(8,128)S(1)} %get-tuple-element.259.refs_13_), channel_id=1, source_target_pairs={{0,4},{4,0},{1,5},{5,1},{2,6},{6,2},{3,7},{7,3},{8,12},{12,8},{9,1... | collective-permute-start | bytes 884744 | tf_op jit(solution)/shard_map/ppermute | solution.py:40
  74.1 15.8 %collective-permute-start.44 = (f32[4,72,256]{2,1,0:T(8,128)S(1)}, f32[4,72,256]{2,1,0:T(8,128)S(1)}, u32[]{:S(2)}, u32[]{:S(2)}) collective-permute-start(f32[4,72,256]{2,1,0:T(8,128)S(1)} %get-tuple-element.262.refs_14_), channel_id=1, source_target_pairs={{0,4},{4,0},{1,5},{5,1},{2,6},{6,2},{3,7},{7,3},{8,12},{12,8},{9,1... | collective-permute-start | bytes 884744 | tf_op jit(solution)/shard_map/ppermute | solution.py:40
  113.3 9.9 %collective-permute-start = (f32[256,1024]{1,0:T(8,128)S(1)}, f32[256,1024]{1,0:T(8,128)S(1)}, u32[]{:S(2)}, u32[]{:S(2)}) collective-permute-start(f32[256,1024]{1,0:T(8,128)S(1)} %branch_1_fun.38.refs_10_), channel_id=1, source_target_pairs={{0,1},{1,0},{2,3},{3,2},{4,5},{5,4},{6,7},{7,6},{8,9},{9,8},{10,11... | collective-permute-start | bytes 3145736 | tf_op jit(solution)/shard_map/cond/branch_1_fun/ppermute | solution.py:40
  113.4 9.1 %collective-permute-start.1 = (f32[4,72,256]{2,1,0:T(8,128)S(1)}, f32[4,72,256]{2,1,0:T(8,128)S(1)}, u32[]{:S(2)}, u32[]{:S(2)}) collective-permute-start(f32[4,72,256]{2,1,0:T(8,128)S(1)} %branch_1_fun.37.refs_9_.refs_0_), channel_id=1, source_target_pairs={{24,16},{25,17},{26,18},{27,19},{28,20},{29,21},{30,22},{31,23}} | collective-permute-start | bytes 884744 | tf_op jit(solution)/shard_map/cond/branch_1_fun/ppermute | solution.py:53
  121.2 34.7 %collective-permute-start.6 = (f32[4,72,256]{2,1,0:T(8,128)S(1)}, f32[4,72,256]{2,1,0:T(8,128)S(1)}, u32[]{:S(2)}, u32[]{:S(2)}) collective-permute-start(f32[4,72,256]{2,1,0:T(8,128)S(1)} %branch_1_fun.41.refs_2_), channel_id=1, source_target_pairs={{8,0},{9,1},{10,2},{11,3},{12,4},{13,5},{14,6},{15,7}} | collective-permute-start | bytes 884744 | tf_op jit(solution)/shard_map/cond/branch_1_fun/ppermute | solution.py:53
  122.6 34.0 %collective-permute-start.5 = (f32[4,72,256]{2,1,0:T(8,128)S(1)}, f32[4,72,256]{2,1,0:T(8,128)S(1)}, u32[]{:S(2)}, u32[]{:S(2)}) collective-permute-start(f32[4,72,256]{2,1,0:T(8,128)S(1)} %branch_1_fun.42.refs_3_), channel_id=1, source_target_pairs={{16,8},{17,9},{18,10},{19,11},{20,12},{21,13},{22,14},{23,15}} | collective-permute-start | bytes 884744 | tf_op jit(solution)/shard_map/cond/branch_1_fun/ppermute | solution.py:53
  123.9 34.0 %collective-permute-start.4 = (f32[64,1024]{1,0:T(8,128)S(1)}, f32[64,1024]{1,0:T(8,128)S(1)}, u32[]{:S(2)}, u32[]{:S(2)}) collective-permute-start(f32[64,1024]{1,0:T(8,128)S(1)} %get-tuple-element.112), channel_id=1, source_target_pairs={{0,4},{4,0},{1,5},{5,1},{2,6},{6,2},{3,7},{7,3},{8,12},{12,8},{9,1... | collective-permute-start | bytes 786440 | tf_op jit(solution)/shard_map/cond/branch_1_fun/ppermute | solution.py:40
  124.0 34.0 %collective-permute-start.3 = (f32[64,1024]{1,0:T(8,128)S(1)}, f32[64,1024]{1,0:T(8,128)S(1)}, u32[]{:S(2)}, u32[]{:S(2)}) collective-permute-start(f32[64,1024]{1,0:T(8,128)S(1)} %get-tuple-element.110.refs_13_), channel_id=1, source_target_pairs={{0,2},{2,0},{1,3},{3,1},{4,6},{6,4},{5,7},{7,5},{8,10},{10,8},{9,1... | collective-permute-start | bytes 786440 | tf_op jit(solution)/shard_map/cond/branch_1_fun/ppermute | solution.py:40
  156.5 14.6 %collective-permute-start.11 = (f32[4,72,256]{2,1,0:T(8,128)S(1)}, f32[4,72,256]{2,1,0:T(8,128)S(1)}, u32[]{:S(2)}, u32[]{:S(2)}) collective-permute-start(f32[4,72,256]{2,1,0:T(8,128)S(1)} %get-tuple-element.127.refs_2_), channel_id=1, source_target_pairs={{0,4},{4,0},{1,5},{5,1},{2,6},{6,2},{3,7},{7,3},{8,12},{12,8},{9,1... | collective-permute-start | bytes 884744 | tf_op jit(solution)/shard_map/cond/branch_1_fun/ppermute | solution.py:40
  156.6 20.9 %collective-permute-start.10 = (f32[4,72,256]{2,1,0:T(8,128)S(1)}, f32[4,72,256]{2,1,0:T(8,128)S(1)}, u32[]{:S(2)}, u32[]{:S(2)}) collective-permute-start(f32[4,72,256]{2,1,0:T(8,128)S(1)} %branch_1_fun.47.refs_5_), channel_id=1, source_target_pairs={{8,0},{9,1},{10,2},{11,3},{12,4},{13,5},{14,6},{15,7}} | collective-permute-start | bytes 884744 | tf_op jit(solution)/shard_map/cond/branch_1_fun/ppermute | solution.py:53
  160.1 10.5 %collective-permute-start.7 = (f32[32,1024]{1,0:T(8,128)S(1)}, f32[32,1024]{1,0:T(8,128)S(1)}, u32[]{:S(2)}, u32[]{:S(2)}) collective-permute-start(f32[32,1024]{1,0:T(8,128)S(1)} %get-tuple-element.129.refs_13_), channel_id=1, source_target_pairs={{0,4},{4,0},{1,5},{5,1},{2,6},{6,2},{3,7},{7,3},{8,12},{12,8},{9,1... | collective-permute-start | bytes 393224 | tf_op jit(solution)/shard_map/cond/branch_1_fun/ppermute | solution.py:40
  201.0 14.3 %collective-permute-start.18 = (f32[64,1664]{1,0:T(8,128)S(1)}, f32[64,1664]{1,0:T(8,128)S(1)}, u32[]{:S(2)}, u32[]{:S(2)}) collective-permute-start(f32[64,1664]{1,0:T(8,128)S(1)} %get-tuple-element.166), channel_id=1, source_target_pairs={{0,4},{4,0},{1,5},{5,1},{2,6},{6,2},{3,7},{7,3},{8,12},{12,8},{9,1... | collective-permute-start | bytes 1277960 | tf_op jit(solution)/shard_map/cond/branch_1_fun/ppermute | solution.py:40
  202.1 13.3 %collective-permute-start.17 = (f32[64,1664]{1,0:T(8,128)S(1)}, f32[64,1664]{1,0:T(8,128)S(1)}, u32[]{:S(2)}, u32[]{:S(2)}) collective-permute-start(f32[64,1664]{1,0:T(8,128)S(1)} %get-tuple-element.163.refs_3_), channel_id=1, source_target_pairs={{0,2},{2,0},{1,3},{3,1},{4,6},{6,4},{5,7},{7,5},{8,10},{10,8},{9,1... | collective-permute-start | bytes 1277960 | tf_op jit(solution)/shard_map/cond/branch_1_fun/ppermute | solution.py:40
  208.5 9.2 %collective-permute-start.16 = (f32[32,1024]{1,0:T(8,128)S(1)}, f32[32,1024]{1,0:T(8,128)S(1)}, u32[]{:S(2)}, u32[]{:S(2)}) collective-permute-start(f32[32,1024]{1,0:T(8,128)S(1)} %branch_1_fun.59.refs_5_.refs_1_), channel_id=1, source_target_pairs={{0,8},{8,0},{16,24},{24,16},{1,9},{9,1},{17,25},{25,17},{2,10},{10... | collective-permute-start | bytes 393224 | tf_op jit(solution)/shard_map/cond/branch_1_fun/ppermute | solution.py:40
  223.2 12.6 %collective-permute-start.25 = (f32[32,1664]{1,0:T(8,128)S(1)}, f32[32,1664]{1,0:T(8,128)S(1)}, u32[]{:S(2)}, u32[]{:S(2)}) collective-permute-start(f32[32,1664]{1,0:T(8,128)S(1)} %get-tuple-element.171.refs_5_), channel_id=1, source_target_pairs={{0,8},{8,0},{16,24},{24,16},{1,9},{9,1},{17,25},{25,17},{2,10},{10... | collective-permute-start | bytes 638984 | tf_op jit(solution)/shard_map/cond/branch_1_fun/ppermute | solution.py:40
  233.6 13.0 %collective-permute-start.24 = (f32[64,1024]{1,0:T(8,128)S(1)}, f32[64,1024]{1,0:T(8,128)S(1)}, u32[]{:S(2)}, u32[]{:S(2)}) collective-permute-start(f32[64,1024]{1,0:T(8,128)S(1)} %get-tuple-element.173.refs_3_), channel_id=1, source_target_pairs={{0,4},{4,0},{1,5},{5,1},{2,6},{6,2},{3,7},{7,3},{8,12},{12,8},{9,1... | collective-permute-start | bytes 786440 | tf_op jit(solution)/shard_map/cond/branch_1_fun/ppermute | solution.py:40
  234.7 11.9 %collective-permute-start.23 = (f32[64,1024]{1,0:T(8,128)S(1)}, f32[64,1024]{1,0:T(8,128)S(1)}, u32[]{:S(2)}, u32[]{:S(2)}) collective-permute-start(f32[64,1024]{1,0:T(8,128)S(1)} %get-tuple-element.172.refs_3_.refs_1_), channel_id=1, source_target_pairs={{0,2},{2,0},{1,3},{3,1},{4,6},{6,4},{5,7},{7,5},{8,10},{10,8},{9,1... | collective-permute-start | bytes 786440 | tf_op jit(solution)/shard_map/cond/branch_1_fun/ppermute | solution.py:40
  236.4 10.1 %collective-permute-start.26 = (f32[16,1664]{1,0:T(8,128)S(1)}, f32[16,1664]{1,0:T(8,128)S(1)}, u32[]{:S(2)}, u32[]{:S(2)}) collective-permute-start(f32[16,1664]{1,0:T(8,128)S(1)} %get-tuple-element.176.refs_2_), channel_id=1, source_target_pairs={{0,16},{16,0},{8,24},{24,8},{1,17},{17,1},{9,25},{25,9},{2,18},{18... | collective-permute-start | bytes 319496 | tf_op jit(solution)/shard_map/cond/branch_1_fun/ppermute | solution.py:40
  253.1 10.4 %collective-permute-start.29 = (f32[32,1664]{1,0:T(8,128)S(1)}, f32[32,1664]{1,0:T(8,128)S(1)}, u32[]{:S(2)}, u32[]{:S(2)}) collective-permute-start(f32[32,1664]{1,0:T(8,128)S(1)} %branch_1_fun.68.refs_1_.refs_3_), channel_id=1, source_target_pairs={{0,8},{8,0},{16,24},{24,16},{1,9},{9,1},{17,25},{25,17},{2,10},{10... | collective-permute-start | bytes 638984 | tf_op jit(solution)/shard_map/cond/branch_1_fun/ppermute | solution.py:40
  253.2 34.5 %collective-permute-start.27 = (f32[256,1024]{1,0:T(8,128)S(1)}, f32[256,1024]{1,0:T(8,128)S(1)}, u32[]{:S(2)}, u32[]{:S(2)}) collective-permute-start(f32[256,1024]{1,0:T(8,128)S(1)} %branch_1_fun.66.refs_1_.refs_3_), channel_id=1, source_target_pairs={{0,1},{1,0},{2,3},{3,2},{4,5},{5,4},{6,7},{7,6},{8,9},{9,8},{10,11... | collective-permute-start | bytes 3145736 | tf_op jit(solution)/shard_map/cond/branch_1_fun/ppermute | solution.py:40
  264.1 11.6 %collective-permute-start.31 = (f32[32,1664]{1,0:T(8,128)S(1)}, f32[32,1664]{1,0:T(8,128)S(1)}, u32[]{:S(2)}, u32[]{:S(2)}) collective-permute-start(f32[32,1664]{1,0:T(8,128)S(1)} %get-tuple-element.301.refs_3_), channel_id=1, source_target_pairs={{0,2},{2,0},{1,3},{3,1},{4,6},{6,4},{5,7},{7,5},{8,10},{10,8},{9,1... | collective-permute-start | bytes 638984 | tf_op jit(solution)/shard_map/cond/branch_1_fun/ppermute | solution.py:40
  265.6 12.2 %collective-permute-start.30 = (f32[32,1664]{1,0:T(8,128)S(1)}, f32[32,1664]{1,0:T(8,128)S(1)}, u32[]{:S(2)}, u32[]{:S(2)}) collective-permute-start(f32[32,1664]{1,0:T(8,128)S(1)} %get-tuple-element.302.refs_1_.refs_5_), channel_id=1, source_target_pairs={{0,4},{4,0},{1,5},{5,1},{2,6},{6,2},{3,7},{7,3},{8,12},{12,8},{9,1... | collective-permute-start | bytes 638984 | tf_op jit(solution)/shard_map/cond/branch_1_fun/ppermute | solution.py:40
  (97 other events, 823.5 us)
Sparse Core Ops, SparseCore 0:
  99.5 191.8 all-reduce.2
